TPU v7x, 32 devices: a whole 2x2x4 slice. The times are simulated.
32 devices in a mesh: ctx: 4 (over y, x), head: 4 (over z), pool: 2 (over core).
Axes of the slice: x: 2, y: 2, z: 4, core: 2. Of those that a mesh axis runs over, the one named last changes fastest.
Arguments:
- queries: bfloat16 [2, 512, 4096], P(None, ('ctx', 'pool'), 'head')
- stretch_keys: bfloat16 [2, 512, 512], P(None, ('ctx', 'pool'), 'head'), may hold values from -6 to 6
- stretch_values: bfloat16 [2, 512, 512], P(None, ('ctx', 'pool'), 'head'), may hold values from -6 to 6
- slot_pool_keys: bfloat16 [64, 64, 512], P(('ctx', 'head', 'pool')), may hold values from -6 to 6
- slot_pool_values: bfloat16 [64, 64, 512], P(('ctx', 'head', 'pool')), may hold values from -6 to 6
- prefix_lengths: int32 [2], replicated, may hold values from 512 to 2048
- page_slot_table: int32 [64], replicated, may hold values from 0 to 63, each once
- vertical: int32 [32, 16], replicated, may hold values from 0 to 31
- slash: int32 [32, 16], replicated, may hold values from 0 to 31
Outputs:
- attended: bfloat16 [2, 512, 4096], P(None, ('ctx', 'pool'), 'head')
Inputs may be any that keep to these rules, and one draw needn't show every extreme that they name: `page_slot_table`: each pool slot is named exactly once; entry 32 * b + j is the slot of page j of prompt b.
All inputs are finite; a program needn't handle non-finite values.
Results may differ from a plain program's by a relative error of at most 0.0075.
Values may be sent and summed in bfloat16 or wider, within the bound.
No kernel may reach another device: no remote copies, remote signals or barrier semaphores. Data moves between devices by JAX's collectives and lax.ppermute only.
A program may use at most 128 MiB of HBM per device.

v0:
```python
import math

import jax
import jax.numpy as jnp
from jax import lax
from jax.sharding import PartitionSpec as P

very_low = -1e30


def absorb(running, scores, allowed, values):
    highest, totals, numerator = running
    new_high = jnp.maximum(highest, jnp.max(jnp.where(allowed, scores, very_low), axis=-1))
    factor = jnp.exp(highest - new_high)
    weights = jnp.where(allowed, jnp.exp(scores - new_high[..., None]), 0.0)
    totals = totals * factor + jnp.sum(weights, axis=-1)
    numerator = numerator * factor[..., None] + jnp.einsum(
        "grk,kd->grd", weights.astype(jnp.bfloat16), values, preferred_element_type=jnp.float32
    )
    return (new_high, totals, numerator)


def body(
    queries,
    stretch_keys,
    stretch_values,
    slot_pool_keys,
    slot_pool_values,
    prefix_lengths,
    page_slot_table,
    vertical,
    slash,
):
    prompts, local_rows, row_width = queries.shape
    head_dim = stretch_keys.shape[2]
    group_size = row_width // head_dim
    page_len = slot_pool_keys.shape[1]
    owner_slots = slot_pool_keys.shape[0]
    slot_total = page_slot_table.shape[0]
    page_count = slot_total // prompts
    head_count = lax.axis_size("head")
    pool_count = lax.axis_size("pool")
    ctx_count = lax.axis_size("ctx")
    plane_size = ctx_count * pool_count
    ctx_index = lax.axis_index("ctx")
    pool_index = lax.axis_index("pool")
    head_index = lax.axis_index("head")
    plane_index = ctx_index * pool_count + pool_index
    stretch_len = plane_size * local_rows
    scaling = 1.0 / math.sqrt(head_dim)
    vert_rows = lax.dynamic_slice_in_dim(vertical, head_index * group_size, group_size, 0)
    slash_rows = lax.dynamic_slice_in_dim(slash, head_index * group_size, group_size, 0)
    page_ids = jnp.arange(page_count, dtype=jnp.int32)
    vert_hit = jnp.any(vert_rows[:, :, None] == page_ids[None, None, :], axis=1)
    row_ids = plane_index * local_rows + jnp.arange(local_rows, dtype=jnp.int32)
    page_keys, page_values = (
        lax.all_to_all(slot_pool_keys, "head", split_axis=2, concat_axis=0, tiled=True),
        lax.all_to_all(slot_pool_values, "head", split_axis=2, concat_axis=0, tiled=True),
    )
    held_slots = owner_slots * head_count
    empty_state = (
        jnp.full((group_size, local_rows), very_low, jnp.float32),
        jnp.zeros((group_size, local_rows), jnp.float32),
        jnp.zeros((group_size, local_rows, head_dim), jnp.float32),
    )
    plane_keys, plane_values = (
        lax.all_gather(page_keys, ("ctx", "pool"), axis=0, tiled=True),
        lax.all_gather(page_values, ("ctx", "pool"), axis=0, tiled=True),
    )
    owner_index = page_slot_table // owner_slots
    within = page_slot_table % owner_slots
    owner_pool = owner_index % pool_count
    owner_head = owner_index // pool_count % head_count
    owner_ctx = owner_index // (pool_count * head_count)
    location = (
        (owner_ctx * pool_count + owner_pool) * held_slots + owner_head * owner_slots + within
    )
    ordered_keys = jnp.take(plane_keys, location, axis=0).reshape(
        prompts, page_count * page_len, head_dim
    )
    ordered_values = jnp.take(plane_values, location, axis=0).reshape(
        prompts, page_count * page_len, head_dim
    )
    key_span = min(2048, page_count * page_len)
    states = []
    for prompt in range(prompts):
        prefix_len = prefix_lengths[prompt]
        query_page = (prefix_len + row_ids) // page_len
        query_block = queries[prompt].reshape(local_rows, group_size, head_dim)
        prompt_keys = ordered_keys[prompt]
        prompt_values = ordered_values[prompt]

        def prefix_step(block_index, running):
            first_key = block_index * key_span
            key_part = lax.dynamic_slice_in_dim(prompt_keys, first_key, key_span, 0)
            value_part = lax.dynamic_slice_in_dim(prompt_values, first_key, key_span, 0)
            key_ids = first_key + jnp.arange(key_span, dtype=jnp.int32)
            first_page = first_key // page_len
            page_part = lax.dynamic_slice_in_dim(vert_hit, first_page, key_span // page_len, 1)
            distance = (
                query_page[:, None]
                - (first_page + jnp.arange(key_span // page_len, dtype=jnp.int32))[None, :]
            )
            slash_hit = jnp.any(slash_rows[:, :, None, None] == distance[None, None], axis=1)
            chosen = page_part[:, None, :] | slash_hit
            allowed = jnp.repeat(chosen, page_len, axis=2) & (key_ids < prefix_len)[None, None, :]
            scores = (
                jnp.einsum("rgd,kd->grk", query_block, key_part, preferred_element_type=jnp.float32)
                * scaling
            )
            return absorb(running, scores, allowed, value_part)

        upper_bound = (prefix_len + key_span - 1) // key_span
        states.append(lax.fori_loop(0, upper_bound, prefix_step, empty_state))
    plane_stretch_keys, plane_stretch_values = (
        lax.all_gather(stretch_keys, ("ctx", "pool"), axis=1, tiled=True),
        lax.all_gather(stretch_values, ("ctx", "pool"), axis=1, tiled=True),
    )
    stretch_span = min(2048, stretch_len)
    outputs = []
    for prompt in range(prompts):
        query_block = queries[prompt].reshape(local_rows, group_size, head_dim)
        prompt_keys = plane_stretch_keys[prompt]
        prompt_values = plane_stretch_values[prompt]

        def stretch_step(block_index, running):
            first_key = block_index * stretch_span
            key_ids = first_key + jnp.arange(stretch_span, dtype=jnp.int32)
            allowed = jnp.broadcast_to(
                (key_ids[None, :] <= row_ids[:, None])[None], (group_size, local_rows, stretch_span)
            )
            scores = (
                jnp.einsum(
                    "rgd,kd->grk", query_block, prompt_keys, preferred_element_type=jnp.float32
                )
                * scaling
            )
            return absorb(running, scores, allowed, prompt_values)

        upper_bound = (plane_index * local_rows + local_rows - 1) // stretch_span + 1
        highest, totals, numerator = lax.fori_loop(0, upper_bound, stretch_step, states[prompt])
        result = numerator / totals[..., None]
        outputs.append(
            result.transpose(1, 0, 2).reshape(local_rows, row_width).astype(jnp.bfloat16)
        )
    return jnp.stack(outputs)


def solution(mesh):
    in_specs = (
        P(None, ("ctx", "pool"), "head"),
        P(None, ("ctx", "pool"), "head"),
        P(None, ("ctx", "pool"), "head"),
        P(("ctx", "head", "pool"), None, None),
        P(("ctx", "head", "pool"), None, None),
        P(),
        P(),
        P(),
        P(),
    )
    out_specs = P(None, ("ctx", "pool"), "head")
    return jax.shard_map(body, mesh=mesh, in_specs=in_specs, out_specs=out_specs, check_vma=False)
```

profile of v0, /device:TPU:0, one launch (start us, length us, event | category | flops | bytes accessed | tf_op | source)
XLA Modules:
  0.0 119.0 jit_solution(515877227580632540)
XLA Ops:
  6.6 1.2 copy.50
  8.0 12.2 %all_to_all.36 = bf16[4,2,8192]{2,1,0:T(2,128)(2,1)S(1)} all-to-all(bf16[4,2,8192]{2,1,0:T(2,128)(2,1)S(1)} %reshape.232), channel_id=1, replica_groups=mesh['ctx'=4,'head'=4,'pool'=2] {'head'}, dimensions={0} | all-to-all | bytes 262144 | tf_op jit(solution)/shard_map/all_to_all | solution.py:57
  21.4 1.1 copy.53
  22.7 8.4 %all_to_all.37 = bf16[4,2,8192]{2,1,0:T(2,128)(2,1)S(1)} all-to-all(bf16[4,2,8192]{2,1,0:T(2,128)(2,1)S(1)} %reshape.234), channel_id=1, replica_groups=mesh['ctx'=4,'head'=4,'pool'=2] {'head'}, dimensions={0} | all-to-all | bytes 262144 | tf_op jit(solution)/shard_map/all_to_all | solution.py:58
  35.2 9.6 %all_gather.14 = bf16[2,512,128]{2,1,0:T(8,128)(2,1)S(1)} all-gather(bf16[2,64,128]{2,1,0:T(8,128)(2,1)S(1)} %copy-done.4), channel_id=1, replica_groups=mesh['ctx'=4,'head'=4,'pool'=2] {'ctx','pool'}, dimensions={1}, use_global_device_ids=true | all-gather | bytes 294912 | tf_op jit(solution)/shard_map/all_gather | solution.py:116
  44.8 9.2 %all_gather.15 = bf16[2,512,128]{2,1,0:T(8,128)(2,1)S(1)} all-gather(bf16[2,64,128]{2,1,0:T(8,128)(2,1)S(1)} %copy-done.5), channel_id=1, replica_groups=mesh['ctx'=4,'head'=4,'pool'=2] {'ctx','pool'}, dimensions={1}, use_global_device_ids=true | all-gather | bytes 294912 | tf_op jit(solution)/shard_map/all_gather | solution.py:117
  54.1 0.7 slice_bitcast_fusion.3
  54.8 0.7 slice_bitcast_fusion.2
  55.5 2.0 %gather_fusion = bf16[64,64,128]{2,1,0:T(8,128)(2,1)S(1)} fusion(bf16[64,64,128]{2,1,0:T(8,128)(2,1)} %all-gather.3.cloned.1.call-done, s32[1024]{0:T(1024)S(1)} %pad_clamp_fusion), kind=kCustom, calls=%fused_computation.clone | custom fusion | bytes 2097408 | tf_op jit(solution)/shard_map/jit(_take)/gather | solution.py:78
  57.5 12.7 %all-gather.5.cloned.1.call-done = bf16[64,64,128]{2,1,0:T(8,128)(2,1)} async-done(((bf16[8,64,128]{2,1,0:T(8,128)(2,1)}), bf16[64,64,128]{2,1,0:T(8,128)(2,1)}) %all-gather.5.cloned.1.call-update) | async-done | bytes 1048592 | tf_op jit(solution)/shard_map/all_gather | solution.py:68
  70.2 2.0 %gather_fusion.1 = bf16[64,64,128]{2,1,0:T(8,128)(2,1)S(1)} fusion(bf16[64,64,128]{2,1,0:T(8,128)(2,1)} %all-gather.5.cloned.1.call-done, s32[1024]{0:T(1024)S(1)} %pad_clamp_fusion), kind=kCustom, calls=%fused_computation.1.clone | custom fusion | bytes 2097408 | tf_op jit(solution)/shard_map/jit(_take)/gather | solution.py:81
  72.4 1.4 %fusion.68 = (bf16[32,64,128]{2,1,0:T(8,128)(2,1)}, bf16[32,64,128]{2,1,0:T(8,128)(2,1)}, bf16[32,64,128]{2,1,0:T(8,128)(2,1)}, bf16[32,64,128]{2,1,0:T(8,128)(2,1)}) fusion(bf16[64,64,128]{2,1,0:T(8,128)(2,1)S(1)} %get-tuple-element.870, bf16[64,64,128]{2,1,0:T(8,128)(2,1)S(1)} %get-tuple-element.871), kind=kLoop, calls=%fused_computation.135 | loop fusion | bytes 4194304 | tf_op jit(solution)/shard_map/slice | solution.py:91
  73.8 15.0 %while.68 = (s32[]{:T(128)}, f32[8,64]{1,0:T(8,128)S(1)}, f32[8,64]{1,0:T(8,128)S(1)}, f32[8,64,128]{2,1,0:T(8,128)S(1)}, s32[]{:T(128)}, /*index=5*/pred[8,32]{...) while((s32[]{:T(128)}, f32[8,64]{1,0:T(8,128)S(1)}, ...), condition=%wide.region_5.7_spmd.clone.clone, body=%wide.region_1.0_spmd.clone.clone.sunk | while | flops 552214656 | bytes 22833016 | solution.py:114
  75.3 2.8 %broadcast_in_dim.211 = pred[8,64,32,64]{3,2,1,0:T(32,128)(4,1)S(1)} broadcast(pred[8,64,32]{2,1,0:T(8,128)(4,1)S(1)} %copy.69), dimensions={0,1,2} | broadcast | bytes 1064960 | tf_op jit(solution)/shard_map/while/body/broadcast_in_dim | solution.py:106
  78.1 5.1 %reshape.238 = pred[8,64,2048]{2,1,0:T(32,128)(4,1)S(1)} reshape(pred[8,64,32,64]{3,2,1,0:T(32,128)(4,1)S(1)} %broadcast_in_dim.211) | data formatting | bytes 2097152 | tf_op jit(solution)/shard_map/while/body/reshape | solution.py:106
  83.9 2.2 %fusion.106 = (f32[8,64]{1,0:T(8,128)S(1)}, f32[2048,64,8]{0,1,2:T(8,128)S(1)}) fusion(pred[8,64,2048]{2,1,0:T(32,128)(4,1)S(1)} %reshape.238, pred[2048]{0:T(1024)(128)(4,1)S(1)} %add_compare_fusion.4, bf16[64,8,128]{2,0,1:T(8,128)(2,1)} %get-tuple-element.1300, bf16[2048,128]{1,0:T(8,128)(2,1)} %get-tuple-element.1299), kind=kOutput, calls=%fused_computation.44.clone.1 | convolution fusion | flops 272629248 | bytes 5902336 | tf_op jit(solution)/shard_map/while/body/rgd,kd->grk/dot_general | solution.py:108
  86.1 1.4 %fusion.107 = f32[8,64]{1,0:T(8,128)S(1)} fusion(f32[2048,64,8]{0,1,2:T(8,128)S(1)} %get-tuple-element.1149, pred[8,64,2048]{2,1,0:T(32,128)(4,1)S(1)} %reshape.238, f32[8,64]{1,0:T(8,128)S(1)} %max.30, pred[2048]{0:T(1024)(128)(4,1)S(1)} %add_compare_fusion.4), kind=kLoop, calls=%fused_computation.48.clone.1 | loop fusion | flops 5242368 | bytes 5249024 | tf_op jit(solution)/shard_map/while/body/reduce_sum | solution.py:16
  87.5 1.3 %fusion.108 = f32[8,64,128]{2,1,0:T(8,128)S(1)} fusion(f32[2048,64,8]{0,1,2:T(8,128)S(1)} %get-tuple-element.1149, pred[8,64,2048]{2,1,0:T(32,128)(4,1)S(1)} %reshape.238, f32[8,64]{1,0:T(8,128)S(1)} %max.30, pred[2048]{0:T(1024)(128)(4,1)S(1)} %add_compare_fusion.4, bf16[2048,128]{1,0:T(8,128)(2,1)S(1)} %copy-done.2, ...), kind=kOutput, calls=%fused_computation.52.clone.1 | convolution fusion | flops 273809408 | bytes 6297600 | tf_op jit(solution)/shard_map/while/body/grk,kd->grd/dot_general | solution.py:17
  88.8 3.2 %while.66 = (s32[]{:T(128)}, f32[8,64]{1,0:T(8,128)S(1)}, f32[8,64]{1,0:T(8,128)S(1)}, f32[8,64,128]{2,1,0:T(8,128)S(1)}, s32[]{:T(128)}, /*index=5*/bf16[512,12...) while((s32[]{:T(128)}, f32[8,64]{1,0:T(8,128)S(1)}, ...), condition=%wide.region_9.11_spmd.clone, body=%wide.region_6.10_spmd.clone.sunk | while | flops 136742464 | bytes 4231809 | solution.py:141
  88.9 1.3 %select_reduce_fusion.4 = (f32[8,64]{1,0:T(8,128)S(1)}, f32[8,64,512]{2,1,0:T(8,128)S(1)}) fusion(pred[64,512]{1,0:T(8,128)(4,1)S(1)} %broadcast_compare_fusion.4, bf16[64,8,128]{2,0,1:T(8,128)(2,1)} %get-tuple-element.1337, bf16[512,128]{1,0:T(8,128)(2,1)} %get-tuple-element.1336), kind=kOutput, calls=%fused_computation.10.clone.1 | convolution fusion | flops 67894784 | bytes 1345536 | tf_op jit(solution)/shard_map/while/body/rgd,kd->grk/dot_general | solution.py:133
  90.7 1.3 %convolution_add_fusion.4 = f32[8,64,128]{2,1,0:T(8,128)S(1)} fusion(f32[8,64,512]{2,1,0:T(8,128)S(1)} %get-tuple-element.1120, f32[8,64]{1,0:T(8,128)S(1)} %max.28, pred[64,512]{1,0:T(8,128)(4,1)S(1)} %broadcast_compare_fusion.4, f32[8,64,128]{2,1,0:T(8,128)S(1)} %get-tuple-element.1323, bf16[512,128]{1,0:T(8,128)(2,1)} %get-tuple-element.1338, ...), kind=kOutput, calls=%fused_computation.8.clone.1 | convolution fusion | flops 68026368 | bytes 1740800 | tf_op jit(solution)/shard_map/while/body/grk,kd->grd/dot_general | solution.py:17
  92.2 0.7 convert_element_type.52
  93.0 15.0 %while.69 = (s32[]{:T(128)}, f32[8,64]{1,0:T(8,128)S(1)}, f32[8,64]{1,0:T(8,128)S(1)}, f32[8,64,128]{2,1,0:T(8,128)S(1)}, s32[]{:T(128)}, /*index=5*/pred[8,32]{...) while((s32[]{:T(128)}, f32[8,64]{1,0:T(8,128)S(1)}, ...), condition=%wide.region_14.16_spmd.clone.clone, body=%wide.region_10.15_spmd.clone.clone.sunk | while | flops 552214656 | bytes 22833016 | solution.py:114
  94.6 2.8 %broadcast_in_dim.215 = pred[8,64,32,64]{3,2,1,0:T(32,128)(4,1)S(1)} broadcast(pred[8,64,32]{2,1,0:T(8,128)(4,1)S(1)} %copy.70), dimensions={0,1,2} | broadcast | bytes 1064960 | tf_op jit(solution)/shard_map/while/body/broadcast_in_dim | solution.py:106
  97.4 5.1 %reshape.239 = pred[8,64,2048]{2,1,0:T(32,128)(4,1)S(1)} reshape(pred[8,64,32,64]{3,2,1,0:T(32,128)(4,1)S(1)} %broadcast_in_dim.215) | data formatting | bytes 2097152 | tf_op jit(solution)/shard_map/while/body/reshape | solution.py:106
  103.1 2.2 %fusion.112 = (f32[8,64]{1,0:T(8,128)S(1)}, f32[2048,64,8]{0,1,2:T(8,128)S(1)}) fusion(pred[8,64,2048]{2,1,0:T(32,128)(4,1)S(1)} %reshape.239, pred[2048]{0:T(1024)(128)(4,1)S(1)} %add_compare_fusion.5, bf16[64,8,128]{2,0,1:T(8,128)(2,1)S(1)} %get-tuple-element.1213, bf16[2048,128]{1,0:T(8,128)(2,1)} %get-tuple-element.1212), kind=kOutput, calls=%fused_computation.70.clone.1 | convolution fusion | flops 272629248 | bytes 5902336 | tf_op jit(solution)/shard_map/while/body/rgd,kd->grk/dot_general | solution.py:108
  105.3 1.4 %fusion.113 = f32[8,64]{1,0:T(8,128)S(1)} fusion(f32[2048,64,8]{0,1,2:T(8,128)S(1)} %get-tuple-element.1165, pred[8,64,2048]{2,1,0:T(32,128)(4,1)S(1)} %reshape.239, f32[8,64]{1,0:T(8,128)S(1)} %max.31, pred[2048]{0:T(1024)(128)(4,1)S(1)} %add_compare_fusion.5), kind=kLoop, calls=%fused_computation.74.clone.1 | loop fusion | flops 5242368 | bytes 5249024 | tf_op jit(solution)/shard_map/while/body/reduce_sum | solution.py:16
  106.6 1.3 %fusion.114 = f32[8,64,128]{2,1,0:T(8,128)S(1)} fusion(f32[2048,64,8]{0,1,2:T(8,128)S(1)} %get-tuple-element.1165, pred[8,64,2048]{2,1,0:T(32,128)(4,1)S(1)} %reshape.239, f32[8,64]{1,0:T(8,128)S(1)} %max.31, pred[2048]{0:T(1024)(128)(4,1)S(1)} %add_compare_fusion.5, bf16[2048,128]{1,0:T(8,128)(2,1)S(1)} %copy-done.1, ...), kind=kOutput, calls=%fused_computation.78.clone.1 | convolution fusion | flops 273809408 | bytes 6297600 | tf_op jit(solution)/shard_map/while/body/grk,kd->grd/dot_general | solution.py:17
  108.0 3.1 %while.67 = (s32[]{:T(128)}, f32[8,64]{1,0:T(8,128)S(1)}, f32[8,64]{1,0:T(8,128)S(1)}, f32[8,64,128]{2,1,0:T(8,128)S(1)}, s32[]{:T(128)}, /*index=5*/bf16[512,12...) while((s32[]{:T(128)}, f32[8,64]{1,0:T(8,128)S(1)}, ...), condition=%wide.region_18.20_spmd.clone, body=%wide.region_15.19_spmd.clone.sunk | while | flops 136742464 | bytes 4231809 | solution.py:141
  108.1 1.3 %select_reduce_fusion.5 = (f32[8,64]{1,0:T(8,128)S(1)}, f32[8,64,512]{2,1,0:T(8,128)S(1)}) fusion(pred[64,512]{1,0:T(8,128)(4,1)S(1)} %broadcast_compare_fusion.5, bf16[64,8,128]{2,0,1:T(8,128)(2,1)S(1)} %get-tuple-element.1250, bf16[512,128]{1,0:T(8,128)(2,1)} %get-tuple-element.1249), kind=kOutput, calls=%fused_computation.28.clone.1 | convolution fusion | flops 67894784 | bytes 1345536 | tf_op jit(solution)/shard_map/while/body/rgd,kd->grk/dot_general | solution.py:133
  109.8 1.3 %convolution_add_fusion.5 = f32[8,64,128]{2,1,0:T(8,128)S(1)} fusion(f32[8,64,512]{2,1,0:T(8,128)S(1)} %get-tuple-element.1133, f32[8,64]{1,0:T(8,128)S(1)} %max.29, pred[64,512]{1,0:T(8,128)(4,1)S(1)} %broadcast_compare_fusion.5, f32[8,64,128]{2,1,0:T(8,128)S(1)} %get-tuple-element.1236, bf16[512,128]{1,0:T(8,128)(2,1)} %get-tuple-element.1251, ...), kind=kOutput, calls=%fused_computation.26.clone.1 | convolution fusion | flops 68026368 | bytes 1740800 | tf_op jit(solution)/shard_map/while/body/grk,kd->grd/dot_general | solution.py:17
  111.4 0.7 pad_maximum_fusion
  (91 shorter events, 10.3 us)
Async XLA Ops:
  6.5 25.7 %copy-start.8 = (s32[2]{0:T(128)S(1)}, s32[2]{0:T(128)}, u32[]{:S(2)}) copy-start(s32[2]{0:T(128)} %param.24) | copy-start | bytes 28
  6.5 27.6 %copy-start.7 = (s32[32,16]{0,1:T(8,128)S(1)}, s32[32,16]{0,1:T(8,128)}, u32[]{:S(2)}) copy-start(s32[32,16]{0,1:T(8,128)} %param.26) | copy-start | bytes 6148
  6.5 27.6 %copy-start.6 = (s32[32,16]{0,1:T(8,128)S(1)}, s32[32,16]{0,1:T(8,128)}, u32[]{:S(2)}) copy-start(s32[32,16]{0,1:T(8,128)} %param.27) | copy-start | bytes 6148
  6.5 27.9 %copy-start.3 = (bf16[2,64,1024]{2,1,0:T(8,128)(2,1)S(1)}, bf16[2,64,1024]{2,1,0:T(8,128)(2,1)}, u32[]{:S(2)}) copy-start(bf16[2,64,1024]{2,1,0:T(8,128)(2,1)} %param.19) | copy-start | bytes 786436
  6.5 28.7 %copy-start.4 = (bf16[2,64,128]{2,1,0:T(8,128)(2,1)S(1)}, bf16[2,64,128]{2,1,0:T(8,128)(2,1)}, u32[]{:S(2)}) copy-start(bf16[2,64,128]{2,1,0:T(8,128)(2,1)} %param.20) | copy-start | bytes 98308
  6.5 38.2 %copy-start.5 = (bf16[2,64,128]{2,1,0:T(8,128)(2,1)S(1)}, bf16[2,64,128]{2,1,0:T(8,128)(2,1)}, u32[]{:S(2)}) copy-start(bf16[2,64,128]{2,1,0:T(8,128)(2,1)} %param.21) | copy-start | bytes 98308
  6.6 47.4 %copy-start.9 = (s32[64]{0:T(128)S(1)}, s32[64]{0:T(128)}, u32[]{:S(2)}) copy-start(s32[64]{0:T(128)} %param.25) | copy-start | bytes 772
  6.6 49.0 %all-gather.3.cloned.1.call-start = ((), (), s32[]{:S(2)}) async-start(), calls=%async_computation.2 | async-start | bytes 1179648 | tf_op jit(solution)/shard_map/all_gather | solution.py:67
  21.3 48.9 %all-gather.5.cloned.1.call-start = ((), (), s32[]{:S(2)}) async-start(), calls=%async_computation.3 | async-start | bytes 1179648 | tf_op jit(solution)/shard_map/all_gather | solution.py:68
  86.1 1.4 %copy-start.2 = (bf16[2048,128]{1,0:T(8,128)(2,1)S(1)}, bf16[2048,128]{1,0:T(8,128)(2,1)}, u32[]{:S(2)}) copy-start(bf16[2048,128]{1,0:T(8,128)(2,1)} %get-tuple-element.1301) | copy-start | bytes 1572868 | tf_op jit(solution)/shard_map/while
  105.2 1.4 %copy-start.1 = (bf16[2048,128]{1,0:T(8,128)(2,1)S(1)}, bf16[2048,128]{1,0:T(8,128)(2,1)}, u32[]{:S(2)}) copy-start(bf16[2048,128]{1,0:T(8,128)(2,1)} %get-tuple-element.1214) | copy-start | bytes 1572868 | tf_op jit(solution)/shard_map/while
  108.0 3.4 %copy-start = (bf16[1,64,1024]{2,1,0:T(8,128)(2,1)S(1)}, bf16[1,64,1024]{2,1,0:T(8,128)(2,1)}, u32[]{:S(2)}) copy-start(bf16[1,64,1024]{2,1,0:T(8,128)(2,1)} %convert_element_type.52) | copy-start | bytes 393220
Sparse Core Ops, SparseCore 0:
  21.4 23.1 all-gather.2
  46.5 23.6 all-gather.4
where the time goes:
time: 120 us; the launch traced here: 119 us
  blocking collectives  39.4 us (33%)
  local copies, waits for them, and re-layouts  30.2 us (25%)
  between operations  15.1 us (13%)
  waiting for transfers between devices  12.7 us (11%)
  matrix products  12.1 us (10%)
  other arithmetic  8.8 us (7%)
    all_gather x1, waiting for transfers between devices, body(): lax.all_gather(page_values, ('ctx', 'pool'), axis=0, tiled=True)  12.7 us
    all_to_all x1, blocking collectives, body(): lax.all_to_all(slot_pool_keys, 'head', split_axis=2, concat_axis=0, tiled...  12.2 us
    reshape x2, local copies, waits for them, and re-layouts, prefix_step(): jnp.repeat(chosen, page_len, axis=2) & (key_ids < prefix_len)[None, None, :]  10.2 us
    all_gather x1, blocking collectives, body(): lax.all_gather(stretch_keys, ('ctx', 'pool'), axis=1, tiled=True)  9.56 us
    all_gather x1, blocking collectives, body(): lax.all_gather(stretch_values, ('ctx', 'pool'), axis=1, tiled=True)  9.18 us
    all_to_all x1, blocking collectives, body(): lax.all_to_all(slot_pool_values, 'head', split_axis=2, concat_axis=0, til...  8.44 us
    broadcast_in_dim x2, local copies, waits for them, and re-layouts, prefix_step(): jnp.repeat(chosen, page_len, axis=2) & (key_ids < prefix_len)[None, None, :]  5.57 us
    dot_general x4, matrix products, absorb(): jnp.einsum('grk,kd->grd', weights.astype(jnp.bfloat16), values, preferred...  5.18 us
  transfers between devices with their start and end apart: 2, of which 1 were waited for; matrix products, arithmetic and copies ran while one was open for 6% of the time, Pallas kernels for 0%

commit v1 on v0

--- a/solution.py
+++ b/solution.py
@@ -3,6 +3,8 @@
 import jax
 import jax.numpy as jnp
 from jax import lax
+from jax.experimental import pallas as pl
+from jax.experimental.pallas import tpu as pltpu
 from jax.sharding import PartitionSpec as P
 
 very_low = -1e30
@@ -146,7 +148,239 @@
     return jnp.stack(outputs)
 
 
+page_axes = ("ctx", "pool")
+roles = 4
+hide = -(2.0**126)
+log2e = 1.4426950408889634
+
+
+def split_kernel(
+    pool_keys, pool_values, stretch_keys, stretch_values, first, second, third, early, sems
+):
+    head = lax.axis_index("head")
+    copies = []
+
+    def add(source, target):
+        copy = pltpu.make_async_copy(source, target, sems.at[len(copies)])
+        copy.start()
+        copies.append(copy)
+
+    for shift, target in ((3, third), (2, second), (1, first), (0, None)):
+        columns = pl.ds(pl.multiple_of((head ^ shift) * 128, 128), 128)
+        for which, pool in enumerate((pool_keys, pool_values)):
+            place = early.at[2 + which] if target is None else target.at[which]
+            add(pool.at[:, :, columns], place)
+    add(stretch_keys, early.at[0])
+    add(stretch_values, early.at[1])
+    for copy in copies:
+        copy.wait()
+
+
+def split(pool_keys, pool_values, stretch_keys, stretch_values):
+    piece = pltpu.VMEM((2, 2, 64, 128), jnp.bfloat16)
+    bundle = pltpu.VMEM((4, 2, 64, 128), jnp.bfloat16)
+    return pl.pallas_call(
+        split_kernel,
+        out_shape=(piece, piece, piece, bundle),
+        in_specs=[pl.BlockSpec(memory_space=pl.ANY)] * 4,
+        out_specs=[pl.BlockSpec(memory_space=pltpu.VMEM)] * 4,
+        scratch_shapes=[pltpu.SemaphoreType.DMA((10,))],
+        name="split",
+    )(pool_keys, pool_values, stretch_keys, stretch_values)
+
+
+def mask_kernel(lengths, queries, vertical, slash, wide_queries, key_tags):
+    head = lax.axis_index("head")
+    plane = lax.axis_index("ctx") * 2 + lax.axis_index("pool")
+    first_row = plane * 64
+    rows8 = pl.ds(pl.multiple_of(head * 8, 8), 8)
+    vert_rows = vertical[rows8, :]
+    slash_rows = slash[rows8, :]
+    lane8 = lax.broadcasted_iota(jnp.int32, (8, 128), 1)
+    lane = lax.broadcasted_iota(jnp.int32, (64, 128), 1)
+    row = lax.broadcasted_iota(jnp.int32, (64, 128), 0)
+    vert_hit = lane8 < 0
+    for entry in range(16):
+        vert_hit = vert_hit | (vert_rows[:, entry : entry + 1] == lane8)
+    causal = jnp.where(lane - 64 <= row, 0.0, hide)
+    for prompt in range(2):
+        length = lengths[prompt]
+        base_page = (length + first_row) // 64
+        cut = (base_page + 1) * 64 - length - first_row
+        tables = []
+        for step in range(2):
+            hit = vert_hit
+            distance = base_page + step - lane8
+            for entry in range(16):
+                hit = hit | (slash_rows[:, entry : entry + 1] == distance)
+            hit = hit & (lane8 * 64 < length)
+            shown = (hit & (lane8 < 32)) | (lane8 > 33)
+            tables.append(jnp.where(shown, 0.0, hide))
+        for group in range(8):
+            own = slice(group * 64, (group + 1) * 64)
+            bias = jnp.where(
+                row < cut, tables[0][group : group + 1, :], tables[1][group : group + 1, :]
+            )
+            bias = jnp.where(lane < 64, bias, causal)
+            wide_queries[prompt, own, :128] = queries[prompt, :, group * 128 : (group + 1) * 128]
+            wide_queries[prompt, own, 128:] = bias.astype(jnp.bfloat16)
+        for page in range(32):
+            tag = (lane == page) | ((lane == 32) & (row + page * 64 >= length))
+            key_tags[prompt, page * 64 : (page + 1) * 64, :] = jnp.where(tag, 1.0, 0.0).astype(
+                jnp.bfloat16
+            )
+        for page in range(8):
+            diagonal = (lane - 64 == row) & (plane == page)
+            tag = diagonal | ((lane == 33) & (plane < page))
+            key_tags[prompt, 2048 + page * 64 : 2048 + (page + 1) * 64, :] = jnp.where(
+                tag, 1.0, 0.0
+            ).astype(jnp.bfloat16)
+
+
+def mask(lengths, queries, vertical, slash):
+    return pl.pallas_call(
+        mask_kernel,
+        out_shape=(
+            pltpu.VMEM((2, 512, 256), jnp.bfloat16),
+            pltpu.VMEM((2, 2560, 128), jnp.bfloat16),
+        ),
+        in_specs=[pl.BlockSpec(memory_space=pltpu.SMEM)]
+        + [pl.BlockSpec(memory_space=pltpu.VMEM)] * 3,
+        out_specs=[pl.BlockSpec(memory_space=pltpu.VMEM)] * 2,
+        name="mask",
+    )(lengths, queries, vertical, slash)
+
+
+def attend_kernel(table, wide_queries, key_tags, *rest):
+    early, late = rest[:8], rest[8:16]
+    result, where_is, keys, values = rest[16:]
+    ctx, head, pool = lax.axis_index("ctx"), lax.axis_index("head"), lax.axis_index("pool")
+
+    def invert(index, carry):
+        where_is[table[index]] = (index // 32) * 2560 + (index % 32) * 64
+        return carry
+
+    lax.fori_loop(0, 64, invert, 0)
+    for other in range(2):
+        from_pool = pool ^ other
+        for role in range(roles):
+            near = (0, 1 + from_pool, 2 - from_pool, 3)[role]
+            from_ctx = ctx ^ near
+            bundle, pieces = early[other * 4 + role], late[other * 4 + role]
+            for prompt in range(2):
+                start = pl.multiple_of(
+                    prompt * 2560 + 2048 + (from_ctx * 2 + from_pool) * 64, 64
+                )
+                keys[pl.ds(start, 64), :] = bundle[0, prompt]
+                values[pl.ds(start, 64), :] = bundle[1, prompt]
+            for shift in range(4):
+                first_slot = ((from_ctx * 4 + (head ^ shift)) * 2 + from_pool) * 2
+                for within in range(2):
+                    start = pl.multiple_of(where_is[first_slot + within], 64)
+                    if shift == 0:
+                        page_keys, page_values = bundle[2, within], bundle[3, within]
+                    else:
+                        page_keys = pieces[shift - 1, 0, within]
+                        page_values = pieces[shift - 1, 1, within]
+                    keys[pl.ds(start, 64), :] = page_keys
+                    values[pl.ds(start, 64), :] = page_values
+    scale = log2e / math.sqrt(128.0)
+    ones = jnp.ones((2560, 128), jnp.bfloat16)
+    for prompt in range(2):
+        span = slice(prompt * 2560, (prompt + 1) * 2560)
+        wide_keys = jnp.concatenate([keys[span, :], key_tags[prompt]], axis=1)
+        wide_values = jnp.concatenate([values[span, :], ones], axis=1)
+        for part in range(2):
+            scores = lax.dot_general(
+                wide_queries[prompt, part * 256 : (part + 1) * 256, :],
+                wide_keys,
+                (((1,), (1,)), ((), ())),
+                preferred_element_type=jnp.float32,
+            )
+            highest = jnp.max(scores, axis=1, keepdims=True)
+            weights = jnp.exp2((scores - highest) * scale).astype(jnp.bfloat16)
+            sums = jnp.dot(weights, wide_values, preferred_element_type=jnp.float32)
+            attended = (sums[:, :128] / sums[:, 128:]).astype(jnp.bfloat16)
+            for group in range(4):
+                column = (part * 4 + group) * 128
+                result[prompt, :, column : column + 128] = attended[
+                    group * 64 : (group + 1) * 64, :
+                ]
+
+
+def attend(table, wide_queries, key_tags, early, late):
+    vmem = pl.BlockSpec(memory_space=pltpu.VMEM)
+    return pl.pallas_call(
+        attend_kernel,
+        out_shape=jax.ShapeDtypeStruct((2, 64, 1024), jnp.bfloat16),
+        in_specs=[pl.BlockSpec(memory_space=pltpu.SMEM)] + [vmem] * 18,
+        out_specs=vmem,
+        scratch_shapes=[
+            pltpu.SMEM((64,), jnp.int32),
+            pltpu.VMEM((5120, 128), jnp.bfloat16),
+            pltpu.VMEM((5120, 128), jnp.bfloat16),
+        ],
+        compiler_params=pltpu.CompilerParams(vmem_limit_bytes=40 * 2**20),
+        name="attend",
+    )(table, wide_queries, key_tags, *early, *late)
+
+
+def to_first(value):
+    pairs = [(2 * c + p, 2 * (c ^ (1 + p)) + p) for c in range(4) for p in range(2)]
+    return lax.ppermute(value, page_axes, pairs)
+
+
+def to_second(value):
+    pairs = [(2 * c + p, 2 * (c ^ (2 - p)) + p) for c in range(4) for p in range(2)]
+    return lax.ppermute(value, page_axes, pairs)
+
+
+def to_sibling(value):
+    return lax.ppermute(value, "pool", [(0, 1), (1, 0)])
+
+
+def spread(value):
+    by_first = to_first(value)
+    by_second = to_second(value)
+    by_both = to_second(by_first)
+    return [value, by_first, by_second, by_both]
+
+
+def with_sibling(mine):
+    return mine + [to_sibling(one) for one in mine]
+
+
+def small_body(
+    queries,
+    stretch_keys,
+    stretch_values,
+    slot_pool_keys,
+    slot_pool_values,
+    prefix_lengths,
+    page_slot_table,
+    vertical,
+    slash,
+):
+    first, second, third, bundle = split(
+        slot_pool_keys, slot_pool_values, stretch_keys, stretch_values
+    )
+    arrived = [
+        lax.ppermute(piece, "head", [(z, z ^ shift) for z in range(4)])
+        for shift, piece in ((3, third), (2, second), (1, first))
+    ]
+    arrived.reverse()
+    wide_queries, key_tags = mask(prefix_lengths, queries, vertical, slash)
+    by_first, by_second = to_first(bundle), to_second(bundle)
+    arrived, by_first, by_second, wide_queries, key_tags = lax.optimization_barrier(
+        (arrived, by_first, by_second, wide_queries, key_tags)
+    )
+    early = with_sibling([bundle, by_first, by_second, to_second(by_first)])
+    late = with_sibling(spread(jnp.stack(arrived)))
+    return attend(page_slot_table, wide_queries, key_tags, early, late)
+
+
 def solution(mesh):
+    small = tuple(mesh.shape[axis] for axis in ("ctx", "head", "pool")) == (4, 4, 2)
     in_specs = (
         P(None, ("ctx", "pool"), "head"),
         P(None, ("ctx", "pool"), "head"),
@@ -159,4 +393,10 @@
         P(),
     )
     out_specs = P(None, ("ctx", "pool"), "head")
-    return jax.shard_map(body, mesh=mesh, in_specs=in_specs, out_specs=out_specs, check_vma=False)
+    return jax.shard_map(
+        small_body if small else body,
+        mesh=mesh,
+        in_specs=in_specs,
+        out_specs=out_specs,
+        check_vma=False,
+    )

time: 120 us -> 39 us (0.33)
  blocking collectives: 39.4 us -> 0 us
  local copies, waits for them, and re-layouts: 30.2 us -> 3.39 us
  between operations: 15.1 us -> 0.07 us
  starting transfers between devices: 0.08 us -> 13.1 us
  matrix products: 12.1 us -> 0 us
  Pallas kernels: 0 us -> 9.03 us
  other arithmetic: 8.8 us -> 0.02 us
    all_to_all x2 -> x0, blocking collectives: 20.6 us -> none  [the longest x1 12.2 us: body(): lax.all_to_all(slot_pool_keys, 'head', split_axis=2, concat_axis=0, tiled...]
    all_gather x2 -> x0, blocking collectives: 18.7 us -> none  [the longest x1 9.56 us: body(): lax.all_gather(stretch_keys, ('ctx', 'pool'), axis=1, tiled=True)]
    ppermute x0 -> x17, starting transfers between devices: none -> 13.1 us  [the longest x4 5.56 us: to_second(): return lax.ppermute(value, page_axes, pairs)]
    ppermute x0 -> x17, waiting for transfers between devices: none -> 13.1 us  [the longest x2 6.66 us: to_first(): return lax.ppermute(value, page_axes, pairs)]
    all_gather x2 -> x0, waiting for transfers between devices: 12.7 us -> none  [the longest x1 12.7 us: body(): lax.all_gather(page_values, ('ctx', 'pool'), axis=0, tiled=True)]
    dot_general x8 -> x0, matrix products: 12.1 us -> none  [the longest x4 5.18 us: absorb(): jnp.einsum('grk,kd->grd', weights.astype(jnp.bfloat16), values, preferred...]
    reshape x2 -> x0, local copies, waits for them, and re-layouts: 10.2 us -> none  [prefix_step(): jnp.repeat(chosen, page_len, axis=2) & (key_ids < prefix_len)[None, None, :]]
    pallas_call x0 -> x3, Pallas kernels: none -> 9.03 us  [the longest x1 6.05 us: attend(): pl.pallas_call(attend_kernel, out_shape=jax.ShapeDtypeStruct((2, 64, 1024...]
  transfers between devices with their start and end apart: 2 -> 17, of which waited for: 1 -> 5; matrix products, arithmetic and copies ran while one was open for 6% -> 7% of each run, Pallas kernels for 0% -> 5%
where the time goes in v1:
time: 39 us; the launch traced here: 38.7 us
  starting transfers between devices  13.1 us (34%)
  waiting for transfers between devices  13.1 us (34%)
  Pallas kernels  9.03 us (23%)
  local copies, waits for them, and re-layouts  3.39 us (9%)
    ppermute x2, waiting for transfers between devices, to_first(): return lax.ppermute(value, page_axes, pairs)  6.66 us
    pallas_call x1, Pallas kernels, attend(): pl.pallas_call(attend_kernel, out_shape=jax.ShapeDtypeStruct((2, 64, 1024...  6.05 us
    ppermute x4, starting transfers between devices, to_second(): return lax.ppermute(value, page_axes, pairs)  5.56 us
    ppermute x3, starting transfers between devices, small_body(): lax.ppermute(piece, 'head', [(z, z ^ shift) for z in range(4)])  4.39 us
    ppermute x4, waiting for transfers between devices, to_second(): return lax.ppermute(value, page_axes, pairs)  3.94 us
    unnamed x4, local copies, waits for them, and re-layouts  3.39 us
    ppermute x2, starting transfers between devices, to_first(): return lax.ppermute(value, page_axes, pairs)  2.09 us
    pallas_call x1, Pallas kernels, mask(): pl.pallas_call(mask_kernel, out_shape=(pltpu.VMEM((2, 512, 256), jnp.bflo...  1.98 us
  transfers between devices with their start and end apart: 17, of which 5 were waited for; matrix products, arithmetic and copies ran while one was open for 7% of the time, Pallas kernels for 5%

profile of v1, /device:TPU:0, one launch (start us, length us, event | category | flops | bytes accessed | tf_op | source)
XLA Modules:
  0.0 38.7 jit_solution(7474999638593111994)
XLA Ops:
  0.0 1.0 %split.1 = (bf16[2,2,64,128]{3,2,1,0:T(8,128)(2,1)S(1)}, bf16[2,2,64,128]{3,2,1,0:T(8,128)(2,1)S(1)}, bf16[2,2,64,128]{3,2,1,0:T(8,128)(2,1)S(1)}, bf16[4,2,64,128]{3,2,1,0:T(8,128)(2,1)S(1)}) custom-call(bf16[2,64,512]{2,1,0:T(8,128)(2,1)} %pool_keys.1, bf16[2,64,512]{2,1,0:T(8,128)(2,1)} %pool_values.1, bf16[2,64,128]{2,1,0:T(8,128)(2,1)} %stretch_keys.1, ...), custom_call_target="tpu_custom_call" | custom-call | tf_op jit(solution)/shard_map/split/pallas_call | solution.py:182
  1.0 3.0 %collective-permute-start.4 = (bf16[4,2,64,128]{3,2,1,0:T(8,128)(2,1)S(1)}, bf16[4,2,64,128]{3,2,1,0:T(8,128)(2,1)S(1)}, u32[]{:S(2)}, u32[]{:S(2)}) collective-permute-start(bf16[4,2,64,128]{3,2,1,0:T(8,128)(2,1)S(1)} %get-tuple-element.21.rest_0_), channel_id=1, source_target_pairs={{0,16},{1,9},{8,24},{9,1},{16,0},{17,25},{24,8},{25,17},{2,18},{3,... | collective-permute-start | bytes 393224 | tf_op jit(solution)/shard_map/ppermute | solution.py:335
  4.0 1.5 %collective-permute-start.3 = (bf16[4,2,64,128]{3,2,1,0:T(8,128)(2,1)S(1)}, bf16[4,2,64,128]{3,2,1,0:T(8,128)(2,1)S(1)}, u32[]{:S(2)}, u32[]{:S(2)}) collective-permute-start(bf16[4,2,64,128]{3,2,1,0:T(8,128)(2,1)S(1)} %get-tuple-element.21.rest_0_), channel_id=1, source_target_pairs={{0,8},{1,17},{8,0},{9,25},{16,24},{17,1},{24,16},{25,9},{2,10},{3,... | collective-permute-start | bytes 393224 | tf_op jit(solution)/shard_map/ppermute | solution.py:330
  5.5 1.6 %collective-permute-start = (bf16[2,2,64,128]{3,2,1,0:T(8,128)(2,1)S(1)}, bf16[2,2,64,128]{3,2,1,0:T(8,128)(2,1)S(1)}, u32[]{:S(2)}, u32[]{:S(2)}) collective-permute-start(bf16[2,2,64,128]{3,2,1,0:T(8,128)(2,1)S(1)} %get-tuple-element.18), channel_id=1, source_target_pairs={{0,2},{2,0},{4,6},{6,4},{1,3},{3,1},{5,7},{7,5},{8,10},{10,8},{12,... | collective-permute-start | bytes 196616 | tf_op jit(solution)/shard_map/ppermute | solution.py:368
  7.1 2.6 %collective-permute-start.1 = (bf16[2,2,64,128]{3,2,1,0:T(8,128)(2,1)S(1)}, bf16[2,2,64,128]{3,2,1,0:T(8,128)(2,1)S(1)}, u32[]{:S(2)}, u32[]{:S(2)}) collective-permute-start(bf16[2,2,64,128]{3,2,1,0:T(8,128)(2,1)S(1)} %get-tuple-element.19), channel_id=1, source_target_pairs={{0,4},{2,6},{4,0},{6,2},{1,5},{3,7},{5,1},{7,3},{8,12},{10,14},{12... | collective-permute-start | bytes 196616 | tf_op jit(solution)/shard_map/ppermute | solution.py:368
  9.7 0.2 collective-permute-start.2
  9.9 1.4 %copy.10.vertical = s32[32,16]{1,0:T(8,128)} copy(s32[32,16]{0,1:T(8,128)} %param.16) | data formatting | bytes 4096 | tf_op args[7]
  11.3 1.4 %copy.11.slash = s32[32,16]{1,0:T(8,128)} copy(s32[32,16]{0,1:T(8,128)} %param.17) | data formatting | bytes 4096 | tf_op args[8]
  12.7 2.0 %mask.1 = (bf16[2,512,256]{2,1,0:T(8,128)(2,1)S(1)}, bf16[2,2560,128]{2,1,0:T(8,128)(2,1)S(1)}) custom-call(s32[2]{0:T(128)} %lengths.1, bf16[2,64,1024]{2,1,0:T(8,128)(2,1)} %queries.1, s32[32,16]{1,0:T(8,128)} %copy.10.vertical, s32[32,16]{1,0:T(8,128)} %copy.11.slash), custom_call_target="tpu_custom_call" | custom-call | tf_op jit(solution)/shard_map/mask/pallas_call | solution.py:241
  14.6 0.0 collective-permute-done
  14.7 1.1 %collective-permute-done.2 = bf16[2,2,64,128]{3,2,1,0:T(8,128)(2,1)S(1)} collective-permute-done((bf16[2,2,64,128]{3,2,1,0:T(8,128)(2,1)S(1)}, bf16[2,2,64,128]{3,2,1,0:T(8,128)(2,1)S(1)}, u32[]{:S(2)}, u32[]{:S(2)}) %collective-permute-start.2) | collective-permute-done | bytes 65568 | tf_op jit(solution)/shard_map/ppermute | solution.py:368
  15.8 0.6 %collective-permute-start.10 = (bf16[3,2,2,64,128]{4,3,2,1,0:T(8,128)(2,1)S(1)}, bf16[3,2,2,64,128]{4,3,2,1,0:T(8,128)(2,1)S(1)}, u32[]{:S(2)}, u32[]{:S(2)}) collective-permute-start(bf16[3,2,2,64,128]{4,3,2,1,0:T(8,128)(2,1)S(1)} %pad_maximum_fusion.rest_8_), channel_id=1, source_target_pairs={{0,8},{1,17},{8,0},{9,25},{16,24},{17,1},{24,16},{25,9},{2,10},{3,... | collective-permute-start | bytes 589832 | tf_op jit(solution)/shard_map/ppermute | solution.py:330
  16.4 0.5 %collective-permute-start.11 = (bf16[3,2,2,64,128]{4,3,2,1,0:T(8,128)(2,1)S(1)}, bf16[3,2,2,64,128]{4,3,2,1,0:T(8,128)(2,1)S(1)}, u32[]{:S(2)}, u32[]{:S(2)}) collective-permute-start(bf16[3,2,2,64,128]{4,3,2,1,0:T(8,128)(2,1)S(1)} %pad_maximum_fusion.rest_8_), channel_id=1, source_target_pairs={{0,16},{1,9},{8,24},{9,1},{16,0},{17,25},{24,8},{25,17},{2,18},{3,... | collective-permute-start | bytes 589832 | tf_op jit(solution)/shard_map/ppermute | solution.py:335
  16.9 6.7 %collective-permute-done.10.rest_9_ = bf16[3,2,2,64,128]{4,3,2,1,0:T(8,128)(2,1)S(1)} collective-permute-done((bf16[3,2,2,64,128]{4,3,2,1,0:T(8,128)(2,1)S(1)}, bf16[3,2,2,64,128]{4,3,2,1,0:T(8,128)(2,1)S(1)}, u32[]{:S(2)}, u32[]{:S(2)}) %collective-permute-start.10) | collective-permute-done | bytes 196640 | tf_op jit(solution)/shard_map/ppermute | solution.py:330
  23.6 0.5 %collective-permute-start.12 = (bf16[3,2,2,64,128]{4,3,2,1,0:T(8,128)(2,1)S(1)}, bf16[3,2,2,64,128]{4,3,2,1,0:T(8,128)(2,1)S(1)}, u32[]{:S(2)}, u32[]{:S(2)}) collective-permute-start(bf16[3,2,2,64,128]{4,3,2,1,0:T(8,128)(2,1)S(1)} %collective-permute-done.10.rest_9_), channel_id=1, source_target_pairs={{0,16},{1,9},{8,24},{9,1},{16,0},{17,25},{24,8},{25,17},{2,18},{3,... | collective-permute-start | bytes 589832 | tf_op jit(solution)/shard_map/ppermute | solution.py:335
  24.1 0.0 collective-permute-start.8
  24.1 0.5 %collective-permute-start.7 = (bf16[4,2,64,128]{3,2,1,0:T(8,128)(2,1)S(1)}, bf16[4,2,64,128]{3,2,1,0:T(8,128)(2,1)S(1)}, u32[]{:S(2)}, u32[]{:S(2)}) collective-permute-start(bf16[4,2,64,128]{3,2,1,0:T(8,128)(2,1)S(1)} %collective-permute-done.3.rest_1_), channel_id=1, source_target_pairs={{0,1},{1,0},{2,3},{3,2},{4,5},{5,4},{6,7},{7,6},{8,9},{9,8},{10,11... | collective-permute-start | bytes 393224 | tf_op jit(solution)/shard_map/ppermute | solution.py:339
  24.6 1.5 %collective-permute-start.5 = (bf16[4,2,64,128]{3,2,1,0:T(8,128)(2,1)S(1)}, bf16[4,2,64,128]{3,2,1,0:T(8,128)(2,1)S(1)}, u32[]{:S(2)}, u32[]{:S(2)}) collective-permute-start(bf16[4,2,64,128]{3,2,1,0:T(8,128)(2,1)S(1)} %collective-permute-done.3.rest_1_), channel_id=1, source_target_pairs={{0,16},{1,9},{8,24},{9,1},{16,0},{17,25},{24,8},{25,17},{2,18},{3,... | collective-permute-start | bytes 393224 | tf_op jit(solution)/shard_map/ppermute | solution.py:335
  26.1 0.5 %collective-permute-start.14 = (bf16[3,2,2,64,128]{4,3,2,1,0:T(8,128)(2,1)S(1)}, bf16[3,2,2,64,128]{4,3,2,1,0:T(8,128)(2,1)S(1)}, u32[]{:S(2)}, u32[]{:S(2)}) collective-permute-start(bf16[3,2,2,64,128]{4,3,2,1,0:T(8,128)(2,1)S(1)} %collective-permute-done.10.rest_9_), channel_id=1, source_target_pairs={{0,1},{1,0},{2,3},{3,2},{4,5},{5,4},{6,7},{7,6},{8,9},{9,8},{10,11... | collective-permute-start | bytes 589832 | tf_op jit(solution)/shard_map/ppermute | solution.py:339
  26.6 0.1 collective-permute-start.15
  26.7 2.5 %collective-permute-done.12.rest_11_ = bf16[3,2,2,64,128]{4,3,2,1,0:T(8,128)(2,1)S(1)} collective-permute-done((bf16[3,2,2,64,128]{4,3,2,1,0:T(8,128)(2,1)S(1)}, bf16[3,2,2,64,128]{4,3,2,1,0:T(8,128)(2,1)S(1)}, u32[]{:S(2)}, u32[]{:S(2)}) %collective-permute-start.12) | collective-permute-done | bytes 196640 | tf_op jit(solution)/shard_map/ppermute | solution.py:335
  29.2 0.0 collective-permute-start.16
  29.2 1.4 %collective-permute-done.5.rest_3_ = bf16[4,2,64,128]{3,2,1,0:T(8,128)(2,1)S(1)} collective-permute-done((bf16[4,2,64,128]{3,2,1,0:T(8,128)(2,1)S(1)}, bf16[4,2,64,128]{3,2,1,0:T(8,128)(2,1)S(1)}, u32[]{:S(2)}, u32[]{:S(2)}) %collective-permute-start.5) | collective-permute-done | bytes 131104 | tf_op jit(solution)/shard_map/ppermute | solution.py:335
  30.6 0.0 collective-permute-start.9
  30.6 0.0 collective-permute-done.13.rest_12_
  30.6 1.3 %collective-permute-done.9.rest_7_ = bf16[4,2,64,128]{3,2,1,0:T(8,128)(2,1)S(1)} collective-permute-done((bf16[4,2,64,128]{3,2,1,0:T(8,128)(2,1)S(1)}, bf16[4,2,64,128]{3,2,1,0:T(8,128)(2,1)S(1)}, u32[]{:S(2)}, u32[]{:S(2)}) %collective-permute-start.9) | collective-permute-done | bytes 131104 | tf_op jit(solution)/shard_map/ppermute | solution.py:339
  32.0 0.0 collective-permute-done.15.rest_14_
  32.0 0.0 collective-permute-done.14.rest_13_
  32.0 0.0 collective-permute-done.16.rest_15_
  32.0 0.0 copy-start
  32.0 0.6 %copy-done = s32[64]{0:T(128)S(1)} copy-done((s32[64]{0:T(128)S(1)}, s32[64]{0:T(128)}, u32[]{:S(2)}) %copy-start) | copy-done | bytes 280
  32.7 6.1 %attend.1 = bf16[2,64,1024]{2,1,0:T(8,128)(2,1)} custom-call(s32[64]{0:T(128)S(1)} %copy-done, bf16[2,512,256]{2,1,0:T(8,128)(2,1)S(1)} %get-tuple-element.24.wide_queries, bf16[2,2560,128]{2,1,0:T(8,128)(2,1)S(1)} %get-tuple-element.25.key_tags, bf16[4,2,64,128]{3,2,1,0:T(8,128)(2,1)S(1)} %get-tuple-element.21.rest_0_, ...), custom_call_target="tpu_custom_call" | custom-call | tf_op jit(solution)/shard_map/attend/pallas_call | solution.py:313
  (10 shorter events, 0.0 us)
Async XLA Ops:
  1.0 14.8 %collective-permute-start.4 = (bf16[4,2,64,128]{3,2,1,0:T(8,128)(2,1)S(1)}, bf16[4,2,64,128]{3,2,1,0:T(8,128)(2,1)S(1)}, u32[]{:S(2)}, u32[]{:S(2)}) collective-permute-start(bf16[4,2,64,128]{3,2,1,0:T(8,128)(2,1)S(1)} %get-tuple-element.21.rest_0_), channel_id=1, source_target_pairs={{0,16},{1,9},{8,24},{9,1},{16,0},{17,25},{24,8},{25,17},{2,18},{3,... | collective-permute-start | bytes 393224 | tf_op jit(solution)/shard_map/ppermute | solution.py:335
  4.0 11.7 %collective-permute-start.3 = (bf16[4,2,64,128]{3,2,1,0:T(8,128)(2,1)S(1)}, bf16[4,2,64,128]{3,2,1,0:T(8,128)(2,1)S(1)}, u32[]{:S(2)}, u32[]{:S(2)}) collective-permute-start(bf16[4,2,64,128]{3,2,1,0:T(8,128)(2,1)S(1)} %get-tuple-element.21.rest_0_), channel_id=1, source_target_pairs={{0,8},{1,17},{8,0},{9,25},{16,24},{17,1},{24,16},{25,9},{2,10},{3,... | collective-permute-start | bytes 393224 | tf_op jit(solution)/shard_map/ppermute | solution.py:330
  5.5 9.1 %collective-permute-start = (bf16[2,2,64,128]{3,2,1,0:T(8,128)(2,1)S(1)}, bf16[2,2,64,128]{3,2,1,0:T(8,128)(2,1)S(1)}, u32[]{:S(2)}, u32[]{:S(2)}) collective-permute-start(bf16[2,2,64,128]{3,2,1,0:T(8,128)(2,1)S(1)} %get-tuple-element.18), channel_id=1, source_target_pairs={{0,2},{2,0},{4,6},{6,4},{1,3},{3,1},{5,7},{7,5},{8,10},{10,8},{12,... | collective-permute-start | bytes 196616 | tf_op jit(solution)/shard_map/ppermute | solution.py:368
  7.1 7.6 %collective-permute-start.1 = (bf16[2,2,64,128]{3,2,1,0:T(8,128)(2,1)S(1)}, bf16[2,2,64,128]{3,2,1,0:T(8,128)(2,1)S(1)}, u32[]{:S(2)}, u32[]{:S(2)}) collective-permute-start(bf16[2,2,64,128]{3,2,1,0:T(8,128)(2,1)S(1)} %get-tuple-element.19), channel_id=1, source_target_pairs={{0,4},{2,6},{4,0},{6,2},{1,5},{3,7},{5,1},{7,3},{8,12},{10,14},{12... | collective-permute-start | bytes 196616 | tf_op jit(solution)/shard_map/ppermute | solution.py:368
  9.7 6.1 %collective-permute-start.2 = (bf16[2,2,64,128]{3,2,1,0:T(8,128)(2,1)S(1)}, bf16[2,2,64,128]{3,2,1,0:T(8,128)(2,1)S(1)}, u32[]{:S(2)}, u32[]{:S(2)}) collective-permute-start(bf16[2,2,64,128]{3,2,1,0:T(8,128)(2,1)S(1)} %get-tuple-element.20), channel_id=1, source_target_pairs={{0,6},{2,4},{4,2},{6,0},{1,7},{3,5},{5,3},{7,1},{8,14},{10,12},{12... | collective-permute-start | bytes 196616 | tf_op jit(solution)/shard_map/ppermute | solution.py:368
  15.8 7.8 %collective-permute-start.10 = (bf16[3,2,2,64,128]{4,3,2,1,0:T(8,128)(2,1)S(1)}, bf16[3,2,2,64,128]{4,3,2,1,0:T(8,128)(2,1)S(1)}, u32[]{:S(2)}, u32[]{:S(2)}) collective-permute-start(bf16[3,2,2,64,128]{4,3,2,1,0:T(8,128)(2,1)S(1)} %pad_maximum_fusion.rest_8_), channel_id=1, source_target_pairs={{0,8},{1,17},{8,0},{9,25},{16,24},{17,1},{24,16},{25,9},{2,10},{3,... | collective-permute-start | bytes 589832 | tf_op jit(solution)/shard_map/ppermute | solution.py:330
  16.4 8.2 %collective-permute-start.6 = (bf16[4,2,64,128]{3,2,1,0:T(8,128)(2,1)S(1)}, bf16[4,2,64,128]{3,2,1,0:T(8,128)(2,1)S(1)}, u32[]{:S(2)}, u32[]{:S(2)}) collective-permute-start(bf16[4,2,64,128]{3,2,1,0:T(8,128)(2,1)S(1)} %get-tuple-element.21.rest_0_), channel_id=1, source_target_pairs={{0,1},{1,0},{2,3},{3,2},{4,5},{5,4},{6,7},{7,6},{8,9},{9,8},{10,11... | collective-permute-start | bytes 393224 | tf_op jit(solution)/shard_map/ppermute | solution.py:339
  16.4 10.2 %collective-permute-start.11 = (bf16[3,2,2,64,128]{4,3,2,1,0:T(8,128)(2,1)S(1)}, bf16[3,2,2,64,128]{4,3,2,1,0:T(8,128)(2,1)S(1)}, u32[]{:S(2)}, u32[]{:S(2)}) collective-permute-start(bf16[3,2,2,64,128]{4,3,2,1,0:T(8,128)(2,1)S(1)} %pad_maximum_fusion.rest_8_), channel_id=1, source_target_pairs={{0,16},{1,9},{8,24},{9,1},{16,0},{17,25},{24,8},{25,17},{2,18},{3,... | collective-permute-start | bytes 589832 | tf_op jit(solution)/shard_map/ppermute | solution.py:335
  23.6 5.7 %collective-permute-start.12 = (bf16[3,2,2,64,128]{4,3,2,1,0:T(8,128)(2,1)S(1)}, bf16[3,2,2,64,128]{4,3,2,1,0:T(8,128)(2,1)S(1)}, u32[]{:S(2)}, u32[]{:S(2)}) collective-permute-start(bf16[3,2,2,64,128]{4,3,2,1,0:T(8,128)(2,1)S(1)} %collective-permute-done.10.rest_9_), channel_id=1, source_target_pairs={{0,16},{1,9},{8,24},{9,1},{16,0},{17,25},{24,8},{25,17},{2,18},{3,... | collective-permute-start | bytes 589832 | tf_op jit(solution)/shard_map/ppermute | solution.py:335
  24.1 2.0 %collective-permute-start.8 = (bf16[4,2,64,128]{3,2,1,0:T(8,128)(2,1)S(1)}, bf16[4,2,64,128]{3,2,1,0:T(8,128)(2,1)S(1)}, u32[]{:S(2)}, u32[]{:S(2)}) collective-permute-start(bf16[4,2,64,128]{3,2,1,0:T(8,128)(2,1)S(1)} %collective-permute-done.4.rest_2_), channel_id=1, source_target_pairs={{0,1},{1,0},{2,3},{3,2},{4,5},{5,4},{6,7},{7,6},{8,9},{9,8},{10,11... | collective-permute-start | bytes 393224 | tf_op jit(solution)/shard_map/ppermute | solution.py:339
  24.1 2.0 %collective-permute-start.7 = (bf16[4,2,64,128]{3,2,1,0:T(8,128)(2,1)S(1)}, bf16[4,2,64,128]{3,2,1,0:T(8,128)(2,1)S(1)}, u32[]{:S(2)}, u32[]{:S(2)}) collective-permute-start(bf16[4,2,64,128]{3,2,1,0:T(8,128)(2,1)S(1)} %collective-permute-done.3.rest_1_), channel_id=1, source_target_pairs={{0,1},{1,0},{2,3},{3,2},{4,5},{5,4},{6,7},{7,6},{8,9},{9,8},{10,11... | collective-permute-start | bytes 393224 | tf_op jit(solution)/shard_map/ppermute | solution.py:339
  24.6 6.1 %collective-permute-start.5 = (bf16[4,2,64,128]{3,2,1,0:T(8,128)(2,1)S(1)}, bf16[4,2,64,128]{3,2,1,0:T(8,128)(2,1)S(1)}, u32[]{:S(2)}, u32[]{:S(2)}) collective-permute-start(bf16[4,2,64,128]{3,2,1,0:T(8,128)(2,1)S(1)} %collective-permute-done.3.rest_1_), channel_id=1, source_target_pairs={{0,16},{1,9},{8,24},{9,1},{16,0},{17,25},{24,8},{25,17},{2,18},{3,... | collective-permute-start | bytes 393224 | tf_op jit(solution)/shard_map/ppermute | solution.py:335
  26.1 4.5 %collective-permute-start.13 = (bf16[3,2,2,64,128]{4,3,2,1,0:T(8,128)(2,1)S(1)}, bf16[3,2,2,64,128]{4,3,2,1,0:T(8,128)(2,1)S(1)}, u32[]{:S(2)}, u32[]{:S(2)}) collective-permute-start(bf16[3,2,2,64,128]{4,3,2,1,0:T(8,128)(2,1)S(1)} %pad_maximum_fusion.rest_8_), channel_id=1, source_target_pairs={{0,1},{1,0},{2,3},{3,2},{4,5},{5,4},{6,7},{7,6},{8,9},{9,8},{10,11... | collective-permute-start | bytes 589832 | tf_op jit(solution)/shard_map/ppermute | solution.py:339
  26.1 5.9 %collective-permute-start.14 = (bf16[3,2,2,64,128]{4,3,2,1,0:T(8,128)(2,1)S(1)}, bf16[3,2,2,64,128]{4,3,2,1,0:T(8,128)(2,1)S(1)}, u32[]{:S(2)}, u32[]{:S(2)}) collective-permute-start(bf16[3,2,2,64,128]{4,3,2,1,0:T(8,128)(2,1)S(1)} %collective-permute-done.10.rest_9_), channel_id=1, source_target_pairs={{0,1},{1,0},{2,3},{3,2},{4,5},{5,4},{6,7},{7,6},{8,9},{9,8},{10,11... | collective-permute-start | bytes 589832 | tf_op jit(solution)/shard_map/ppermute | solution.py:339
  26.6 5.4 %collective-permute-start.15 = (bf16[3,2,2,64,128]{4,3,2,1,0:T(8,128)(2,1)S(1)}, bf16[3,2,2,64,128]{4,3,2,1,0:T(8,128)(2,1)S(1)}, u32[]{:S(2)}, u32[]{:S(2)}) collective-permute-start(bf16[3,2,2,64,128]{4,3,2,1,0:T(8,128)(2,1)S(1)} %collective-permute-done.11.rest_10_), channel_id=1, source_target_pairs={{0,1},{1,0},{2,3},{3,2},{4,5},{5,4},{6,7},{7,6},{8,9},{9,8},{10,11... | collective-permute-start | bytes 589832 | tf_op jit(solution)/shard_map/ppermute | solution.py:339
  29.2 2.8 %collective-permute-start.16 = (bf16[3,2,2,64,128]{4,3,2,1,0:T(8,128)(2,1)S(1)}, bf16[3,2,2,64,128]{4,3,2,1,0:T(8,128)(2,1)S(1)}, u32[]{:S(2)}, u32[]{:S(2)}) collective-permute-start(bf16[3,2,2,64,128]{4,3,2,1,0:T(8,128)(2,1)S(1)} %collective-permute-done.12.rest_11_), channel_id=1, source_target_pairs={{0,1},{1,0},{2,3},{3,2},{4,5},{5,4},{6,7},{7,6},{8,9},{9,8},{10,11... | collective-permute-start | bytes 589832 | tf_op jit(solution)/shard_map/ppermute | solution.py:339
  30.6 1.3 %collective-permute-start.9 = (bf16[4,2,64,128]{3,2,1,0:T(8,128)(2,1)S(1)}, bf16[4,2,64,128]{3,2,1,0:T(8,128)(2,1)S(1)}, u32[]{:S(2)}, u32[]{:S(2)}) collective-permute-start(bf16[4,2,64,128]{3,2,1,0:T(8,128)(2,1)S(1)} %collective-permute-done.5.rest_3_), channel_id=1, source_target_pairs={{0,1},{1,0},{2,3},{3,2},{4,5},{5,4},{6,7},{7,6},{8,9},{9,8},{10,11... | collective-permute-start | bytes 393224 | tf_op jit(solution)/shard_map/ppermute | solution.py:339
  32.0 0.7 %copy-start = (s32[64]{0:T(128)S(1)}, s32[64]{0:T(128)}, u32[]{:S(2)}) copy-start(s32[64]{0:T(128)} %table.1) | copy-start | bytes 772

commit v2 on v0

--- a/solution.py
+++ b/solution.py
@@ -3,6 +3,8 @@
 import jax
 import jax.numpy as jnp
 from jax import lax
+from jax.experimental import pallas as pl
+from jax.experimental.pallas import tpu as pltpu
 from jax.sharding import PartitionSpec as P
 
 very_low = -1e30
@@ -146,7 +148,438 @@
     return jnp.stack(outputs)
 
 
+page_axes = ("ctx", "pool")
+hide = -(2.0**126)
+scale = 1.4426950408889634 / math.sqrt(128.0)
+join_flops = 6 * 10**9
+mask_flops = 0
+vmem = pl.BlockSpec(memory_space=pltpu.VMEM)
+smem = pl.BlockSpec(memory_space=pltpu.SMEM)
+
+
+def split_kernel(
+    pool_keys, pool_values, stretch_keys, stretch_values, first, second, third, early, sems
+):
+    head = lax.axis_index("head")
+    copies = []
+
+    def add(source, target):
+        copy = pltpu.make_async_copy(source, target, sems.at[len(copies)])
+        copy.start()
+        copies.append(copy)
+
+    for shift, target in ((3, third), (2, second), (1, first), (0, None)):
+        columns = pl.ds(pl.multiple_of((head ^ shift) * 128, 128), 128)
+        for which, pool in enumerate((pool_keys, pool_values)):
+            place = early.at[2 + which] if target is None else target.at[which]
+            add(pool.at[:, :, columns], place)
+    add(stretch_keys, early.at[0])
+    add(stretch_values, early.at[1])
+    for copy in copies:
+        copy.wait()
+
+
+def split(pool_keys, pool_values, stretch_keys, stretch_values):
+    piece = pltpu.VMEM((2, 2, 64, 128), jnp.bfloat16)
+    bundle = pltpu.VMEM((6, 2, 64, 128), jnp.bfloat16)
+    return pl.pallas_call(
+        split_kernel,
+        out_shape=(piece, piece, piece, bundle),
+        in_specs=[pl.BlockSpec(memory_space=pltpu.HBM)] * 4,
+        out_specs=[vmem] * 4,
+        scratch_shapes=[pltpu.SemaphoreType.DMA((10,))],
+        name="split",
+    )(pool_keys, pool_values, stretch_keys, stretch_values)
+
+
+def widen_kernel(bundle, piece, wide):
+    wide[4:] = piece[...]
+
+
+def widen(bundle, piece):
+    return pl.pallas_call(
+        widen_kernel,
+        out_shape=pltpu.VMEM((6, 2, 64, 128), jnp.bfloat16),
+        in_specs=[vmem] * 2,
+        out_specs=vmem,
+        input_output_aliases={0: 0},
+        compiler_params=pltpu.CompilerParams(vmem_limit_bytes=4 * 2**20),
+        cost_estimate=pl.CostEstimate(flops=0, bytes_accessed=1000, transcendentals=0),
+        name="widen",
+    )(bundle, piece)
+
+
+def join_kernel(second, third, joined):
+    for index, piece in enumerate((second, third)):
+        for which in range(2):
+            for within in range(2):
+                start = index * 128 + within * 64
+                joined[which, start : start + 64, :] = piece[which, within]
+
+
+def join(second, third):
+    return pl.pallas_call(
+        join_kernel,
+        out_shape=pltpu.VMEM((2, 256, 128), jnp.bfloat16),
+        in_specs=[vmem] * 2,
+        out_specs=vmem,
+        compiler_params=pltpu.CompilerParams(vmem_limit_bytes=4 * 2**20),
+        cost_estimate=pl.CostEstimate(
+            flops=join_flops, bytes_accessed=400000, transcendentals=0
+        ),
+        name="join",
+    )(second, third)
+
+
+def mask_kernel(
+    lengths_in,
+    table_in,
+    queries_in,
+    vertical_in,
+    slash_in,
+    wide_queries,
+    key_tags,
+    meta,
+    lengths,
+    table,
+    queries,
+    vertical,
+    slash,
+    sems,
+):
+    pairs = (
+        (table_in, table),
+        (lengths_in, lengths),
+        (vertical_in, vertical),
+        (slash_in, slash),
+        (queries_in, queries),
+    )
+    copies = []
+    for index, (source, target) in enumerate(pairs):
+        copies.append(pltpu.make_async_copy(source, target, sems.at[index]))
+        copies[-1].start()
+    head = lax.axis_index("head")
+    plane = lax.axis_index("ctx") * 2 + lax.axis_index("pool")
+    first_row = plane * 64
+    lane8 = lax.broadcasted_iota(jnp.int32, (8, 128), 1)
+    lane = lax.broadcasted_iota(jnp.int32, (64, 128), 1)
+    row = lax.broadcasted_iota(jnp.int32, (64, 128), 0)
+    causal = jnp.where(lane - 64 <= row, 0.0, hide)
+    own_heads = lax.broadcasted_iota(jnp.int32, (8, 32), 0) + head * 8
+    pick = (own_heads == lax.broadcasted_iota(jnp.int32, (8, 32), 1)).astype(jnp.float32)
+    for page in range(8):
+        diagonal = (lane - 64 == row) & (plane == page)
+        tag = diagonal | (((lane == 0) | (lane == 32)) & (plane < page))
+        start = 4096 + page * 64
+        key_tags[start : start + 64, :] = jnp.where(tag, 1.0, 0.0).astype(jnp.bfloat16)
+    for copy in copies:
+        copy.wait()
+    for index in range(64):
+        meta[table[index]] = index * 64
+    for prompt in range(2):
+        meta[64 + prompt] = lengths[prompt]
+
+    def own(entries):
+        picked = lax.dot_general(
+            pick,
+            entries[...].astype(jnp.float32),
+            (((1,), (1,)), ((), ())),
+            preferred_element_type=jnp.float32,
+        )
+        return (picked + 0.5).astype(jnp.int32)
+
+    vert_rows, slash_rows = own(vertical), own(slash)
+    page8 = lane8 % 32
+    vert_hit = lane8 < 0
+    for entry in range(16):
+        vert_hit = vert_hit | (vert_rows[:, entry : entry + 1] == page8)
+    for prompt in range(2):
+        length = lengths[prompt]
+        base_page = (length + first_row) // 64
+        cut = (base_page + 1) * 64 - length - first_row
+        tables = []
+        for step in range(2):
+            hit = vert_hit
+            distance = base_page + step - page8
+            for entry in range(16):
+                hit = hit | (slash_rows[:, entry : entry + 1] == distance)
+            shown = hit & (page8 * 64 < length) & (lane8 // 32 == prompt)
+            tables.append(jnp.where(shown, 0.0, hide))
+        for group in range(8):
+            rows = slice(group * 64, (group + 1) * 64)
+            bias = jnp.where(
+                row < cut, tables[0][group : group + 1, :], tables[1][group : group + 1, :]
+            )
+            bias = jnp.where(lane < 64, bias, causal)
+            wide_queries[prompt, rows, :128] = queries[prompt, :, group * 128 : (group + 1) * 128]
+            wide_queries[prompt, rows, 128:] = bias.astype(jnp.bfloat16)
+        for page in range(32):
+            live = row + page * 64 < length
+            tag = (live & (lane == prompt * 32 + page)) | (
+                ~live & ((lane == 0) | (lane == 32))
+            )
+            start = prompt * 2048 + page * 64
+            key_tags[start : start + 64, :] = jnp.where(tag, 1.0, 0.0).astype(jnp.bfloat16)
+
+
+def mask(lengths, table, queries, vertical, slash):
+    return pl.pallas_call(
+        mask_kernel,
+        out_shape=(
+            pltpu.VMEM((2, 512, 256), jnp.bfloat16),
+            pltpu.VMEM((4608, 128), jnp.bfloat16),
+            pltpu.SMEM((72,), jnp.int32),
+        ),
+        in_specs=[pl.BlockSpec(memory_space=pltpu.HBM)] * 5,
+        out_specs=[vmem] * 2 + [smem],
+        scratch_shapes=[
+            pltpu.SMEM((2,), jnp.int32),
+            pltpu.SMEM((64,), jnp.int32),
+            pltpu.VMEM((2, 64, 1024), jnp.bfloat16),
+            pltpu.VMEM((16, 32), jnp.int32),
+            pltpu.VMEM((16, 32), jnp.int32),
+            pltpu.SemaphoreType.DMA((5,)),
+        ],
+        cost_estimate=pl.CostEstimate(
+            flops=mask_flops, bytes_accessed=1000, transcendentals=0
+        ),
+        name="mask",
+    )(lengths, table, queries, vertical, slash)
+
+
+def origin(other, role):
+    from_pool = lax.axis_index("pool") ^ other
+    return lax.axis_index("ctx") ^ (0, 1 + from_pool, 2 - from_pool, 3)[role], from_pool
+
+
+def tags_at(meta, key_tags, slot):
+    return key_tags[pl.ds(pl.multiple_of(meta[slot], 64), 64), :]
+
+
+def bundle_pages(meta, key_tags, bundle, other, role):
+    from_ctx, from_pool = origin(other, role)
+    pages = []
+    for shift in range(2):
+        slot = ((from_ctx * 4 + (lax.axis_index("head") ^ shift)) * 2 + from_pool) * 2
+        for within in range(2):
+            tags = tags_at(meta, key_tags, slot + within)
+            pages.append((bundle[2 + 2 * shift, within], tags, bundle[3 + 2 * shift, within]))
+    return pages
+
+
+def bundle_stretch(key_tags, bundle, other, role, prompt):
+    from_ctx, from_pool = origin(other, role)
+    start = pl.multiple_of(4096 + (from_ctx * 2 + from_pool) * 64, 64)
+    return [(bundle[0, prompt], key_tags[pl.ds(start, 64), :], bundle[1, prompt])]
+
+
+def joined_pages(meta, key_tags, pieces, other, role):
+    from_ctx, from_pool = origin(other, role)
+    pages = []
+    for shift in range(2, 4):
+        slot = ((from_ctx * 4 + (lax.axis_index("head") ^ shift)) * 2 + from_pool) * 2
+        for within in range(2):
+            place = slice((shift - 2) * 128 + within * 64, (shift - 2) * 128 + within * 64 + 64)
+            tags = tags_at(meta, key_tags, slot + within)
+            pages.append((pieces[0, place, :], tags, pieces[1, place, :]))
+    return pages
+
+
+def stack(pages):
+    keys = jnp.concatenate([page[0] for page in pages], axis=0)
+    tags = jnp.concatenate([page[1] for page in pages], axis=0)
+    values = jnp.concatenate([page[2] for page in pages], axis=0)
+    ones = jnp.ones(values.shape, jnp.bfloat16)
+    return jnp.concatenate([keys, tags], axis=1), jnp.concatenate([values, ones], axis=1)
+
+
+def absorb_pages(wide_queries, shared, own, state, scores):
+    shared_keys, shared_values = stack(shared)
+    width = shared_keys.shape[0]
+    own = [stack(pages) if pages else None for pages in own]
+    highs, results = [], []
+    for prompt in range(2):
+        high = None
+        for start, pair in ((0, (shared_keys,)), (width, own[prompt])):
+            if pair is None:
+                continue
+            found = lax.dot_general(
+                wide_queries[prompt],
+                pair[0],
+                (((1,), (1,)), ((), ())),
+                preferred_element_type=jnp.float32,
+            )
+            scores[prompt, :, start : start + found.shape[1]] = found
+            for column in range(0, found.shape[1], 128):
+                part = found[:, column : column + 128]
+                high = part if high is None else jnp.maximum(high, part)
+        if state is not None:
+            high = jnp.maximum(high, state[0][prompt])
+        highs.append(jnp.max(high, axis=1, keepdims=True))
+    for prompt in range(2):
+        highest = highs[prompt]
+        weights = jnp.exp2((scores[prompt] - highest) * scale).astype(jnp.bfloat16)
+        sums = jnp.dot(
+            weights[:, :width], shared_values, preferred_element_type=jnp.float32
+        )
+        if own[prompt] is not None:
+            sums += jnp.dot(
+                weights[:, width:], own[prompt][1], preferred_element_type=jnp.float32
+            )
+        numerator, totals = sums[:, :128], sums[:, 128:]
+        if state is not None:
+            factor = jnp.exp2((state[0][prompt] - highest) * scale)
+            numerator = numerator + state[1][prompt, :, :128] * factor
+            totals = totals + state[1][prompt, :, 128:] * factor
+        results.append((highest, numerator, totals))
+    return results
+
+
+def keep(results, high_out, sums_out):
+    for prompt, (highest, numerator, totals) in enumerate(results):
+        high_out[prompt] = jnp.broadcast_to(highest, (512, 128))
+        sums_out[prompt, :, :128] = numerator
+        sums_out[prompt, :, 128:] = totals
+
+
+def open_kernel(meta, wide_queries, key_tags, *rest):
+    bundles, pieces = rest[:6], rest[6:8]
+    high_out, sums_out, scores = rest[8:]
+    shared, own = [], ([], [])
+    for other in range(2):
+        for role in range(3):
+            bundle = bundles[other * 3 + role]
+            shared += bundle_pages(meta, key_tags, bundle, other, role)
+            for prompt in range(2):
+                own[prompt].extend(bundle_stretch(key_tags, bundle, other, role, prompt))
+        shared += joined_pages(meta, key_tags, pieces[other], other, 0)
+    keep(absorb_pages(wide_queries, shared, own, None, scores), high_out, sums_out)
+
+
+def middle_kernel(meta, wide_queries, key_tags, before, given, *rest):
+    bundles, pieces = rest[:2], rest[2:6]
+    high_out, sums_out, scores = rest[6:]
+    shared, own = [], ([], [])
+    for other in range(2):
+        shared += bundle_pages(meta, key_tags, bundles[other], other, 3)
+        for prompt in range(2):
+            own[prompt].extend(bundle_stretch(key_tags, bundles[other], other, 3, prompt))
+        for role in range(2):
+            shared += joined_pages(meta, key_tags, pieces[other * 2 + role], other, 1 + role)
+    keep(absorb_pages(wide_queries, shared, own, (before, given), scores), high_out, sums_out)
+
+
+def close_kernel(meta, wide_queries, key_tags, before, given, mine, theirs, result, scores):
+    shared = joined_pages(meta, key_tags, mine, 0, 3) + joined_pages(meta, key_tags, theirs, 1, 3)
+    results = absorb_pages(wide_queries, shared, ([], []), (before, given), scores)
+    for prompt, (_, numerator, totals) in enumerate(results):
+        attended = (numerator / totals).astype(jnp.bfloat16)
+        for group in range(8):
+            rows = slice(group * 64, (group + 1) * 64)
+            result[prompt, :, group * 128 : (group + 1) * 128] = attended[rows, :]
+
+
+def call(kernel, name, out_shape, keys, *operands):
+    single = not isinstance(out_shape, tuple)
+    return pl.pallas_call(
+        kernel,
+        out_shape=out_shape,
+        in_specs=[smem] + [vmem] * (len(operands) - 1),
+        out_specs=vmem if single else (vmem,) * len(out_shape),
+        scratch_shapes=[pltpu.VMEM((2, 512, keys), jnp.float32)],
+        compiler_params=pltpu.CompilerParams(vmem_limit_bytes=40 * 2**20),
+        cost_estimate=pl.CostEstimate(flops=0, bytes_accessed=1000, transcendentals=0),
+        name=name,
+    )(*operands)
+
+
+def running():
+    return (pltpu.VMEM((2, 512, 128), jnp.float32), pltpu.VMEM((2, 512, 256), jnp.float32))
+
+
+def open_stage(meta, wide_queries, key_tags, bundles, pieces):
+    return call(
+        open_kernel, "open", running(), 38 * 64, meta, wide_queries, key_tags, *bundles, *pieces
+    )
+
+
+def middle_stage(meta, wide_queries, key_tags, state, bundles, pieces):
+    return call(
+        middle_kernel, "middle", running(), 26 * 64,
+        meta, wide_queries, key_tags, *state, *bundles, *pieces,
+    )
+
+
+def close_stage(meta, wide_queries, key_tags, state, mine, theirs):
+    return call(
+        close_kernel, "close", jax.ShapeDtypeStruct((2, 64, 1024), jnp.bfloat16), 8 * 64,
+        meta, wide_queries, key_tags, *state, mine, theirs,
+    )
+
+
+def to_first(value):
+    pairs = [(2 * c + p, 2 * (c ^ (1 + p)) + p) for c in range(4) for p in range(2)]
+    return lax.ppermute(value, page_axes, pairs)
+
+
+def to_second(value):
+    pairs = [(2 * c + p, 2 * (c ^ (2 - p)) + p) for c in range(4) for p in range(2)]
+    return lax.ppermute(value, page_axes, pairs)
+
+
+def to_sibling(value):
+    return lax.ppermute(value, "pool", [(0, 1), (1, 0)])
+
+
+def small_body(
+    queries,
+    stretch_keys,
+    stretch_values,
+    slot_pool_keys,
+    slot_pool_values,
+    prefix_lengths,
+    page_slot_table,
+    vertical,
+    slash,
+):
+    first, second, third, bundle = split(
+        slot_pool_keys, slot_pool_values, stretch_keys, stretch_values
+    )
+    third, second, first = (
+        lax.ppermute(piece, "head", [(z, z ^ shift) for z in range(4)])
+        for shift, piece in ((3, third), (2, second), (1, first))
+    )
+    joined = join(second, third)
+    bundle = widen(bundle, first)
+    bundle, lengths = lax.optimization_barrier((bundle, prefix_lengths))
+    by_first, by_second = to_first(bundle), to_second(bundle)
+    masks = mask(lengths, page_slot_table, queries, vertical.T, slash.T)
+    by_first, by_second, joined, masks = lax.optimization_barrier(
+        (by_first, by_second, joined, masks)
+    )
+    wide_queries, key_tags, meta = masks
+    late_first, late_second = to_first(joined), to_second(joined)
+    by_both = to_second(by_first)
+    early = [bundle, by_first, by_second]
+    early += [to_sibling(one) for one in early]
+    state = open_stage(meta, wide_queries, key_tags, early, [joined, to_sibling(joined)])
+    late_first, late_second, by_both, state = lax.optimization_barrier(
+        (late_first, late_second, by_both, state)
+    )
+    late_both = to_second(late_first)
+    late = [late_first, late_second]
+    late += [to_sibling(one) for one in late]
+    state = middle_stage(
+        meta, wide_queries, key_tags, state, [by_both, to_sibling(by_both)], late
+    )
+    state, late_both = lax.optimization_barrier((state, late_both))
+    return close_stage(
+        meta, wide_queries, key_tags, state, late_both, to_sibling(late_both)
+    )
+
+
 def solution(mesh):
+    small = tuple(mesh.shape[axis] for axis in ("ctx", "head", "pool")) == (4, 4, 2)
     in_specs = (
         P(None, ("ctx", "pool"), "head"),
         P(None, ("ctx", "pool"), "head"),
@@ -159,4 +592,10 @@
         P(),
     )
     out_specs = P(None, ("ctx", "pool"), "head")
-    return jax.shard_map(body, mesh=mesh, in_specs=in_specs, out_specs=out_specs, check_vma=False)
+    return jax.shard_map(
+        small_body if small else body,
+        mesh=mesh,
+        in_specs=in_specs,
+        out_specs=out_specs,
+        check_vma=False,
+    )

time: 120 us -> 33.1 us (0.28)
  blocking collectives: 39.4 us -> 0 us
  local copies, waits for them, and re-layouts: 30.2 us -> 0 us
  starting transfers between devices: 0.08 us -> 15.2 us
  between operations: 15.1 us -> 0.08 us
  matrix products: 12.1 us -> 0 us
  Pallas kernels: 0 us -> 10.4 us
  other arithmetic: 8.8 us -> 0 us
  waiting for transfers between devices: 12.7 us -> 7.21 us
    all_to_all x2 -> x0, blocking collectives: 20.6 us -> none  [the longest x1 12.2 us: body(): lax.all_to_all(slot_pool_keys, 'head', split_axis=2, concat_axis=0, tiled...]
    all_gather x2 -> x0, blocking collectives: 18.7 us -> none  [the longest x1 9.56 us: body(): lax.all_gather(stretch_keys, ('ctx', 'pool'), axis=1, tiled=True)]
    ppermute x0 -> x17, starting transfers between devices: none -> 15.2 us  [the longest x3 5.68 us: small_body(): lax.ppermute(piece, 'head', [(z, z ^ shift) for z in range(4)])]
    all_gather x2 -> x0, waiting for transfers between devices: 12.7 us -> none  [the longest x1 12.7 us: body(): lax.all_gather(page_values, ('ctx', 'pool'), axis=0, tiled=True)]
    dot_general x8 -> x0, matrix products: 12.1 us -> none  [the longest x4 5.18 us: absorb(): jnp.einsum('grk,kd->grd', weights.astype(jnp.bfloat16), values, preferred...]
    pallas_call x0 -> x7, Pallas kernels: none -> 10.4 us  [the longest x3 6.98 us: call(): pl.pallas_call(kernel, out_shape=out_shape, in_specs=[smem] + [vmem] * (l...]
    reshape x2 -> x0, local copies, waits for them, and re-layouts: 10.2 us -> none  [prefix_step(): jnp.repeat(chosen, page_len, axis=2) & (key_ids < prefix_len)[None, None, :]]
    ppermute x0 -> x17, waiting for transfers between devices: none -> 7.21 us  [the longest x3 2.76 us: small_body(): lax.ppermute(piece, 'head', [(z, z ^ shift) for z in range(4)])]
  transfers between devices with their start and end apart: 2 -> 17, of which waited for: 1 -> 6; matrix products, arithmetic and copies ran while one was open for 6% -> 0% of each run, Pallas kernels for 0% -> 23%
where the time goes in v2:
time: 33.1 us; the launch traced here: 32.9 us
  starting transfers between devices  15.2 us (46%)
  Pallas kernels  10.4 us (31%)
  waiting for transfers between devices  7.21 us (22%)
    pallas_call x3, Pallas kernels, call(): pl.pallas_call(kernel, out_shape=out_shape, in_specs=[smem] + [vmem] * (l...  6.98 us
    ppermute x3, starting transfers between devices, small_body(): lax.ppermute(piece, 'head', [(z, z ^ shift) for z in range(4)])  5.68 us
    ppermute x4, starting transfers between devices, to_second(): return lax.ppermute(value, page_axes, pairs)  5.07 us
    ppermute x2, starting transfers between devices, to_first(): return lax.ppermute(value, page_axes, pairs)  3.27 us
    ppermute x3, waiting for transfers between devices, small_body(): lax.ppermute(piece, 'head', [(z, z ^ shift) for z in range(4)])  2.76 us
    pallas_call x1, Pallas kernels, mask(): pl.pallas_call(mask_kernel, out_shape=(pltpu.VMEM((2, 512, 256), jnp.bflo...  2.41 us
    ppermute x4, waiting for transfers between devices, to_second(): return lax.ppermute(value, page_axes, pairs)  2 us
    ppermute x8, waiting for transfers between devices, to_sibling(): return lax.ppermute(value, 'pool', [(0, 1), (1, 0)])  1.36 us
  transfers between devices with their start and end apart: 17, of which 6 were waited for; matrix products, arithmetic and copies ran while one was open for 0% of the time, Pallas kernels for 23%

profile of v2, /device:TPU:0, one launch (start us, length us, event | category | flops | bytes accessed | tf_op | source)
XLA Modules:
  0.0 32.9 jit_solution(3791756815656712409)
XLA Ops:
  0.0 1.0 %split.1 = (bf16[2,2,64,128]{3,2,1,0:T(8,128)(2,1)S(1)}, bf16[2,2,64,128]{3,2,1,0:T(8,128)(2,1)S(1)}, bf16[2,2,64,128]{3,2,1,0:T(8,128)(2,1)S(1)}, bf16[6,2,64,128]{3,2,1,0:T(8,128)(2,1)S(1)}) custom-call(bf16[2,64,512]{2,1,0:T(8,128)(2,1)} %pool_keys.1, bf16[2,64,512]{2,1,0:T(8,128)(2,1)} %pool_values.1, bf16[2,64,128]{2,1,0:T(8,128)(2,1)} %stretch_keys.1, ...), custom_call_target="tpu_custom_call" | custom-call | tf_op jit(solution)/shard_map/split/pallas_call | solution.py:185
  1.0 3.1 %collective-permute-start = (bf16[2,2,64,128]{3,2,1,0:T(8,128)(2,1)S(1)}, bf16[2,2,64,128]{3,2,1,0:T(8,128)(2,1)S(1)}, u32[]{:S(2)}, u32[]{:S(2)}) collective-permute-start(bf16[2,2,64,128]{3,2,1,0:T(8,128)(2,1)S(1)} %get-tuple-element.33), channel_id=1, source_target_pairs={{0,2},{2,0},{4,6},{6,4},{1,3},{3,1},{5,7},{7,5},{8,10},{10,8},{12,... | collective-permute-start | bytes 196616 | tf_op jit(solution)/shard_map/ppermute | solution.py:549
  4.1 2.6 %collective-permute-start.3 = (bf16[2,2,64,128]{3,2,1,0:T(8,128)(2,1)S(1)}, bf16[2,2,64,128]{3,2,1,0:T(8,128)(2,1)S(1)}, u32[]{:S(2)}, u32[]{:S(2)}) collective-permute-start(bf16[2,2,64,128]{3,2,1,0:T(8,128)(2,1)S(1)} %get-tuple-element.35), channel_id=1, source_target_pairs={{0,4},{2,6},{4,0},{6,2},{1,5},{3,7},{5,1},{7,3},{8,12},{10,14},{12... | collective-permute-start | bytes 196616 | tf_op jit(solution)/shard_map/ppermute | solution.py:549
  6.7 1.8 %collective-permute-start.1 = (bf16[6,2,64,128]{3,2,1,0:T(8,128)(2,1)S(1)}, bf16[6,2,64,128]{3,2,1,0:T(8,128)(2,1)S(1)}, u32[]{:S(2)}, u32[]{:S(2)}) collective-permute-start(bf16[6,2,64,128]{3,2,1,0:T(8,128)(2,1)S(1)} %widen.1.rest_0_), channel_id=1, source_target_pairs={{0,8},{1,17},{8,0},{9,25},{16,24},{17,1},{24,16},{25,9},{2,10},{3,... | collective-permute-start | bytes 589832 | tf_op jit(solution)/shard_map/ppermute | solution.py:522
  8.5 1.5 %collective-permute-start.2 = (bf16[6,2,64,128]{3,2,1,0:T(8,128)(2,1)S(1)}, bf16[6,2,64,128]{3,2,1,0:T(8,128)(2,1)S(1)}, u32[]{:S(2)}, u32[]{:S(2)}) collective-permute-start(bf16[6,2,64,128]{3,2,1,0:T(8,128)(2,1)S(1)} %widen.1.rest_0_), channel_id=1, source_target_pairs={{0,16},{1,9},{8,24},{9,1},{16,0},{17,25},{24,8},{25,17},{2,18},{3,... | collective-permute-start | bytes 589832 | tf_op jit(solution)/shard_map/ppermute | solution.py:527
  10.0 0.0 collective-permute-start.8
  10.0 1.4 %collective-permute-done.3.second = bf16[2,2,64,128]{3,2,1,0:T(8,128)(2,1)S(1)} collective-permute-done((bf16[2,2,64,128]{3,2,1,0:T(8,128)(2,1)S(1)}, bf16[2,2,64,128]{3,2,1,0:T(8,128)(2,1)S(1)}, u32[]{:S(2)}, u32[]{:S(2)}) %collective-permute-start.3) | collective-permute-done | bytes 65568 | tf_op jit(solution)/shard_map/ppermute | solution.py:549
  11.4 1.4 %collective-permute-done.4.third = bf16[2,2,64,128]{3,2,1,0:T(8,128)(2,1)S(1)} collective-permute-done((bf16[2,2,64,128]{3,2,1,0:T(8,128)(2,1)S(1)}, bf16[2,2,64,128]{3,2,1,0:T(8,128)(2,1)S(1)}, u32[]{:S(2)}, u32[]{:S(2)}) %collective-permute-start.4) | collective-permute-done | bytes 65568 | tf_op jit(solution)/shard_map/ppermute | solution.py:549
  12.8 2.4 %mask.1 = (bf16[2,512,256]{2,1,0:T(8,128)(2,1)S(1)}, bf16[4608,128]{1,0:T(8,128)(2,1)S(1)}, s32[72]{0:T(128)S(4)}) custom-call(s32[2]{0:T(128)} %lengths_in, s32[64]{0:T(128)} %table_in.1, bf16[2,64,1024]{2,1,0:T(8,128)(2,1)} %queries_in.1, s32[16,32]{1,0:T(8,128)} %bitcast.2, s32[16,32]{1,0:T(8,128)} %bitcast.3), custom_call_target="tpu_custom_call" | custom-call | bytes 1000 | tf_op jit(solution)/shard_map/mask/pallas_call | solution.py:326
  15.2 0.0 collective-permute-done.1.rest_1_
  15.2 0.1 collective-permute-start.11
  15.3 0.5 %collective-permute-start.9 = (bf16[6,2,64,128]{3,2,1,0:T(8,128)(2,1)S(1)}, bf16[6,2,64,128]{3,2,1,0:T(8,128)(2,1)S(1)}, u32[]{:S(2)}, u32[]{:S(2)}) collective-permute-start(bf16[6,2,64,128]{3,2,1,0:T(8,128)(2,1)S(1)} %collective-permute-done.1.rest_1_), channel_id=1, source_target_pairs={{0,1},{1,0},{2,3},{3,2},{4,5},{5,4},{6,7},{7,6},{8,9},{9,8},{10,11... | collective-permute-start | bytes 589832 | tf_op jit(solution)/shard_map/ppermute | solution.py:531
  15.8 0.1 collective-permute-start.10
  15.9 1.5 %collective-permute-start.7 = (bf16[6,2,64,128]{3,2,1,0:T(8,128)(2,1)S(1)}, bf16[6,2,64,128]{3,2,1,0:T(8,128)(2,1)S(1)}, u32[]{:S(2)}, u32[]{:S(2)}) collective-permute-start(bf16[6,2,64,128]{3,2,1,0:T(8,128)(2,1)S(1)} %collective-permute-done.1.rest_1_), channel_id=1, source_target_pairs={{0,16},{1,9},{8,24},{9,1},{16,0},{17,25},{24,8},{25,17},{2,18},{3,... | collective-permute-start | bytes 589832 | tf_op jit(solution)/shard_map/ppermute | solution.py:527
  17.4 0.0 collective-permute-done.8.rest_3_
  17.4 1.5 %collective-permute-start.5 = (bf16[2,256,128]{2,1,0:T(8,128)(2,1)S(1)}, bf16[2,256,128]{2,1,0:T(8,128)(2,1)S(1)}, u32[]{:S(2)}, u32[]{:S(2)}) collective-permute-start(bf16[2,256,128]{2,1,0:T(8,128)(2,1)S(1)} %join.1.rest_6_), channel_id=1, source_target_pairs={{0,8},{1,17},{8,0},{9,25},{16,24},{17,1},{24,16},{25,9},{2,10},{3,... | collective-permute-start | bytes 393224 | tf_op jit(solution)/shard_map/ppermute | solution.py:522
  18.9 0.0 collective-permute-done.11.rest_7_
  18.9 0.5 %collective-permute-start.6 = (bf16[2,256,128]{2,1,0:T(8,128)(2,1)S(1)}, bf16[2,256,128]{2,1,0:T(8,128)(2,1)S(1)}, u32[]{:S(2)}, u32[]{:S(2)}) collective-permute-start(bf16[2,256,128]{2,1,0:T(8,128)(2,1)S(1)} %join.1.rest_6_), channel_id=1, source_target_pairs={{0,16},{1,9},{8,24},{9,1},{16,0},{17,25},{24,8},{25,17},{2,18},{3,... | collective-permute-start | bytes 393224 | tf_op jit(solution)/shard_map/ppermute | solution.py:527
  19.4 3.1 %open.1 = (f32[2,512,128]{2,1,0:T(8,128)S(1)}, f32[2,512,256]{2,1,0:T(8,128)S(1)}) custom-call(s32[72]{0:T(128)S(4)} %get-tuple-element.41.meta, bf16[2,512,256]{2,1,0:T(8,128)(2,1)S(1)} %get-tuple-element.42.wide_queries, bf16[4608,128]{1,0:T(8,128)(2,1)S(1)} %get-tuple-element.43.key_tags, bf16[6,2,64,128]{3,2,1,0:T(8,128)(2,1)S(1)} %widen.1.rest_0_, ...), custom_call_target="tpu_custom_call" | custom-call | bytes 1000 | tf_op jit(solution)/shard_map/open/pallas_call | solution.py:484
  22.5 1.1 %collective-permute-done.5.rest_2_ = bf16[2,256,128]{2,1,0:T(8,128)(2,1)S(1)} collective-permute-done((bf16[2,256,128]{2,1,0:T(8,128)(2,1)S(1)}, bf16[2,256,128]{2,1,0:T(8,128)(2,1)S(1)}, u32[]{:S(2)}, u32[]{:S(2)}) %collective-permute-start.5) | collective-permute-done | bytes 131104 | tf_op jit(solution)/shard_map/ppermute | solution.py:522
  23.5 0.8 %collective-permute-done.6.rest_3_ = bf16[2,256,128]{2,1,0:T(8,128)(2,1)S(1)} collective-permute-done((bf16[2,256,128]{2,1,0:T(8,128)(2,1)S(1)}, bf16[2,256,128]{2,1,0:T(8,128)(2,1)S(1)}, u32[]{:S(2)}, u32[]{:S(2)}) %collective-permute-start.6) | collective-permute-done | bytes 131104 | tf_op jit(solution)/shard_map/ppermute | solution.py:527
  24.3 0.5 %collective-permute-start.13 = (bf16[2,256,128]{2,1,0:T(8,128)(2,1)S(1)}, bf16[2,256,128]{2,1,0:T(8,128)(2,1)S(1)}, u32[]{:S(2)}, u32[]{:S(2)}) collective-permute-start(bf16[2,256,128]{2,1,0:T(8,128)(2,1)S(1)} %collective-permute-done.5.rest_2_), channel_id=1, source_target_pairs={{0,1},{1,0},{2,3},{3,2},{4,5},{5,4},{6,7},{7,6},{8,9},{9,8},{10,11... | collective-permute-start | bytes 393224 | tf_op jit(solution)/shard_map/ppermute | solution.py:531
  24.9 0.0 collective-permute-start.14
  24.9 1.5 %collective-permute-start.15 = (bf16[2,256,128]{2,1,0:T(8,128)(2,1)S(1)}, bf16[2,256,128]{2,1,0:T(8,128)(2,1)S(1)}, u32[]{:S(2)}, u32[]{:S(2)}) collective-permute-start(bf16[2,256,128]{2,1,0:T(8,128)(2,1)S(1)} %collective-permute-done.5.rest_2_), channel_id=1, source_target_pairs={{0,16},{1,9},{8,24},{9,1},{16,0},{17,25},{24,8},{25,17},{2,18},{3,... | collective-permute-start | bytes 393224 | tf_op jit(solution)/shard_map/ppermute | solution.py:527
  26.4 0.0 collective-permute-done.13.rest_4_
  26.4 0.0 collective-permute-done.14.rest_5_
  26.4 0.0 collective-permute-done.12.rest_1_
  26.4 2.2 %middle.1 = (f32[2,512,128]{2,1,0:T(8,128)S(1)}, f32[2,512,256]{2,1,0:T(8,128)S(1)}) custom-call(s32[72]{0:T(128)S(4)} %get-tuple-element.41.meta, bf16[2,512,256]{2,1,0:T(8,128)(2,1)S(1)} %get-tuple-element.42.wide_queries, bf16[4608,128]{1,0:T(8,128)(2,1)S(1)} %get-tuple-element.43.key_tags, f32[2,512,128]{2,1,0:T(8,128)S(1)} %get-tuple-element.49.before, ...), custom_call_target="tpu_custom_call" | custom-call | bytes 1000 | tf_op jit(solution)/shard_map/middle/pallas_call | solution.py:484
  28.6 1.2 %collective-permute-done.15.mine = bf16[2,256,128]{2,1,0:T(8,128)(2,1)S(1)} collective-permute-done((bf16[2,256,128]{2,1,0:T(8,128)(2,1)S(1)}, bf16[2,256,128]{2,1,0:T(8,128)(2,1)S(1)}, u32[]{:S(2)}, u32[]{:S(2)}) %collective-permute-start.15) | collective-permute-done | bytes 131104 | tf_op jit(solution)/shard_map/ppermute | solution.py:527
  29.8 0.0 collective-permute-start.16
  29.8 1.3 %collective-permute-done.16.theirs = bf16[2,256,128]{2,1,0:T(8,128)(2,1)S(1)} collective-permute-done((bf16[2,256,128]{2,1,0:T(8,128)(2,1)S(1)}, bf16[2,256,128]{2,1,0:T(8,128)(2,1)S(1)}, u32[]{:S(2)}, u32[]{:S(2)}) %collective-permute-start.16) | collective-permute-done | bytes 131104 | tf_op jit(solution)/shard_map/ppermute | solution.py:531
  31.2 1.7 %close.1 = bf16[2,64,1024]{2,1,0:T(8,128)(2,1)} custom-call(s32[72]{0:T(128)S(4)} %get-tuple-element.41.meta, bf16[2,512,256]{2,1,0:T(8,128)(2,1)S(1)} %get-tuple-element.42.wide_queries, bf16[4608,128]{1,0:T(8,128)(2,1)S(1)} %get-tuple-element.43.key_tags, f32[2,512,128]{2,1,0:T(8,128)S(1)} %get-tuple-element.56.before, ...), custom_call_target="tpu_custom_call" | custom-call | bytes 1000 | tf_op jit(solution)/shard_map/close/pallas_call | solution.py:484
  (9 shorter events, 0.0 us)
Async XLA Ops:
  1.0 5.7 %collective-permute-start = (bf16[2,2,64,128]{3,2,1,0:T(8,128)(2,1)S(1)}, bf16[2,2,64,128]{3,2,1,0:T(8,128)(2,1)S(1)}, u32[]{:S(2)}, u32[]{:S(2)}) collective-permute-start(bf16[2,2,64,128]{3,2,1,0:T(8,128)(2,1)S(1)} %get-tuple-element.33), channel_id=1, source_target_pairs={{0,2},{2,0},{4,6},{6,4},{1,3},{3,1},{5,7},{7,5},{8,10},{10,8},{12,... | collective-permute-start | bytes 196616 | tf_op jit(solution)/shard_map/ppermute | solution.py:549
  4.1 7.3 %collective-permute-start.3 = (bf16[2,2,64,128]{3,2,1,0:T(8,128)(2,1)S(1)}, bf16[2,2,64,128]{3,2,1,0:T(8,128)(2,1)S(1)}, u32[]{:S(2)}, u32[]{:S(2)}) collective-permute-start(bf16[2,2,64,128]{3,2,1,0:T(8,128)(2,1)S(1)} %get-tuple-element.35), channel_id=1, source_target_pairs={{0,4},{2,6},{4,0},{6,2},{1,5},{3,7},{5,1},{7,3},{8,12},{10,14},{12... | collective-permute-start | bytes 196616 | tf_op jit(solution)/shard_map/ppermute | solution.py:549
  6.7 6.1 %collective-permute-start.4 = (bf16[2,2,64,128]{3,2,1,0:T(8,128)(2,1)S(1)}, bf16[2,2,64,128]{3,2,1,0:T(8,128)(2,1)S(1)}, u32[]{:S(2)}, u32[]{:S(2)}) collective-permute-start(bf16[2,2,64,128]{3,2,1,0:T(8,128)(2,1)S(1)} %get-tuple-element.36), channel_id=1, source_target_pairs={{0,6},{2,4},{4,2},{6,0},{1,7},{3,5},{5,3},{7,1},{8,14},{10,12},{12... | collective-permute-start | bytes 196616 | tf_op jit(solution)/shard_map/ppermute | solution.py:549
  6.7 8.5 %collective-permute-start.1 = (bf16[6,2,64,128]{3,2,1,0:T(8,128)(2,1)S(1)}, bf16[6,2,64,128]{3,2,1,0:T(8,128)(2,1)S(1)}, u32[]{:S(2)}, u32[]{:S(2)}) collective-permute-start(bf16[6,2,64,128]{3,2,1,0:T(8,128)(2,1)S(1)} %widen.1.rest_0_), channel_id=1, source_target_pairs={{0,8},{1,17},{8,0},{9,25},{16,24},{17,1},{24,16},{25,9},{2,10},{3,... | collective-permute-start | bytes 589832 | tf_op jit(solution)/shard_map/ppermute | solution.py:522
  8.5 6.7 %collective-permute-start.2 = (bf16[6,2,64,128]{3,2,1,0:T(8,128)(2,1)S(1)}, bf16[6,2,64,128]{3,2,1,0:T(8,128)(2,1)S(1)}, u32[]{:S(2)}, u32[]{:S(2)}) collective-permute-start(bf16[6,2,64,128]{3,2,1,0:T(8,128)(2,1)S(1)} %widen.1.rest_0_), channel_id=1, source_target_pairs={{0,16},{1,9},{8,24},{9,1},{16,0},{17,25},{24,8},{25,17},{2,18},{3,... | collective-permute-start | bytes 589832 | tf_op jit(solution)/shard_map/ppermute | solution.py:527
  10.0 7.4 %collective-permute-start.8 = (bf16[6,2,64,128]{3,2,1,0:T(8,128)(2,1)S(1)}, bf16[6,2,64,128]{3,2,1,0:T(8,128)(2,1)S(1)}, u32[]{:S(2)}, u32[]{:S(2)}) collective-permute-start(bf16[6,2,64,128]{3,2,1,0:T(8,128)(2,1)S(1)} %widen.1.rest_0_), channel_id=1, source_target_pairs={{0,1},{1,0},{2,3},{3,2},{4,5},{5,4},{6,7},{7,6},{8,9},{9,8},{10,11... | collective-permute-start | bytes 589832 | tf_op jit(solution)/shard_map/ppermute | solution.py:531
  15.2 3.7 %collective-permute-start.11 = (bf16[2,256,128]{2,1,0:T(8,128)(2,1)S(1)}, bf16[2,256,128]{2,1,0:T(8,128)(2,1)S(1)}, u32[]{:S(2)}, u32[]{:S(2)}) collective-permute-start(bf16[2,256,128]{2,1,0:T(8,128)(2,1)S(1)} %join.1.rest_6_), channel_id=1, source_target_pairs={{0,1},{1,0},{2,3},{3,2},{4,5},{5,4},{6,7},{7,6},{8,9},{9,8},{10,11... | collective-permute-start | bytes 393224 | tf_op jit(solution)/shard_map/ppermute | solution.py:531
  15.3 4.1 %collective-permute-start.9 = (bf16[6,2,64,128]{3,2,1,0:T(8,128)(2,1)S(1)}, bf16[6,2,64,128]{3,2,1,0:T(8,128)(2,1)S(1)}, u32[]{:S(2)}, u32[]{:S(2)}) collective-permute-start(bf16[6,2,64,128]{3,2,1,0:T(8,128)(2,1)S(1)} %collective-permute-done.1.rest_1_), channel_id=1, source_target_pairs={{0,1},{1,0},{2,3},{3,2},{4,5},{5,4},{6,7},{7,6},{8,9},{9,8},{10,11... | collective-permute-start | bytes 589832 | tf_op jit(solution)/shard_map/ppermute | solution.py:531
  15.8 3.6 %collective-permute-start.10 = (bf16[6,2,64,128]{3,2,1,0:T(8,128)(2,1)S(1)}, bf16[6,2,64,128]{3,2,1,0:T(8,128)(2,1)S(1)}, u32[]{:S(2)}, u32[]{:S(2)}) collective-permute-start(bf16[6,2,64,128]{3,2,1,0:T(8,128)(2,1)S(1)} %collective-permute-done.2.rest_2_), channel_id=1, source_target_pairs={{0,1},{1,0},{2,3},{3,2},{4,5},{5,4},{6,7},{7,6},{8,9},{9,8},{10,11... | collective-permute-start | bytes 589832 | tf_op jit(solution)/shard_map/ppermute | solution.py:531
  15.9 8.5 %collective-permute-start.7 = (bf16[6,2,64,128]{3,2,1,0:T(8,128)(2,1)S(1)}, bf16[6,2,64,128]{3,2,1,0:T(8,128)(2,1)S(1)}, u32[]{:S(2)}, u32[]{:S(2)}) collective-permute-start(bf16[6,2,64,128]{3,2,1,0:T(8,128)(2,1)S(1)} %collective-permute-done.1.rest_1_), channel_id=1, source_target_pairs={{0,16},{1,9},{8,24},{9,1},{16,0},{17,25},{24,8},{25,17},{2,18},{3,... | collective-permute-start | bytes 589832 | tf_op jit(solution)/shard_map/ppermute | solution.py:527
  17.4 6.1 %collective-permute-start.5 = (bf16[2,256,128]{2,1,0:T(8,128)(2,1)S(1)}, bf16[2,256,128]{2,1,0:T(8,128)(2,1)S(1)}, u32[]{:S(2)}, u32[]{:S(2)}) collective-permute-start(bf16[2,256,128]{2,1,0:T(8,128)(2,1)S(1)} %join.1.rest_6_), channel_id=1, source_target_pairs={{0,8},{1,17},{8,0},{9,25},{16,24},{17,1},{24,16},{25,9},{2,10},{3,... | collective-permute-start | bytes 393224 | tf_op jit(solution)/shard_map/ppermute | solution.py:522
  18.9 5.5 %collective-permute-start.6 = (bf16[2,256,128]{2,1,0:T(8,128)(2,1)S(1)}, bf16[2,256,128]{2,1,0:T(8,128)(2,1)S(1)}, u32[]{:S(2)}, u32[]{:S(2)}) collective-permute-start(bf16[2,256,128]{2,1,0:T(8,128)(2,1)S(1)} %join.1.rest_6_), channel_id=1, source_target_pairs={{0,16},{1,9},{8,24},{9,1},{16,0},{17,25},{24,8},{25,17},{2,18},{3,... | collective-permute-start | bytes 393224 | tf_op jit(solution)/shard_map/ppermute | solution.py:527
  24.3 2.0 %collective-permute-start.12 = (bf16[6,2,64,128]{3,2,1,0:T(8,128)(2,1)S(1)}, bf16[6,2,64,128]{3,2,1,0:T(8,128)(2,1)S(1)}, u32[]{:S(2)}, u32[]{:S(2)}) collective-permute-start(bf16[6,2,64,128]{3,2,1,0:T(8,128)(2,1)S(1)} %collective-permute-done.7.rest_0_), channel_id=1, source_target_pairs={{0,1},{1,0},{2,3},{3,2},{4,5},{5,4},{6,7},{7,6},{8,9},{9,8},{10,11... | collective-permute-start | bytes 589832 | tf_op jit(solution)/shard_map/ppermute | solution.py:531
  24.3 2.0 %collective-permute-start.13 = (bf16[2,256,128]{2,1,0:T(8,128)(2,1)S(1)}, bf16[2,256,128]{2,1,0:T(8,128)(2,1)S(1)}, u32[]{:S(2)}, u32[]{:S(2)}) collective-permute-start(bf16[2,256,128]{2,1,0:T(8,128)(2,1)S(1)} %collective-permute-done.5.rest_2_), channel_id=1, source_target_pairs={{0,1},{1,0},{2,3},{3,2},{4,5},{5,4},{6,7},{7,6},{8,9},{9,8},{10,11... | collective-permute-start | bytes 393224 | tf_op jit(solution)/shard_map/ppermute | solution.py:531
  24.9 1.5 %collective-permute-start.14 = (bf16[2,256,128]{2,1,0:T(8,128)(2,1)S(1)}, bf16[2,256,128]{2,1,0:T(8,128)(2,1)S(1)}, u32[]{:S(2)}, u32[]{:S(2)}) collective-permute-start(bf16[2,256,128]{2,1,0:T(8,128)(2,1)S(1)} %collective-permute-done.6.rest_3_), channel_id=1, source_target_pairs={{0,1},{1,0},{2,3},{3,2},{4,5},{5,4},{6,7},{7,6},{8,9},{9,8},{10,11... | collective-permute-start | bytes 393224 | tf_op jit(solution)/shard_map/ppermute | solution.py:531
  24.9 5.0 %collective-permute-start.15 = (bf16[2,256,128]{2,1,0:T(8,128)(2,1)S(1)}, bf16[2,256,128]{2,1,0:T(8,128)(2,1)S(1)}, u32[]{:S(2)}, u32[]{:S(2)}) collective-permute-start(bf16[2,256,128]{2,1,0:T(8,128)(2,1)S(1)} %collective-permute-done.5.rest_2_), channel_id=1, source_target_pairs={{0,16},{1,9},{8,24},{9,1},{16,0},{17,25},{24,8},{25,17},{2,18},{3,... | collective-permute-start | bytes 393224 | tf_op jit(solution)/shard_map/ppermute | solution.py:527
  29.8 1.3 %collective-permute-start.16 = (bf16[2,256,128]{2,1,0:T(8,128)(2,1)S(1)}, bf16[2,256,128]{2,1,0:T(8,128)(2,1)S(1)}, u32[]{:S(2)}, u32[]{:S(2)}) collective-permute-start(bf16[2,256,128]{2,1,0:T(8,128)(2,1)S(1)} %collective-permute-done.15.mine), channel_id=1, source_target_pairs={{0,1},{1,0},{2,3},{3,2},{4,5},{5,4},{6,7},{7,6},{8,9},{9,8},{10,11... | collective-permute-start | bytes 393224 | tf_op jit(solution)/shard_map/ppermute | solution.py:531

commit v3 on v2

--- a/solution.py
+++ b/solution.py
@@ -181,7 +181,7 @@
 
 def split(pool_keys, pool_values, stretch_keys, stretch_values):
     piece = pltpu.VMEM((2, 2, 64, 128), jnp.bfloat16)
-    bundle = pltpu.VMEM((6, 2, 64, 128), jnp.bfloat16)
+    bundle = pltpu.VMEM((4, 2, 64, 128), jnp.bfloat16)
     return pl.pallas_call(
         split_kernel,
         out_shape=(piece, piece, piece, bundle),
@@ -192,43 +192,26 @@
     )(pool_keys, pool_values, stretch_keys, stretch_values)
 
 
-def widen_kernel(bundle, piece, wide):
-    wide[4:] = piece[...]
-
-
-def widen(bundle, piece):
-    return pl.pallas_call(
-        widen_kernel,
-        out_shape=pltpu.VMEM((6, 2, 64, 128), jnp.bfloat16),
-        in_specs=[vmem] * 2,
-        out_specs=vmem,
-        input_output_aliases={0: 0},
-        compiler_params=pltpu.CompilerParams(vmem_limit_bytes=4 * 2**20),
-        cost_estimate=pl.CostEstimate(flops=0, bytes_accessed=1000, transcendentals=0),
-        name="widen",
-    )(bundle, piece)
-
-
-def join_kernel(second, third, joined):
-    for index, piece in enumerate((second, third)):
+def join_kernel(first, second, third, joined):
+    for index, piece in enumerate((first, second, third)):
         for which in range(2):
             for within in range(2):
                 start = index * 128 + within * 64
                 joined[which, start : start + 64, :] = piece[which, within]
 
 
-def join(second, third):
+def join(first, second, third):
     return pl.pallas_call(
         join_kernel,
-        out_shape=pltpu.VMEM((2, 256, 128), jnp.bfloat16),
-        in_specs=[vmem] * 2,
+        out_shape=pltpu.VMEM((2, 384, 128), jnp.bfloat16),
+        in_specs=[vmem] * 3,
         out_specs=vmem,
         compiler_params=pltpu.CompilerParams(vmem_limit_bytes=4 * 2**20),
         cost_estimate=pl.CostEstimate(
             flops=join_flops, bytes_accessed=400000, transcendentals=0
         ),
         name="join",
-    )(second, third)
+    )(first, second, third)
 
 
 def mask_kernel(
@@ -359,11 +342,10 @@
 def bundle_pages(meta, key_tags, bundle, other, role):
     from_ctx, from_pool = origin(other, role)
     pages = []
-    for shift in range(2):
-        slot = ((from_ctx * 4 + (lax.axis_index("head") ^ shift)) * 2 + from_pool) * 2
-        for within in range(2):
-            tags = tags_at(meta, key_tags, slot + within)
-            pages.append((bundle[2 + 2 * shift, within], tags, bundle[3 + 2 * shift, within]))
+    slot = ((from_ctx * 4 + lax.axis_index("head")) * 2 + from_pool) * 2
+    for within in range(2):
+        tags = tags_at(meta, key_tags, slot + within)
+        pages.append((bundle[2, within], tags, bundle[3, within]))
     return pages
 
 
@@ -376,10 +358,10 @@
 def joined_pages(meta, key_tags, pieces, other, role):
     from_ctx, from_pool = origin(other, role)
     pages = []
-    for shift in range(2, 4):
+    for shift in range(1, 4):
         slot = ((from_ctx * 4 + (lax.axis_index("head") ^ shift)) * 2 + from_pool) * 2
         for within in range(2):
-            place = slice((shift - 2) * 128 + within * 64, (shift - 2) * 128 + within * 64 + 64)
+            place = slice((shift - 1) * 128 + within * 64, (shift - 1) * 128 + within * 64 + 64)
             tags = tags_at(meta, key_tags, slot + within)
             pages.append((pieces[0, place, :], tags, pieces[1, place, :]))
     return pages
@@ -499,20 +481,20 @@
 
 def open_stage(meta, wide_queries, key_tags, bundles, pieces):
     return call(
-        open_kernel, "open", running(), 38 * 64, meta, wide_queries, key_tags, *bundles, *pieces
+        open_kernel, "open", running(), 30 * 64, meta, wide_queries, key_tags, *bundles, *pieces
     )
 
 
 def middle_stage(meta, wide_queries, key_tags, state, bundles, pieces):
     return call(
-        middle_kernel, "middle", running(), 26 * 64,
+        middle_kernel, "middle", running(), 30 * 64,
         meta, wide_queries, key_tags, *state, *bundles, *pieces,
     )
 
 
 def close_stage(meta, wide_queries, key_tags, state, mine, theirs):
     return call(
-        close_kernel, "close", jax.ShapeDtypeStruct((2, 64, 1024), jnp.bfloat16), 8 * 64,
+        close_kernel, "close", jax.ShapeDtypeStruct((2, 64, 1024), jnp.bfloat16), 12 * 64,
         meta, wide_queries, key_tags, *state, mine, theirs,
     )
 
@@ -549,23 +531,18 @@
         lax.ppermute(piece, "head", [(z, z ^ shift) for z in range(4)])
         for shift, piece in ((3, third), (2, second), (1, first))
     )
-    joined = join(second, third)
-    bundle = widen(bundle, first)
-    bundle, lengths = lax.optimization_barrier((bundle, prefix_lengths))
     by_first, by_second = to_first(bundle), to_second(bundle)
+    first, lengths = lax.optimization_barrier((first, prefix_lengths))
     masks = mask(lengths, page_slot_table, queries, vertical.T, slash.T)
-    by_first, by_second, joined, masks = lax.optimization_barrier(
-        (by_first, by_second, joined, masks)
-    )
+    first, second, third, masks = lax.optimization_barrier((first, second, third, masks))
+    joined = join(first, second, third)
     wide_queries, key_tags, meta = masks
     late_first, late_second = to_first(joined), to_second(joined)
     by_both = to_second(by_first)
     early = [bundle, by_first, by_second]
     early += [to_sibling(one) for one in early]
     state = open_stage(meta, wide_queries, key_tags, early, [joined, to_sibling(joined)])
-    late_first, late_second, by_both, state = lax.optimization_barrier(
-        (late_first, late_second, by_both, state)
-    )
+    late_first, late_second, state = lax.optimization_barrier((late_first, late_second, state))
     late_both = to_second(late_first)
     late = [late_first, late_second]
     late += [to_sibling(one) for one in late]

time: 33.1 us -> 30.3 us (0.915)
  waiting for transfers between devices: 7.21 us -> 3.78 us
  starting transfers between devices: 15.2 us -> 15.9 us
    ppermute x3, waiting for transfers between devices: 2.76 us -> 0.42 us  [small_body(): lax.ppermute(piece, 'head', [(z, z ^ shift) for z in range(4)])]
    ppermute x4, waiting for transfers between devices: 2 us -> 0.06 us  [to_second(): return lax.ppermute(value, page_axes, pairs)]
    ppermute x8, waiting for transfers between devices: 1.36 us -> 3.16 us  [to_sibling(): return lax.ppermute(value, 'pool', [(0, 1), (1, 0)])]
    ppermute x2, waiting for transfers between devices: 1.08 us -> 0.14 us  [to_first(): return lax.ppermute(value, page_axes, pairs)]
    ppermute x8, starting transfers between devices: 1.17 us -> 1.59 us  [to_sibling(): return lax.ppermute(value, 'pool', [(0, 1), (1, 0)])]
    ppermute x4, starting transfers between devices: 5.07 us -> 5.43 us  [to_second(): return lax.ppermute(value, page_axes, pairs)]
  transfers between devices with their start and end apart: 17 -> 17, of which waited for: 6 -> 7; matrix products, arithmetic and copies ran while one was open for 0% -> 0% of each run, Pallas kernels for 23% -> 25%
where the time goes in v3:
time: 30.3 us; the launch traced here: 30.1 us
  starting transfers between devices  15.9 us (52%)
  Pallas kernels  10.3 us (34%)
  waiting for transfers between devices  3.78 us (12%)
    pallas_call x3, Pallas kernels, call(): pl.pallas_call(kernel, out_shape=out_shape, in_specs=[smem] + [vmem] * (l...  6.92 us
    ppermute x3, starting transfers between devices, small_body(): lax.ppermute(piece, 'head', [(z, z ^ shift) for z in range(4)])  5.68 us
    ppermute x4, starting transfers between devices, to_second(): return lax.ppermute(value, page_axes, pairs)  5.43 us
    ppermute x2, starting transfers between devices, to_first(): return lax.ppermute(value, page_axes, pairs)  3.17 us
    ppermute x8, waiting for transfers between devices, to_sibling(): return lax.ppermute(value, 'pool', [(0, 1), (1, 0)])  3.16 us
    pallas_call x1, Pallas kernels, mask(): pl.pallas_call(mask_kernel, out_shape=(pltpu.VMEM((2, 512, 256), jnp.bflo...  2.41 us
    ppermute x8, starting transfers between devices, to_sibling(): return lax.ppermute(value, 'pool', [(0, 1), (1, 0)])  1.59 us
    pallas_call x1, Pallas kernels, split(): pl.pallas_call(split_kernel, out_shape=(piece, piece, piece, bundle), in_...  0.99 us
  transfers between devices with their start and end apart: 17, of which 7 were waited for; matrix products, arithmetic and copies ran while one was open for 0% of the time, Pallas kernels for 25%

profile of v3, /device:TPU:0, one launch (start us, length us, event | category | flops | bytes accessed | tf_op | source)
XLA Modules:
  0.0 30.1 jit_solution(11070786398853973339)
XLA Ops:
  0.0 1.0 %split.1 = (bf16[2,2,64,128]{3,2,1,0:T(8,128)(2,1)S(1)}, bf16[2,2,64,128]{3,2,1,0:T(8,128)(2,1)S(1)}, bf16[2,2,64,128]{3,2,1,0:T(8,128)(2,1)S(1)}, bf16[4,2,64,128]{3,2,1,0:T(8,128)(2,1)S(1)}) custom-call(bf16[2,64,512]{2,1,0:T(8,128)(2,1)} %pool_keys.1, bf16[2,64,512]{2,1,0:T(8,128)(2,1)} %pool_values.1, bf16[2,64,128]{2,1,0:T(8,128)(2,1)} %stretch_keys.1, ...), custom_call_target="tpu_custom_call" | custom-call | tf_op jit(solution)/shard_map/split/pallas_call | solution.py:185
  1.0 3.1 %collective-permute-start = (bf16[2,2,64,128]{3,2,1,0:T(8,128)(2,1)S(1)}, bf16[2,2,64,128]{3,2,1,0:T(8,128)(2,1)S(1)}, u32[]{:S(2)}, u32[]{:S(2)}) collective-permute-start(bf16[2,2,64,128]{3,2,1,0:T(8,128)(2,1)S(1)} %get-tuple-element.31), channel_id=1, source_target_pairs={{0,2},{2,0},{4,6},{6,4},{1,3},{3,1},{5,7},{7,5},{8,10},{10,8},{12,... | collective-permute-start | bytes 196616 | tf_op jit(solution)/shard_map/ppermute | solution.py:531
  4.1 2.6 %collective-permute-start.1 = (bf16[2,2,64,128]{3,2,1,0:T(8,128)(2,1)S(1)}, bf16[2,2,64,128]{3,2,1,0:T(8,128)(2,1)S(1)}, u32[]{:S(2)}, u32[]{:S(2)}) collective-permute-start(bf16[2,2,64,128]{3,2,1,0:T(8,128)(2,1)S(1)} %get-tuple-element.33), channel_id=1, source_target_pairs={{0,4},{2,6},{4,0},{6,2},{1,5},{3,7},{5,1},{7,3},{8,12},{10,14},{12... | collective-permute-start | bytes 196616 | tf_op jit(solution)/shard_map/ppermute | solution.py:531
  6.7 0.0 collective-permute-start.2
  6.7 1.7 %collective-permute-start.5 = (bf16[4,2,64,128]{3,2,1,0:T(8,128)(2,1)S(1)}, bf16[4,2,64,128]{3,2,1,0:T(8,128)(2,1)S(1)}, u32[]{:S(2)}, u32[]{:S(2)}) collective-permute-start(bf16[4,2,64,128]{3,2,1,0:T(8,128)(2,1)S(1)} %get-tuple-element.45.rest_0_), channel_id=1, source_target_pairs={{0,8},{1,17},{8,0},{9,25},{16,24},{17,1},{24,16},{25,9},{2,10},{3,... | collective-permute-start | bytes 393224 | tf_op jit(solution)/shard_map/ppermute | solution.py:504
  8.4 1.5 %collective-permute-start.6 = (bf16[4,2,64,128]{3,2,1,0:T(8,128)(2,1)S(1)}, bf16[4,2,64,128]{3,2,1,0:T(8,128)(2,1)S(1)}, u32[]{:S(2)}, u32[]{:S(2)}) collective-permute-start(bf16[4,2,64,128]{3,2,1,0:T(8,128)(2,1)S(1)} %get-tuple-element.45.rest_0_), channel_id=1, source_target_pairs={{0,16},{1,9},{8,24},{9,1},{16,0},{17,25},{24,8},{25,17},{2,18},{3,... | collective-permute-start | bytes 393224 | tf_op jit(solution)/shard_map/ppermute | solution.py:509
  9.9 0.0 collective-permute-done.first
  9.9 0.0 collective-permute-start.7
  9.9 2.4 %mask.1 = (bf16[2,512,256]{2,1,0:T(8,128)(2,1)S(1)}, bf16[4608,128]{1,0:T(8,128)(2,1)S(1)}, s32[72]{0:T(128)S(4)}) custom-call(s32[2]{0:T(128)} %lengths_in, s32[64]{0:T(128)} %table_in.1, bf16[2,64,1024]{2,1,0:T(8,128)(2,1)} %queries_in.1, s32[16,32]{1,0:T(8,128)} %bitcast.2, s32[16,32]{1,0:T(8,128)} %bitcast.3), custom_call_target="tpu_custom_call" | custom-call | bytes 1000 | tf_op jit(solution)/shard_map/mask/pallas_call | solution.py:309
  12.3 0.4 %collective-permute-done.2.third = bf16[2,2,64,128]{3,2,1,0:T(8,128)(2,1)S(1)} collective-permute-done((bf16[2,2,64,128]{3,2,1,0:T(8,128)(2,1)S(1)}, bf16[2,2,64,128]{3,2,1,0:T(8,128)(2,1)S(1)}, u32[]{:S(2)}, u32[]{:S(2)}) %collective-permute-start.2) | collective-permute-done | bytes 65568 | tf_op jit(solution)/shard_map/ppermute | solution.py:531
  12.8 0.2 collective-permute-start.10
  12.9 1.5 %collective-permute-start.3 = (bf16[2,384,128]{2,1,0:T(8,128)(2,1)S(1)}, bf16[2,384,128]{2,1,0:T(8,128)(2,1)S(1)}, u32[]{:S(2)}, u32[]{:S(2)}) collective-permute-start(bf16[2,384,128]{2,1,0:T(8,128)(2,1)S(1)} %join.1.rest_6_), channel_id=1, source_target_pairs={{0,8},{1,17},{8,0},{9,25},{16,24},{17,1},{24,16},{25,9},{2,10},{3,... | collective-permute-start | bytes 589832 | tf_op jit(solution)/shard_map/ppermute | solution.py:504
  14.4 0.0 collective-permute-done.5.rest_1_
  14.4 1.5 %collective-permute-start.4 = (bf16[2,384,128]{2,1,0:T(8,128)(2,1)S(1)}, bf16[2,384,128]{2,1,0:T(8,128)(2,1)S(1)}, u32[]{:S(2)}, u32[]{:S(2)}) collective-permute-start(bf16[2,384,128]{2,1,0:T(8,128)(2,1)S(1)} %join.1.rest_6_), channel_id=1, source_target_pairs={{0,16},{1,9},{8,24},{9,1},{16,0},{17,25},{24,8},{25,17},{2,18},{3,... | collective-permute-start | bytes 589832 | tf_op jit(solution)/shard_map/ppermute | solution.py:509
  15.9 0.0 collective-permute-start.8
  15.9 0.0 collective-permute-done.7.rest_3_
  15.9 0.5 %collective-permute-start.9 = (bf16[4,2,64,128]{3,2,1,0:T(8,128)(2,1)S(1)}, bf16[4,2,64,128]{3,2,1,0:T(8,128)(2,1)S(1)}, u32[]{:S(2)}, u32[]{:S(2)}) collective-permute-start(bf16[4,2,64,128]{3,2,1,0:T(8,128)(2,1)S(1)} %collective-permute-done.6.rest_2_), channel_id=1, source_target_pairs={{0,1},{1,0},{2,3},{3,2},{4,5},{5,4},{6,7},{7,6},{8,9},{9,8},{10,11... | collective-permute-start | bytes 393224 | tf_op jit(solution)/shard_map/ppermute | solution.py:513
  16.5 0.5 %collective-permute-start.11 = (bf16[4,2,64,128]{3,2,1,0:T(8,128)(2,1)S(1)}, bf16[4,2,64,128]{3,2,1,0:T(8,128)(2,1)S(1)}, u32[]{:S(2)}, u32[]{:S(2)}) collective-permute-start(bf16[4,2,64,128]{3,2,1,0:T(8,128)(2,1)S(1)} %collective-permute-done.5.rest_1_), channel_id=1, source_target_pairs={{0,16},{1,9},{8,24},{9,1},{16,0},{17,25},{24,8},{25,17},{2,18},{3,... | collective-permute-start | bytes 393224 | tf_op jit(solution)/shard_map/ppermute | solution.py:509
  17.0 0.3 %collective-permute-done.8.rest_4_ = bf16[4,2,64,128]{3,2,1,0:T(8,128)(2,1)S(1)} collective-permute-done((bf16[4,2,64,128]{3,2,1,0:T(8,128)(2,1)S(1)}, bf16[4,2,64,128]{3,2,1,0:T(8,128)(2,1)S(1)}, u32[]{:S(2)}, u32[]{:S(2)}) %collective-permute-start.8) | collective-permute-done | bytes 131104 | tf_op jit(solution)/shard_map/ppermute | solution.py:513
  17.3 0.2 collective-permute-done.9.rest_5_
  17.5 2.5 %open.1 = (f32[2,512,128]{2,1,0:T(8,128)S(1)}, f32[2,512,256]{2,1,0:T(8,128)S(1)}) custom-call(s32[72]{0:T(128)S(4)} %get-tuple-element.39.meta, bf16[2,512,256]{2,1,0:T(8,128)(2,1)S(1)} %get-tuple-element.40.wide_queries, bf16[4608,128]{1,0:T(8,128)(2,1)S(1)} %get-tuple-element.41.key_tags, bf16[4,2,64,128]{3,2,1,0:T(8,128)(2,1)S(1)} %get-tuple-element.45.rest_0_, ...), custom_call_target="tpu_custom_call" | custom-call | bytes 1000 | tf_op jit(solution)/shard_map/open/pallas_call | solution.py:466
  20.0 0.1 collective-permute-done.3.rest_2_
  20.1 0.1 collective-permute-done.4.rest_3_
  20.2 0.7 %collective-permute-start.13 = (bf16[2,384,128]{2,1,0:T(8,128)(2,1)S(1)}, bf16[2,384,128]{2,1,0:T(8,128)(2,1)S(1)}, u32[]{:S(2)}, u32[]{:S(2)}) collective-permute-start(bf16[2,384,128]{2,1,0:T(8,128)(2,1)S(1)} %collective-permute-done.3.rest_2_), channel_id=1, source_target_pairs={{0,1},{1,0},{2,3},{3,2},{4,5},{5,4},{6,7},{7,6},{8,9},{9,8},{10,11... | collective-permute-start | bytes 589832 | tf_op jit(solution)/shard_map/ppermute | solution.py:513
  20.8 0.0 collective-permute-start.14
  20.8 1.9 %collective-permute-start.15 = (bf16[2,384,128]{2,1,0:T(8,128)(2,1)S(1)}, bf16[2,384,128]{2,1,0:T(8,128)(2,1)S(1)}, u32[]{:S(2)}, u32[]{:S(2)}) collective-permute-start(bf16[2,384,128]{2,1,0:T(8,128)(2,1)S(1)} %collective-permute-done.3.rest_2_), channel_id=1, source_target_pairs={{0,16},{1,9},{8,24},{9,1},{16,0},{17,25},{24,8},{25,17},{2,18},{3,... | collective-permute-start | bytes 589832 | tf_op jit(solution)/shard_map/ppermute | solution.py:509
  22.7 0.0 collective-permute-done.11.rest_0_
  22.7 1.3 %collective-permute-done.12.rest_1_ = bf16[4,2,64,128]{3,2,1,0:T(8,128)(2,1)S(1)} collective-permute-done((bf16[4,2,64,128]{3,2,1,0:T(8,128)(2,1)S(1)}, bf16[4,2,64,128]{3,2,1,0:T(8,128)(2,1)S(1)}, u32[]{:S(2)}, u32[]{:S(2)}) %collective-permute-start.12) | collective-permute-done | bytes 131104 | tf_op jit(solution)/shard_map/ppermute | solution.py:513
  24.1 2.5 %middle.1 = (f32[2,512,128]{2,1,0:T(8,128)S(1)}, f32[2,512,256]{2,1,0:T(8,128)S(1)}) custom-call(s32[72]{0:T(128)S(4)} %get-tuple-element.39.meta, bf16[2,512,256]{2,1,0:T(8,128)(2,1)S(1)} %get-tuple-element.40.wide_queries, bf16[4608,128]{1,0:T(8,128)(2,1)S(1)} %get-tuple-element.41.key_tags, f32[2,512,128]{2,1,0:T(8,128)S(1)} %get-tuple-element.48.before, ...), custom_call_target="tpu_custom_call" | custom-call | bytes 1000 | tf_op jit(solution)/shard_map/middle/pallas_call | solution.py:466
  26.6 0.2 collective-permute-start.16
  26.8 1.3 %collective-permute-done.16.theirs = bf16[2,384,128]{2,1,0:T(8,128)(2,1)S(1)} collective-permute-done((bf16[2,384,128]{2,1,0:T(8,128)(2,1)S(1)}, bf16[2,384,128]{2,1,0:T(8,128)(2,1)S(1)}, u32[]{:S(2)}, u32[]{:S(2)}) %collective-permute-start.16) | collective-permute-done | bytes 196640 | tf_op jit(solution)/shard_map/ppermute | solution.py:513
  28.1 1.9 %close.1 = bf16[2,64,1024]{2,1,0:T(8,128)(2,1)} custom-call(s32[72]{0:T(128)S(4)} %get-tuple-element.39.meta, bf16[2,512,256]{2,1,0:T(8,128)(2,1)S(1)} %get-tuple-element.40.wide_queries, bf16[4608,128]{1,0:T(8,128)(2,1)S(1)} %get-tuple-element.41.key_tags, f32[2,512,128]{2,1,0:T(8,128)S(1)} %get-tuple-element.54.before, ...), custom_call_target="tpu_custom_call" | custom-call | bytes 1000 | tf_op jit(solution)/shard_map/close/pallas_call | solution.py:466
  (8 shorter events, 0.0 us)
Async XLA Ops:
  1.0 8.9 %collective-permute-start = (bf16[2,2,64,128]{3,2,1,0:T(8,128)(2,1)S(1)}, bf16[2,2,64,128]{3,2,1,0:T(8,128)(2,1)S(1)}, u32[]{:S(2)}, u32[]{:S(2)}) collective-permute-start(bf16[2,2,64,128]{3,2,1,0:T(8,128)(2,1)S(1)} %get-tuple-element.31), channel_id=1, source_target_pairs={{0,2},{2,0},{4,6},{6,4},{1,3},{3,1},{5,7},{7,5},{8,10},{10,8},{12,... | collective-permute-start | bytes 196616 | tf_op jit(solution)/shard_map/ppermute | solution.py:531
  4.1 8.2 %collective-permute-start.1 = (bf16[2,2,64,128]{3,2,1,0:T(8,128)(2,1)S(1)}, bf16[2,2,64,128]{3,2,1,0:T(8,128)(2,1)S(1)}, u32[]{:S(2)}, u32[]{:S(2)}) collective-permute-start(bf16[2,2,64,128]{3,2,1,0:T(8,128)(2,1)S(1)} %get-tuple-element.33), channel_id=1, source_target_pairs={{0,4},{2,6},{4,0},{6,2},{1,5},{3,7},{5,1},{7,3},{8,12},{10,14},{12... | collective-permute-start | bytes 196616 | tf_op jit(solution)/shard_map/ppermute | solution.py:531
  6.7 6.1 %collective-permute-start.2 = (bf16[2,2,64,128]{3,2,1,0:T(8,128)(2,1)S(1)}, bf16[2,2,64,128]{3,2,1,0:T(8,128)(2,1)S(1)}, u32[]{:S(2)}, u32[]{:S(2)}) collective-permute-start(bf16[2,2,64,128]{3,2,1,0:T(8,128)(2,1)S(1)} %get-tuple-element.34), channel_id=1, source_target_pairs={{0,6},{2,4},{4,2},{6,0},{1,7},{3,5},{5,3},{7,1},{8,14},{10,12},{12... | collective-permute-start | bytes 196616 | tf_op jit(solution)/shard_map/ppermute | solution.py:531
  6.7 7.7 %collective-permute-start.5 = (bf16[4,2,64,128]{3,2,1,0:T(8,128)(2,1)S(1)}, bf16[4,2,64,128]{3,2,1,0:T(8,128)(2,1)S(1)}, u32[]{:S(2)}, u32[]{:S(2)}) collective-permute-start(bf16[4,2,64,128]{3,2,1,0:T(8,128)(2,1)S(1)} %get-tuple-element.45.rest_0_), channel_id=1, source_target_pairs={{0,8},{1,17},{8,0},{9,25},{16,24},{17,1},{24,16},{25,9},{2,10},{3,... | collective-permute-start | bytes 393224 | tf_op jit(solution)/shard_map/ppermute | solution.py:504
  8.4 7.5 %collective-permute-start.6 = (bf16[4,2,64,128]{3,2,1,0:T(8,128)(2,1)S(1)}, bf16[4,2,64,128]{3,2,1,0:T(8,128)(2,1)S(1)}, u32[]{:S(2)}, u32[]{:S(2)}) collective-permute-start(bf16[4,2,64,128]{3,2,1,0:T(8,128)(2,1)S(1)} %get-tuple-element.45.rest_0_), channel_id=1, source_target_pairs={{0,16},{1,9},{8,24},{9,1},{16,0},{17,25},{24,8},{25,17},{2,18},{3,... | collective-permute-start | bytes 393224 | tf_op jit(solution)/shard_map/ppermute | solution.py:509
  9.9 6.0 %collective-permute-start.7 = (bf16[4,2,64,128]{3,2,1,0:T(8,128)(2,1)S(1)}, bf16[4,2,64,128]{3,2,1,0:T(8,128)(2,1)S(1)}, u32[]{:S(2)}, u32[]{:S(2)}) collective-permute-start(bf16[4,2,64,128]{3,2,1,0:T(8,128)(2,1)S(1)} %get-tuple-element.45.rest_0_), channel_id=1, source_target_pairs={{0,1},{1,0},{2,3},{3,2},{4,5},{5,4},{6,7},{7,6},{8,9},{9,8},{10,11... | collective-permute-start | bytes 393224 | tf_op jit(solution)/shard_map/ppermute | solution.py:513
  12.8 3.7 %collective-permute-start.10 = (bf16[2,384,128]{2,1,0:T(8,128)(2,1)S(1)}, bf16[2,384,128]{2,1,0:T(8,128)(2,1)S(1)}, u32[]{:S(2)}, u32[]{:S(2)}) collective-permute-start(bf16[2,384,128]{2,1,0:T(8,128)(2,1)S(1)} %join.1.rest_6_), channel_id=1, source_target_pairs={{0,1},{1,0},{2,3},{3,2},{4,5},{5,4},{6,7},{7,6},{8,9},{9,8},{10,11... | collective-permute-start | bytes 589832 | tf_op jit(solution)/shard_map/ppermute | solution.py:513
  12.9 7.2 %collective-permute-start.3 = (bf16[2,384,128]{2,1,0:T(8,128)(2,1)S(1)}, bf16[2,384,128]{2,1,0:T(8,128)(2,1)S(1)}, u32[]{:S(2)}, u32[]{:S(2)}) collective-permute-start(bf16[2,384,128]{2,1,0:T(8,128)(2,1)S(1)} %join.1.rest_6_), channel_id=1, source_target_pairs={{0,8},{1,17},{8,0},{9,25},{16,24},{17,1},{24,16},{25,9},{2,10},{3,... | collective-permute-start | bytes 589832 | tf_op jit(solution)/shard_map/ppermute | solution.py:504
  14.4 5.7 %collective-permute-start.4 = (bf16[2,384,128]{2,1,0:T(8,128)(2,1)S(1)}, bf16[2,384,128]{2,1,0:T(8,128)(2,1)S(1)}, u32[]{:S(2)}, u32[]{:S(2)}) collective-permute-start(bf16[2,384,128]{2,1,0:T(8,128)(2,1)S(1)} %join.1.rest_6_), channel_id=1, source_target_pairs={{0,16},{1,9},{8,24},{9,1},{16,0},{17,25},{24,8},{25,17},{2,18},{3,... | collective-permute-start | bytes 589832 | tf_op jit(solution)/shard_map/ppermute | solution.py:509
  15.9 1.3 %collective-permute-start.8 = (bf16[4,2,64,128]{3,2,1,0:T(8,128)(2,1)S(1)}, bf16[4,2,64,128]{3,2,1,0:T(8,128)(2,1)S(1)}, u32[]{:S(2)}, u32[]{:S(2)}) collective-permute-start(bf16[4,2,64,128]{3,2,1,0:T(8,128)(2,1)S(1)} %collective-permute-done.5.rest_1_), channel_id=1, source_target_pairs={{0,1},{1,0},{2,3},{3,2},{4,5},{5,4},{6,7},{7,6},{8,9},{9,8},{10,11... | collective-permute-start | bytes 393224 | tf_op jit(solution)/shard_map/ppermute | solution.py:513
  15.9 1.5 %collective-permute-start.9 = (bf16[4,2,64,128]{3,2,1,0:T(8,128)(2,1)S(1)}, bf16[4,2,64,128]{3,2,1,0:T(8,128)(2,1)S(1)}, u32[]{:S(2)}, u32[]{:S(2)}) collective-permute-start(bf16[4,2,64,128]{3,2,1,0:T(8,128)(2,1)S(1)} %collective-permute-done.6.rest_2_), channel_id=1, source_target_pairs={{0,1},{1,0},{2,3},{3,2},{4,5},{5,4},{6,7},{7,6},{8,9},{9,8},{10,11... | collective-permute-start | bytes 393224 | tf_op jit(solution)/shard_map/ppermute | solution.py:513
  16.5 6.3 %collective-permute-start.11 = (bf16[4,2,64,128]{3,2,1,0:T(8,128)(2,1)S(1)}, bf16[4,2,64,128]{3,2,1,0:T(8,128)(2,1)S(1)}, u32[]{:S(2)}, u32[]{:S(2)}) collective-permute-start(bf16[4,2,64,128]{3,2,1,0:T(8,128)(2,1)S(1)} %collective-permute-done.5.rest_1_), channel_id=1, source_target_pairs={{0,16},{1,9},{8,24},{9,1},{16,0},{17,25},{24,8},{25,17},{2,18},{3,... | collective-permute-start | bytes 393224 | tf_op jit(solution)/shard_map/ppermute | solution.py:509
  20.2 3.9 %collective-permute-start.13 = (bf16[2,384,128]{2,1,0:T(8,128)(2,1)S(1)}, bf16[2,384,128]{2,1,0:T(8,128)(2,1)S(1)}, u32[]{:S(2)}, u32[]{:S(2)}) collective-permute-start(bf16[2,384,128]{2,1,0:T(8,128)(2,1)S(1)} %collective-permute-done.3.rest_2_), channel_id=1, source_target_pairs={{0,1},{1,0},{2,3},{3,2},{4,5},{5,4},{6,7},{7,6},{8,9},{9,8},{10,11... | collective-permute-start | bytes 589832 | tf_op jit(solution)/shard_map/ppermute | solution.py:513
  20.8 3.2 %collective-permute-start.14 = (bf16[2,384,128]{2,1,0:T(8,128)(2,1)S(1)}, bf16[2,384,128]{2,1,0:T(8,128)(2,1)S(1)}, u32[]{:S(2)}, u32[]{:S(2)}) collective-permute-start(bf16[2,384,128]{2,1,0:T(8,128)(2,1)S(1)} %collective-permute-done.4.rest_3_), channel_id=1, source_target_pairs={{0,1},{1,0},{2,3},{3,2},{4,5},{5,4},{6,7},{7,6},{8,9},{9,8},{10,11... | collective-permute-start | bytes 589832 | tf_op jit(solution)/shard_map/ppermute | solution.py:513
  20.8 5.7 %collective-permute-start.15 = (bf16[2,384,128]{2,1,0:T(8,128)(2,1)S(1)}, bf16[2,384,128]{2,1,0:T(8,128)(2,1)S(1)}, u32[]{:S(2)}, u32[]{:S(2)}) collective-permute-start(bf16[2,384,128]{2,1,0:T(8,128)(2,1)S(1)} %collective-permute-done.3.rest_2_), channel_id=1, source_target_pairs={{0,16},{1,9},{8,24},{9,1},{16,0},{17,25},{24,8},{25,17},{2,18},{3,... | collective-permute-start | bytes 589832 | tf_op jit(solution)/shard_map/ppermute | solution.py:509
  22.7 1.3 %collective-permute-start.12 = (bf16[4,2,64,128]{3,2,1,0:T(8,128)(2,1)S(1)}, bf16[4,2,64,128]{3,2,1,0:T(8,128)(2,1)S(1)}, u32[]{:S(2)}, u32[]{:S(2)}) collective-permute-start(bf16[4,2,64,128]{3,2,1,0:T(8,128)(2,1)S(1)} %collective-permute-done.11.rest_0_), channel_id=1, source_target_pairs={{0,1},{1,0},{2,3},{3,2},{4,5},{5,4},{6,7},{7,6},{8,9},{9,8},{10,11... | collective-permute-start | bytes 393224 | tf_op jit(solution)/shard_map/ppermute | solution.py:513
  26.6 1.5 %collective-permute-start.16 = (bf16[2,384,128]{2,1,0:T(8,128)(2,1)S(1)}, bf16[2,384,128]{2,1,0:T(8,128)(2,1)S(1)}, u32[]{:S(2)}, u32[]{:S(2)}) collective-permute-start(bf16[2,384,128]{2,1,0:T(8,128)(2,1)S(1)} %collective-permute-done.15.mine), channel_id=1, source_target_pairs={{0,1},{1,0},{2,3},{3,2},{4,5},{5,4},{6,7},{7,6},{8,9},{9,8},{10,11... | collective-permute-start | bytes 589832 | tf_op jit(solution)/shard_map/ppermute | solution.py:513

commit v4 on v3

--- a/solution.py
+++ b/solution.py
@@ -158,7 +158,7 @@
 
 
 def split_kernel(
-    pool_keys, pool_values, stretch_keys, stretch_values, first, second, third, early, sems
+    pool_keys, pool_values, stretch_keys, stretch_values, third, second, first, early, sems
 ):
     head = lax.axis_index("head")
     copies = []
@@ -192,7 +192,7 @@
     )(pool_keys, pool_values, stretch_keys, stretch_values)
 
 
-def join_kernel(first, second, third, joined):
+def join_kernel(third, second, first, joined):
     for index, piece in enumerate((first, second, third)):
         for which in range(2):
             for within in range(2):
@@ -200,7 +200,7 @@
                 joined[which, start : start + 64, :] = piece[which, within]
 
 
-def join(first, second, third):
+def join(third, second, first):
     return pl.pallas_call(
         join_kernel,
         out_shape=pltpu.VMEM((2, 384, 128), jnp.bfloat16),
@@ -211,7 +211,7 @@
             flops=join_flops, bytes_accessed=400000, transcendentals=0
         ),
         name="join",
-    )(first, second, third)
+    )(third, second, first)
 
 
 def mask_kernel(
@@ -248,6 +248,7 @@
     lane = lax.broadcasted_iota(jnp.int32, (64, 128), 1)
     row = lax.broadcasted_iota(jnp.int32, (64, 128), 0)
     causal = jnp.where(lane - 64 <= row, 0.0, hide)
+    hidden = jnp.where((lane == 0) | (lane == 32), 1.0, 0.0)
     own_heads = lax.broadcasted_iota(jnp.int32, (8, 32), 0) + head * 8
     pick = (own_heads == lax.broadcasted_iota(jnp.int32, (8, 32), 1)).astype(jnp.float32)
     for page in range(8):
@@ -297,12 +298,14 @@
             wide_queries[prompt, rows, :128] = queries[prompt, :, group * 128 : (group + 1) * 128]
             wide_queries[prompt, rows, 128:] = bias.astype(jnp.bfloat16)
         for page in range(32):
-            live = row + page * 64 < length
-            tag = (live & (lane == prompt * 32 + page)) | (
-                ~live & ((lane == 0) | (lane == 32))
-            )
+            tag = jnp.where(lane[:16] == prompt * 32 + page, 1.0, 0.0)
+            tag = jnp.where(page * 64 < length, tag, hidden[:16]).astype(jnp.bfloat16)
             start = prompt * 2048 + page * 64
-            key_tags[start : start + 64, :] = jnp.where(tag, 1.0, 0.0).astype(jnp.bfloat16)
+            key_tags[start : start + 64, :] = jnp.concatenate([tag] * 4, axis=0)
+        page = jnp.minimum(length // 64, 31)
+        tag = jnp.where(lane == prompt * 32 + page, 1.0, 0.0)
+        tag = jnp.where(row + page * 64 < length, tag, hidden).astype(jnp.bfloat16)
+        key_tags[pl.ds(pl.multiple_of(prompt * 2048 + page * 64, 64), 64), :] = tag
 
 
 def mask(lengths, table, queries, vertical, slash):
@@ -524,7 +527,7 @@
     vertical,
     slash,
 ):
-    first, second, third, bundle = split(
+    third, second, first, bundle = split(
         slot_pool_keys, slot_pool_values, stretch_keys, stretch_values
     )
     third, second, first = (
@@ -532,10 +535,10 @@
         for shift, piece in ((3, third), (2, second), (1, first))
     )
     by_first, by_second = to_first(bundle), to_second(bundle)
-    first, lengths = lax.optimization_barrier((first, prefix_lengths))
+    third, lengths = lax.optimization_barrier((third, prefix_lengths))
     masks = mask(lengths, page_slot_table, queries, vertical.T, slash.T)
-    first, second, third, masks = lax.optimization_barrier((first, second, third, masks))
-    joined = join(first, second, third)
+    third, second, first, masks = lax.optimization_barrier((third, second, first, masks))
+    joined = join(third, second, first)
     wide_queries, key_tags, meta = masks
     late_first, late_second = to_first(joined), to_second(joined)
     by_both = to_second(by_first)

time: 30.3 us -> 29.2 us (0.964)
  Pallas kernels: 10.3 us -> 9.29 us
    pallas_call x1, Pallas kernels: 2.41 us -> 1.36 us  [mask(): pl.pallas_call(mask_kernel, out_shape=(pltpu.VMEM((2, 512, 256), jnp.bflo...]
  transfers between devices with their start and end apart: 17 -> 17, of which waited for: 7 -> 7; matrix products, arithmetic and copies ran while one was open for 0% -> 0% of each run, Pallas kernels for 25% -> 22%
where the time goes in v4:
time: 29.2 us; the launch traced here: 29 us
  starting transfers between devices  15.9 us (54%)
  Pallas kernels  9.29 us (32%)
  waiting for transfers between devices  3.79 us (13%)
    pallas_call x3, Pallas kernels, call(): pl.pallas_call(kernel, out_shape=out_shape, in_specs=[smem] + [vmem] * (l...  6.93 us
    ppermute x3, starting transfers between devices, small_body(): lax.ppermute(piece, 'head', [(z, z ^ shift) for z in range(4)])  5.76 us
    ppermute x4, starting transfers between devices, to_second(): return lax.ppermute(value, page_axes, pairs)  5.43 us
    ppermute x8, waiting for transfers between devices, to_sibling(): return lax.ppermute(value, 'pool', [(0, 1), (1, 0)])  3.16 us
    ppermute x2, starting transfers between devices, to_first(): return lax.ppermute(value, page_axes, pairs)  3.12 us
    ppermute x8, starting transfers between devices, to_sibling(): return lax.ppermute(value, 'pool', [(0, 1), (1, 0)])  1.56 us
    pallas_call x1, Pallas kernels, mask(): pl.pallas_call(mask_kernel, out_shape=(pltpu.VMEM((2, 512, 256), jnp.bflo...  1.36 us
    pallas_call x1, Pallas kernels, split(): pl.pallas_call(split_kernel, out_shape=(piece, piece, piece, bundle), in_...  0.99 us
  transfers between devices with their start and end apart: 17, of which 7 were waited for; matrix products, arithmetic and copies ran while one was open for 0% of the time, Pallas kernels for 22%

profile of v4, /device:TPU:0, one launch (start us, length us, event | category | flops | bytes accessed | tf_op | source)
XLA Modules:
  0.0 29.0 jit_solution(10708459230389821483)
XLA Ops:
  0.0 1.0 %split.1 = (bf16[2,2,64,128]{3,2,1,0:T(8,128)(2,1)S(1)}, bf16[2,2,64,128]{3,2,1,0:T(8,128)(2,1)S(1)}, bf16[2,2,64,128]{3,2,1,0:T(8,128)(2,1)S(1)}, bf16[4,2,64,128]{3,2,1,0:T(8,128)(2,1)S(1)}) custom-call(bf16[2,64,512]{2,1,0:T(8,128)(2,1)} %pool_keys.1, bf16[2,64,512]{2,1,0:T(8,128)(2,1)} %pool_values.1, bf16[2,64,128]{2,1,0:T(8,128)(2,1)} %stretch_keys.1, ...), custom_call_target="tpu_custom_call" | custom-call | tf_op jit(solution)/shard_map/split/pallas_call | solution.py:185
  1.0 5.1 %collective-permute-start = (bf16[2,2,64,128]{3,2,1,0:T(8,128)(2,1)S(1)}, bf16[2,2,64,128]{3,2,1,0:T(8,128)(2,1)S(1)}, u32[]{:S(2)}, u32[]{:S(2)}) collective-permute-start(bf16[2,2,64,128]{3,2,1,0:T(8,128)(2,1)S(1)} %get-tuple-element.31), channel_id=1, source_target_pairs={{0,6},{2,4},{4,2},{6,0},{1,7},{3,5},{5,3},{7,1},{8,14},{10,12},{12... | collective-permute-start | bytes 196616 | tf_op jit(solution)/shard_map/ppermute | solution.py:534
  6.1 0.0 collective-permute-start.1
  6.1 0.6 %collective-permute-start.2 = (bf16[2,2,64,128]{3,2,1,0:T(8,128)(2,1)S(1)}, bf16[2,2,64,128]{3,2,1,0:T(8,128)(2,1)S(1)}, u32[]{:S(2)}, u32[]{:S(2)}) collective-permute-start(bf16[2,2,64,128]{3,2,1,0:T(8,128)(2,1)S(1)} %get-tuple-element.34), channel_id=1, source_target_pairs={{0,2},{2,0},{4,6},{6,4},{1,3},{3,1},{5,7},{7,5},{8,10},{10,8},{12,... | collective-permute-start | bytes 196616 | tf_op jit(solution)/shard_map/ppermute | solution.py:534
  6.8 1.6 %collective-permute-start.5 = (bf16[4,2,64,128]{3,2,1,0:T(8,128)(2,1)S(1)}, bf16[4,2,64,128]{3,2,1,0:T(8,128)(2,1)S(1)}, u32[]{:S(2)}, u32[]{:S(2)}) collective-permute-start(bf16[4,2,64,128]{3,2,1,0:T(8,128)(2,1)S(1)} %get-tuple-element.45.rest_0_), channel_id=1, source_target_pairs={{0,8},{1,17},{8,0},{9,25},{16,24},{17,1},{24,16},{25,9},{2,10},{3,... | collective-permute-start | bytes 393224 | tf_op jit(solution)/shard_map/ppermute | solution.py:507
  8.4 1.5 %collective-permute-start.6 = (bf16[4,2,64,128]{3,2,1,0:T(8,128)(2,1)S(1)}, bf16[4,2,64,128]{3,2,1,0:T(8,128)(2,1)S(1)}, u32[]{:S(2)}, u32[]{:S(2)}) collective-permute-start(bf16[4,2,64,128]{3,2,1,0:T(8,128)(2,1)S(1)} %get-tuple-element.45.rest_0_), channel_id=1, source_target_pairs={{0,16},{1,9},{8,24},{9,1},{16,0},{17,25},{24,8},{25,17},{2,18},{3,... | collective-permute-start | bytes 393224 | tf_op jit(solution)/shard_map/ppermute | solution.py:512
  9.9 0.0 collective-permute-done.third
  9.9 0.0 collective-permute-start.7
  9.9 1.4 %mask.1 = (bf16[2,512,256]{2,1,0:T(8,128)(2,1)S(1)}, bf16[4608,128]{1,0:T(8,128)(2,1)S(1)}, s32[72]{0:T(128)S(4)}) custom-call(s32[2]{0:T(128)} %lengths_in, s32[64]{0:T(128)} %table_in.1, bf16[2,64,1024]{2,1,0:T(8,128)(2,1)} %queries_in.1, s32[16,32]{1,0:T(8,128)} %bitcast.2, s32[16,32]{1,0:T(8,128)} %bitcast.3), custom_call_target="tpu_custom_call" | custom-call | bytes 1000 | tf_op jit(solution)/shard_map/mask/pallas_call | solution.py:312
  11.3 0.4 %collective-permute-done.1.second = bf16[2,2,64,128]{3,2,1,0:T(8,128)(2,1)S(1)} collective-permute-done((bf16[2,2,64,128]{3,2,1,0:T(8,128)(2,1)S(1)}, bf16[2,2,64,128]{3,2,1,0:T(8,128)(2,1)S(1)}, u32[]{:S(2)}, u32[]{:S(2)}) %collective-permute-start.1) | collective-permute-done | bytes 65568 | tf_op jit(solution)/shard_map/ppermute | solution.py:534
  11.7 0.2 collective-permute-start.10
  11.9 1.5 %collective-permute-start.3 = (bf16[2,384,128]{2,1,0:T(8,128)(2,1)S(1)}, bf16[2,384,128]{2,1,0:T(8,128)(2,1)S(1)}, u32[]{:S(2)}, u32[]{:S(2)}) collective-permute-start(bf16[2,384,128]{2,1,0:T(8,128)(2,1)S(1)} %join.1.rest_6_), channel_id=1, source_target_pairs={{0,8},{1,17},{8,0},{9,25},{16,24},{17,1},{24,16},{25,9},{2,10},{3,... | collective-permute-start | bytes 589832 | tf_op jit(solution)/shard_map/ppermute | solution.py:507
  13.4 0.0 collective-permute-done.5.rest_1_
  13.4 1.5 %collective-permute-start.4 = (bf16[2,384,128]{2,1,0:T(8,128)(2,1)S(1)}, bf16[2,384,128]{2,1,0:T(8,128)(2,1)S(1)}, u32[]{:S(2)}, u32[]{:S(2)}) collective-permute-start(bf16[2,384,128]{2,1,0:T(8,128)(2,1)S(1)} %join.1.rest_6_), channel_id=1, source_target_pairs={{0,16},{1,9},{8,24},{9,1},{16,0},{17,25},{24,8},{25,17},{2,18},{3,... | collective-permute-start | bytes 589832 | tf_op jit(solution)/shard_map/ppermute | solution.py:512
  14.9 0.0 collective-permute-done.6.rest_2_
  14.9 0.0 collective-permute-start.8
  14.9 0.0 collective-permute-done.7.rest_3_
  14.9 0.5 %collective-permute-start.9 = (bf16[4,2,64,128]{3,2,1,0:T(8,128)(2,1)S(1)}, bf16[4,2,64,128]{3,2,1,0:T(8,128)(2,1)S(1)}, u32[]{:S(2)}, u32[]{:S(2)}) collective-permute-start(bf16[4,2,64,128]{3,2,1,0:T(8,128)(2,1)S(1)} %collective-permute-done.6.rest_2_), channel_id=1, source_target_pairs={{0,1},{1,0},{2,3},{3,2},{4,5},{5,4},{6,7},{7,6},{8,9},{9,8},{10,11... | collective-permute-start | bytes 393224 | tf_op jit(solution)/shard_map/ppermute | solution.py:516
  15.4 0.5 %collective-permute-start.11 = (bf16[4,2,64,128]{3,2,1,0:T(8,128)(2,1)S(1)}, bf16[4,2,64,128]{3,2,1,0:T(8,128)(2,1)S(1)}, u32[]{:S(2)}, u32[]{:S(2)}) collective-permute-start(bf16[4,2,64,128]{3,2,1,0:T(8,128)(2,1)S(1)} %collective-permute-done.5.rest_1_), channel_id=1, source_target_pairs={{0,16},{1,9},{8,24},{9,1},{16,0},{17,25},{24,8},{25,17},{2,18},{3,... | collective-permute-start | bytes 393224 | tf_op jit(solution)/shard_map/ppermute | solution.py:512
  15.9 0.3 %collective-permute-done.8.rest_4_ = bf16[4,2,64,128]{3,2,1,0:T(8,128)(2,1)S(1)} collective-permute-done((bf16[4,2,64,128]{3,2,1,0:T(8,128)(2,1)S(1)}, bf16[4,2,64,128]{3,2,1,0:T(8,128)(2,1)S(1)}, u32[]{:S(2)}, u32[]{:S(2)}) %collective-permute-start.8) | collective-permute-done | bytes 131104 | tf_op jit(solution)/shard_map/ppermute | solution.py:516
  16.3 0.2 collective-permute-done.9.rest_5_
  16.4 2.5 %open.1 = (f32[2,512,128]{2,1,0:T(8,128)S(1)}, f32[2,512,256]{2,1,0:T(8,128)S(1)}) custom-call(s32[72]{0:T(128)S(4)} %get-tuple-element.39.meta, bf16[2,512,256]{2,1,0:T(8,128)(2,1)S(1)} %get-tuple-element.40.wide_queries, bf16[4608,128]{1,0:T(8,128)(2,1)S(1)} %get-tuple-element.41.key_tags, bf16[4,2,64,128]{3,2,1,0:T(8,128)(2,1)S(1)} %get-tuple-element.45.rest_0_, ...), custom_call_target="tpu_custom_call" | custom-call | bytes 1000 | tf_op jit(solution)/shard_map/open/pallas_call | solution.py:469
  18.9 0.1 collective-permute-done.3.rest_2_
  19.0 0.1 collective-permute-done.4.rest_3_
  19.1 0.7 %collective-permute-start.13 = (bf16[2,384,128]{2,1,0:T(8,128)(2,1)S(1)}, bf16[2,384,128]{2,1,0:T(8,128)(2,1)S(1)}, u32[]{:S(2)}, u32[]{:S(2)}) collective-permute-start(bf16[2,384,128]{2,1,0:T(8,128)(2,1)S(1)} %collective-permute-done.3.rest_2_), channel_id=1, source_target_pairs={{0,1},{1,0},{2,3},{3,2},{4,5},{5,4},{6,7},{7,6},{8,9},{9,8},{10,11... | collective-permute-start | bytes 589832 | tf_op jit(solution)/shard_map/ppermute | solution.py:516
  19.8 0.0 collective-permute-start.14
  19.8 1.9 %collective-permute-start.15 = (bf16[2,384,128]{2,1,0:T(8,128)(2,1)S(1)}, bf16[2,384,128]{2,1,0:T(8,128)(2,1)S(1)}, u32[]{:S(2)}, u32[]{:S(2)}) collective-permute-start(bf16[2,384,128]{2,1,0:T(8,128)(2,1)S(1)} %collective-permute-done.3.rest_2_), channel_id=1, source_target_pairs={{0,16},{1,9},{8,24},{9,1},{16,0},{17,25},{24,8},{25,17},{2,18},{3,... | collective-permute-start | bytes 589832 | tf_op jit(solution)/shard_map/ppermute | solution.py:512
  21.7 1.3 %collective-permute-done.12.rest_1_ = bf16[4,2,64,128]{3,2,1,0:T(8,128)(2,1)S(1)} collective-permute-done((bf16[4,2,64,128]{3,2,1,0:T(8,128)(2,1)S(1)}, bf16[4,2,64,128]{3,2,1,0:T(8,128)(2,1)S(1)}, u32[]{:S(2)}, u32[]{:S(2)}) %collective-permute-start.12) | collective-permute-done | bytes 131104 | tf_op jit(solution)/shard_map/ppermute | solution.py:516
  23.1 2.5 %middle.1 = (f32[2,512,128]{2,1,0:T(8,128)S(1)}, f32[2,512,256]{2,1,0:T(8,128)S(1)}) custom-call(s32[72]{0:T(128)S(4)} %get-tuple-element.39.meta, bf16[2,512,256]{2,1,0:T(8,128)(2,1)S(1)} %get-tuple-element.40.wide_queries, bf16[4608,128]{1,0:T(8,128)(2,1)S(1)} %get-tuple-element.41.key_tags, f32[2,512,128]{2,1,0:T(8,128)S(1)} %get-tuple-element.48.before, ...), custom_call_target="tpu_custom_call" | custom-call | bytes 1000 | tf_op jit(solution)/shard_map/middle/pallas_call | solution.py:469
  25.6 0.2 collective-permute-start.16
  25.8 1.3 %collective-permute-done.16.theirs = bf16[2,384,128]{2,1,0:T(8,128)(2,1)S(1)} collective-permute-done((bf16[2,384,128]{2,1,0:T(8,128)(2,1)S(1)}, bf16[2,384,128]{2,1,0:T(8,128)(2,1)S(1)}, u32[]{:S(2)}, u32[]{:S(2)}) %collective-permute-start.16) | collective-permute-done | bytes 196640 | tf_op jit(solution)/shard_map/ppermute | solution.py:516
  27.1 1.9 %close.1 = bf16[2,64,1024]{2,1,0:T(8,128)(2,1)} custom-call(s32[72]{0:T(128)S(4)} %get-tuple-element.39.meta, bf16[2,512,256]{2,1,0:T(8,128)(2,1)S(1)} %get-tuple-element.40.wide_queries, bf16[4608,128]{1,0:T(8,128)(2,1)S(1)} %get-tuple-element.41.key_tags, f32[2,512,128]{2,1,0:T(8,128)S(1)} %get-tuple-element.54.before, ...), custom_call_target="tpu_custom_call" | custom-call | bytes 1000 | tf_op jit(solution)/shard_map/close/pallas_call | solution.py:469
  (8 shorter events, 0.0 us)
Async XLA Ops:
  1.0 8.9 %collective-permute-start = (bf16[2,2,64,128]{3,2,1,0:T(8,128)(2,1)S(1)}, bf16[2,2,64,128]{3,2,1,0:T(8,128)(2,1)S(1)}, u32[]{:S(2)}, u32[]{:S(2)}) collective-permute-start(bf16[2,2,64,128]{3,2,1,0:T(8,128)(2,1)S(1)} %get-tuple-element.31), channel_id=1, source_target_pairs={{0,6},{2,4},{4,2},{6,0},{1,7},{3,5},{5,3},{7,1},{8,14},{10,12},{12... | collective-permute-start | bytes 196616 | tf_op jit(solution)/shard_map/ppermute | solution.py:534
  6.1 5.6 %collective-permute-start.1 = (bf16[2,2,64,128]{3,2,1,0:T(8,128)(2,1)S(1)}, bf16[2,2,64,128]{3,2,1,0:T(8,128)(2,1)S(1)}, u32[]{:S(2)}, u32[]{:S(2)}) collective-permute-start(bf16[2,2,64,128]{3,2,1,0:T(8,128)(2,1)S(1)} %get-tuple-element.33), channel_id=1, source_target_pairs={{0,4},{2,6},{4,0},{6,2},{1,5},{3,7},{5,1},{7,3},{8,12},{10,14},{12... | collective-permute-start | bytes 196616 | tf_op jit(solution)/shard_map/ppermute | solution.py:534
  6.1 5.6 %collective-permute-start.2 = (bf16[2,2,64,128]{3,2,1,0:T(8,128)(2,1)S(1)}, bf16[2,2,64,128]{3,2,1,0:T(8,128)(2,1)S(1)}, u32[]{:S(2)}, u32[]{:S(2)}) collective-permute-start(bf16[2,2,64,128]{3,2,1,0:T(8,128)(2,1)S(1)} %get-tuple-element.34), channel_id=1, source_target_pairs={{0,2},{2,0},{4,6},{6,4},{1,3},{3,1},{5,7},{7,5},{8,10},{10,8},{12,... | collective-permute-start | bytes 196616 | tf_op jit(solution)/shard_map/ppermute | solution.py:534
  6.8 6.6 %collective-permute-start.5 = (bf16[4,2,64,128]{3,2,1,0:T(8,128)(2,1)S(1)}, bf16[4,2,64,128]{3,2,1,0:T(8,128)(2,1)S(1)}, u32[]{:S(2)}, u32[]{:S(2)}) collective-permute-start(bf16[4,2,64,128]{3,2,1,0:T(8,128)(2,1)S(1)} %get-tuple-element.45.rest_0_), channel_id=1, source_target_pairs={{0,8},{1,17},{8,0},{9,25},{16,24},{17,1},{24,16},{25,9},{2,10},{3,... | collective-permute-start | bytes 393224 | tf_op jit(solution)/shard_map/ppermute | solution.py:507
  8.4 6.5 %collective-permute-start.6 = (bf16[4,2,64,128]{3,2,1,0:T(8,128)(2,1)S(1)}, bf16[4,2,64,128]{3,2,1,0:T(8,128)(2,1)S(1)}, u32[]{:S(2)}, u32[]{:S(2)}) collective-permute-start(bf16[4,2,64,128]{3,2,1,0:T(8,128)(2,1)S(1)} %get-tuple-element.45.rest_0_), channel_id=1, source_target_pairs={{0,16},{1,9},{8,24},{9,1},{16,0},{17,25},{24,8},{25,17},{2,18},{3,... | collective-permute-start | bytes 393224 | tf_op jit(solution)/shard_map/ppermute | solution.py:512
  9.9 5.0 %collective-permute-start.7 = (bf16[4,2,64,128]{3,2,1,0:T(8,128)(2,1)S(1)}, bf16[4,2,64,128]{3,2,1,0:T(8,128)(2,1)S(1)}, u32[]{:S(2)}, u32[]{:S(2)}) collective-permute-start(bf16[4,2,64,128]{3,2,1,0:T(8,128)(2,1)S(1)} %get-tuple-element.45.rest_0_), channel_id=1, source_target_pairs={{0,1},{1,0},{2,3},{3,2},{4,5},{5,4},{6,7},{7,6},{8,9},{9,8},{10,11... | collective-permute-start | bytes 393224 | tf_op jit(solution)/shard_map/ppermute | solution.py:516
  11.7 3.7 %collective-permute-start.10 = (bf16[2,384,128]{2,1,0:T(8,128)(2,1)S(1)}, bf16[2,384,128]{2,1,0:T(8,128)(2,1)S(1)}, u32[]{:S(2)}, u32[]{:S(2)}) collective-permute-start(bf16[2,384,128]{2,1,0:T(8,128)(2,1)S(1)} %join.1.rest_6_), channel_id=1, source_target_pairs={{0,1},{1,0},{2,3},{3,2},{4,5},{5,4},{6,7},{7,6},{8,9},{9,8},{10,11... | collective-permute-start | bytes 589832 | tf_op jit(solution)/shard_map/ppermute | solution.py:516
  11.9 7.1 %collective-permute-start.3 = (bf16[2,384,128]{2,1,0:T(8,128)(2,1)S(1)}, bf16[2,384,128]{2,1,0:T(8,128)(2,1)S(1)}, u32[]{:S(2)}, u32[]{:S(2)}) collective-permute-start(bf16[2,384,128]{2,1,0:T(8,128)(2,1)S(1)} %join.1.rest_6_), channel_id=1, source_target_pairs={{0,8},{1,17},{8,0},{9,25},{16,24},{17,1},{24,16},{25,9},{2,10},{3,... | collective-permute-start | bytes 589832 | tf_op jit(solution)/shard_map/ppermute | solution.py:507
  13.4 5.7 %collective-permute-start.4 = (bf16[2,384,128]{2,1,0:T(8,128)(2,1)S(1)}, bf16[2,384,128]{2,1,0:T(8,128)(2,1)S(1)}, u32[]{:S(2)}, u32[]{:S(2)}) collective-permute-start(bf16[2,384,128]{2,1,0:T(8,128)(2,1)S(1)} %join.1.rest_6_), channel_id=1, source_target_pairs={{0,16},{1,9},{8,24},{9,1},{16,0},{17,25},{24,8},{25,17},{2,18},{3,... | collective-permute-start | bytes 589832 | tf_op jit(solution)/shard_map/ppermute | solution.py:512
  14.9 1.3 %collective-permute-start.8 = (bf16[4,2,64,128]{3,2,1,0:T(8,128)(2,1)S(1)}, bf16[4,2,64,128]{3,2,1,0:T(8,128)(2,1)S(1)}, u32[]{:S(2)}, u32[]{:S(2)}) collective-permute-start(bf16[4,2,64,128]{3,2,1,0:T(8,128)(2,1)S(1)} %collective-permute-done.5.rest_1_), channel_id=1, source_target_pairs={{0,1},{1,0},{2,3},{3,2},{4,5},{5,4},{6,7},{7,6},{8,9},{9,8},{10,11... | collective-permute-start | bytes 393224 | tf_op jit(solution)/shard_map/ppermute | solution.py:516
  14.9 1.5 %collective-permute-start.9 = (bf16[4,2,64,128]{3,2,1,0:T(8,128)(2,1)S(1)}, bf16[4,2,64,128]{3,2,1,0:T(8,128)(2,1)S(1)}, u32[]{:S(2)}, u32[]{:S(2)}) collective-permute-start(bf16[4,2,64,128]{3,2,1,0:T(8,128)(2,1)S(1)} %collective-permute-done.6.rest_2_), channel_id=1, source_target_pairs={{0,1},{1,0},{2,3},{3,2},{4,5},{5,4},{6,7},{7,6},{8,9},{9,8},{10,11... | collective-permute-start | bytes 393224 | tf_op jit(solution)/shard_map/ppermute | solution.py:516
  15.4 6.3 %collective-permute-start.11 = (bf16[4,2,64,128]{3,2,1,0:T(8,128)(2,1)S(1)}, bf16[4,2,64,128]{3,2,1,0:T(8,128)(2,1)S(1)}, u32[]{:S(2)}, u32[]{:S(2)}) collective-permute-start(bf16[4,2,64,128]{3,2,1,0:T(8,128)(2,1)S(1)} %collective-permute-done.5.rest_1_), channel_id=1, source_target_pairs={{0,16},{1,9},{8,24},{9,1},{16,0},{17,25},{24,8},{25,17},{2,18},{3,... | collective-permute-start | bytes 393224 | tf_op jit(solution)/shard_map/ppermute | solution.py:512
  19.1 3.9 %collective-permute-start.13 = (bf16[2,384,128]{2,1,0:T(8,128)(2,1)S(1)}, bf16[2,384,128]{2,1,0:T(8,128)(2,1)S(1)}, u32[]{:S(2)}, u32[]{:S(2)}) collective-permute-start(bf16[2,384,128]{2,1,0:T(8,128)(2,1)S(1)} %collective-permute-done.3.rest_2_), channel_id=1, source_target_pairs={{0,1},{1,0},{2,3},{3,2},{4,5},{5,4},{6,7},{7,6},{8,9},{9,8},{10,11... | collective-permute-start | bytes 589832 | tf_op jit(solution)/shard_map/ppermute | solution.py:516
  19.8 3.3 %collective-permute-start.14 = (bf16[2,384,128]{2,1,0:T(8,128)(2,1)S(1)}, bf16[2,384,128]{2,1,0:T(8,128)(2,1)S(1)}, u32[]{:S(2)}, u32[]{:S(2)}) collective-permute-start(bf16[2,384,128]{2,1,0:T(8,128)(2,1)S(1)} %collective-permute-done.4.rest_3_), channel_id=1, source_target_pairs={{0,1},{1,0},{2,3},{3,2},{4,5},{5,4},{6,7},{7,6},{8,9},{9,8},{10,11... | collective-permute-start | bytes 589832 | tf_op jit(solution)/shard_map/ppermute | solution.py:516
  19.8 5.8 %collective-permute-start.15 = (bf16[2,384,128]{2,1,0:T(8,128)(2,1)S(1)}, bf16[2,384,128]{2,1,0:T(8,128)(2,1)S(1)}, u32[]{:S(2)}, u32[]{:S(2)}) collective-permute-start(bf16[2,384,128]{2,1,0:T(8,128)(2,1)S(1)} %collective-permute-done.3.rest_2_), channel_id=1, source_target_pairs={{0,16},{1,9},{8,24},{9,1},{16,0},{17,25},{24,8},{25,17},{2,18},{3,... | collective-permute-start | bytes 589832 | tf_op jit(solution)/shard_map/ppermute | solution.py:512
  21.7 1.3 %collective-permute-start.12 = (bf16[4,2,64,128]{3,2,1,0:T(8,128)(2,1)S(1)}, bf16[4,2,64,128]{3,2,1,0:T(8,128)(2,1)S(1)}, u32[]{:S(2)}, u32[]{:S(2)}) collective-permute-start(bf16[4,2,64,128]{3,2,1,0:T(8,128)(2,1)S(1)} %collective-permute-done.11.rest_0_), channel_id=1, source_target_pairs={{0,1},{1,0},{2,3},{3,2},{4,5},{5,4},{6,7},{7,6},{8,9},{9,8},{10,11... | collective-permute-start | bytes 393224 | tf_op jit(solution)/shard_map/ppermute | solution.py:516
  25.6 1.5 %collective-permute-start.16 = (bf16[2,384,128]{2,1,0:T(8,128)(2,1)S(1)}, bf16[2,384,128]{2,1,0:T(8,128)(2,1)S(1)}, u32[]{:S(2)}, u32[]{:S(2)}) collective-permute-start(bf16[2,384,128]{2,1,0:T(8,128)(2,1)S(1)} %collective-permute-done.15.mine), channel_id=1, source_target_pairs={{0,1},{1,0},{2,3},{3,2},{4,5},{5,4},{6,7},{7,6},{8,9},{9,8},{10,11... | collective-permute-start | bytes 589832 | tf_op jit(solution)/shard_map/ppermute | solution.py:516

commit v5 on v4

--- a/solution.py
+++ b/solution.py
@@ -153,6 +153,7 @@
 scale = 1.4426950408889634 / math.sqrt(128.0)
 join_flops = 6 * 10**9
 mask_flops = 0
+beside_flops = 20 * 10**8
 vmem = pl.BlockSpec(memory_space=pltpu.VMEM)
 smem = pl.BlockSpec(memory_space=pltpu.SMEM)
 
@@ -442,20 +443,30 @@
 
 
 def middle_kernel(meta, wide_queries, key_tags, before, given, *rest):
-    bundles, pieces = rest[:2], rest[2:6]
-    high_out, sums_out, scores = rest[6:]
-    shared, own = [], ([], [])
+    pieces = rest[:4]
+    high_out, sums_out, scores = rest[4:]
+    shared = []
+    for other in range(2):
+        for role in range(2):
+            shared += joined_pages(meta, key_tags, pieces[other * 2 + role], other, 1 + role)
+    state = (before, given)
+    keep(absorb_pages(wide_queries, shared, ([], []), state, scores), high_out, sums_out)
+
+
+def beside_kernel(meta, wide_queries, key_tags, before, given, *rest):
+    bundles, mine = rest[:2], rest[2]
+    high_out, sums_out, scores = rest[3:]
+    shared, own = joined_pages(meta, key_tags, mine, 0, 3), ([], [])
     for other in range(2):
         shared += bundle_pages(meta, key_tags, bundles[other], other, 3)
         for prompt in range(2):
             own[prompt].extend(bundle_stretch(key_tags, bundles[other], other, 3, prompt))
-        for role in range(2):
-            shared += joined_pages(meta, key_tags, pieces[other * 2 + role], other, 1 + role)
-    keep(absorb_pages(wide_queries, shared, own, (before, given), scores), high_out, sums_out)
-
-
-def close_kernel(meta, wide_queries, key_tags, before, given, mine, theirs, result, scores):
-    shared = joined_pages(meta, key_tags, mine, 0, 3) + joined_pages(meta, key_tags, theirs, 1, 3)
+    state = (before, given)
+    keep(absorb_pages(wide_queries, shared, own, state, scores), high_out, sums_out)
+
+
+def close_kernel(meta, wide_queries, key_tags, before, given, theirs, result, scores):
+    shared = joined_pages(meta, key_tags, theirs, 1, 3)
     results = absorb_pages(wide_queries, shared, ([], []), (before, given), scores)
     for prompt, (_, numerator, totals) in enumerate(results):
         attended = (numerator / totals).astype(jnp.bfloat16)
@@ -464,7 +475,7 @@
             result[prompt, :, group * 128 : (group + 1) * 128] = attended[rows, :]
 
 
-def call(kernel, name, out_shape, keys, *operands):
+def call(kernel, name, out_shape, keys, *operands, flops=0):
     single = not isinstance(out_shape, tuple)
     return pl.pallas_call(
         kernel,
@@ -473,7 +484,7 @@
         out_specs=vmem if single else (vmem,) * len(out_shape),
         scratch_shapes=[pltpu.VMEM((2, 512, keys), jnp.float32)],
         compiler_params=pltpu.CompilerParams(vmem_limit_bytes=40 * 2**20),
-        cost_estimate=pl.CostEstimate(flops=0, bytes_accessed=1000, transcendentals=0),
+        cost_estimate=pl.CostEstimate(flops=flops, bytes_accessed=1000, transcendentals=0),
         name=name,
     )(*operands)
 
@@ -488,17 +499,24 @@
     )
 
 
-def middle_stage(meta, wide_queries, key_tags, state, bundles, pieces):
+def middle_stage(meta, wide_queries, key_tags, state, pieces):
     return call(
-        middle_kernel, "middle", running(), 30 * 64,
-        meta, wide_queries, key_tags, *state, *bundles, *pieces,
-    )
-
-
-def close_stage(meta, wide_queries, key_tags, state, mine, theirs):
+        middle_kernel, "middle", running(), 24 * 64,
+        meta, wide_queries, key_tags, *state, *pieces,
+    )
+
+
+def beside_stage(meta, wide_queries, key_tags, state, bundles, mine):
     return call(
-        close_kernel, "close", jax.ShapeDtypeStruct((2, 64, 1024), jnp.bfloat16), 12 * 64,
-        meta, wide_queries, key_tags, *state, mine, theirs,
+        beside_kernel, "beside", running(), 12 * 64,
+        meta, wide_queries, key_tags, *state, *bundles, mine, flops=beside_flops,
+    )
+
+
+def close_stage(meta, wide_queries, key_tags, state, theirs):
+    return call(
+        close_kernel, "close", jax.ShapeDtypeStruct((2, 64, 1024), jnp.bfloat16), 6 * 64,
+        meta, wide_queries, key_tags, *state, theirs,
     )
 
 
@@ -549,13 +567,12 @@
     late_both = to_second(late_first)
     late = [late_first, late_second]
     late += [to_sibling(one) for one in late]
-    state = middle_stage(
-        meta, wide_queries, key_tags, state, [by_both, to_sibling(by_both)], late
-    )
+    state = middle_stage(meta, wide_queries, key_tags, state, late)
     state, late_both = lax.optimization_barrier((state, late_both))
-    return close_stage(
-        meta, wide_queries, key_tags, state, late_both, to_sibling(late_both)
-    )
+    far = [by_both, to_sibling(by_both)]
+    theirs = to_sibling(late_both)
+    state = beside_stage(meta, wide_queries, key_tags, state, far, late_both)
+    return close_stage(meta, wide_queries, key_tags, state, theirs)
 
 
 def solution(mesh):

time: 29.2 us -> 28.9 us (0.990)
  waiting for transfers between devices: 3.79 us -> 2.94 us
  Pallas kernels: 9.29 us -> 9.94 us
    ppermute x8, waiting for transfers between devices: 3.16 us -> 0.53 us  [to_sibling(): return lax.ppermute(value, 'pool', [(0, 1), (1, 0)])]
    ppermute x4, waiting for transfers between devices: 0.1 us -> 1.88 us  [to_second(): return lax.ppermute(value, page_axes, pairs)]
    pallas_call x3 -> x4, Pallas kernels: 6.93 us -> 7.58 us  [call(): pl.pallas_call(kernel, out_shape=out_shape, in_specs=[smem] + [vmem] * (l...]
  transfers between devices with their start and end apart: 17 -> 17, of which waited for: 7 -> 6; matrix products, arithmetic and copies ran while one was open for 0% -> 0% of each run, Pallas kernels for 22% -> 26%
where the time goes in v5:
time: 28.9 us; the launch traced here: 28.6 us
  starting transfers between devices  15.7 us (54%)
  Pallas kernels  9.94 us (34%)
  waiting for transfers between devices  2.94 us (10%)
    pallas_call x4, Pallas kernels, call(): pl.pallas_call(kernel, out_shape=out_shape, in_specs=[smem] + [vmem] * (l...  7.58 us
    ppermute x3, starting transfers between devices, small_body(): lax.ppermute(piece, 'head', [(z, z ^ shift) for z in range(4)])  5.76 us
    ppermute x4, starting transfers between devices, to_second(): return lax.ppermute(value, page_axes, pairs)  5.43 us
    ppermute x2, starting transfers between devices, to_first(): return lax.ppermute(value, page_axes, pairs)  3.12 us
    ppermute x4, waiting for transfers between devices, to_second(): return lax.ppermute(value, page_axes, pairs)  1.88 us
    pallas_call x1, Pallas kernels, mask(): pl.pallas_call(mask_kernel, out_shape=(pltpu.VMEM((2, 512, 256), jnp.bflo...  1.36 us
    ppermute x8, starting transfers between devices, to_sibling(): return lax.ppermute(value, 'pool', [(0, 1), (1, 0)])  1.35 us
    pallas_call x1, Pallas kernels, split(): pl.pallas_call(split_kernel, out_shape=(piece, piece, piece, bundle), in_...  0.99 us
  transfers between devices with their start and end apart: 17, of which 6 were waited for; matrix products, arithmetic and copies ran while one was open for 0% of the time, Pallas kernels for 26%

profile of v5, /device:TPU:0, one launch (start us, length us, event | category | flops | bytes accessed | tf_op | source)
XLA Modules:
  0.0 28.6 jit_solution(5228403671574433884)
XLA Ops:
  0.0 1.0 %split.1 = (bf16[2,2,64,128]{3,2,1,0:T(8,128)(2,1)S(1)}, bf16[2,2,64,128]{3,2,1,0:T(8,128)(2,1)S(1)}, bf16[2,2,64,128]{3,2,1,0:T(8,128)(2,1)S(1)}, bf16[4,2,64,128]{3,2,1,0:T(8,128)(2,1)S(1)}) custom-call(bf16[2,64,512]{2,1,0:T(8,128)(2,1)} %pool_keys.1, bf16[2,64,512]{2,1,0:T(8,128)(2,1)} %pool_values.1, bf16[2,64,128]{2,1,0:T(8,128)(2,1)} %stretch_keys.1, ...), custom_call_target="tpu_custom_call" | custom-call | tf_op jit(solution)/shard_map/split/pallas_call | solution.py:186
  1.0 5.1 %collective-permute-start = (bf16[2,2,64,128]{3,2,1,0:T(8,128)(2,1)S(1)}, bf16[2,2,64,128]{3,2,1,0:T(8,128)(2,1)S(1)}, u32[]{:S(2)}, u32[]{:S(2)}) collective-permute-start(bf16[2,2,64,128]{3,2,1,0:T(8,128)(2,1)S(1)} %get-tuple-element.33), channel_id=1, source_target_pairs={{0,6},{2,4},{4,2},{6,0},{1,7},{3,5},{5,3},{7,1},{8,14},{10,12},{12... | collective-permute-start | bytes 196616 | tf_op jit(solution)/shard_map/ppermute | solution.py:552
  6.1 0.0 collective-permute-start.1
  6.1 0.6 %collective-permute-start.2 = (bf16[2,2,64,128]{3,2,1,0:T(8,128)(2,1)S(1)}, bf16[2,2,64,128]{3,2,1,0:T(8,128)(2,1)S(1)}, u32[]{:S(2)}, u32[]{:S(2)}) collective-permute-start(bf16[2,2,64,128]{3,2,1,0:T(8,128)(2,1)S(1)} %get-tuple-element.36), channel_id=1, source_target_pairs={{0,2},{2,0},{4,6},{6,4},{1,3},{3,1},{5,7},{7,5},{8,10},{10,8},{12,... | collective-permute-start | bytes 196616 | tf_op jit(solution)/shard_map/ppermute | solution.py:552
  6.8 1.6 %collective-permute-start.5 = (bf16[4,2,64,128]{3,2,1,0:T(8,128)(2,1)S(1)}, bf16[4,2,64,128]{3,2,1,0:T(8,128)(2,1)S(1)}, u32[]{:S(2)}, u32[]{:S(2)}) collective-permute-start(bf16[4,2,64,128]{3,2,1,0:T(8,128)(2,1)S(1)} %get-tuple-element.47.rest_0_), channel_id=1, source_target_pairs={{0,8},{1,17},{8,0},{9,25},{16,24},{17,1},{24,16},{25,9},{2,10},{3,... | collective-permute-start | bytes 393224 | tf_op jit(solution)/shard_map/ppermute | solution.py:525
  8.4 1.5 %collective-permute-start.6 = (bf16[4,2,64,128]{3,2,1,0:T(8,128)(2,1)S(1)}, bf16[4,2,64,128]{3,2,1,0:T(8,128)(2,1)S(1)}, u32[]{:S(2)}, u32[]{:S(2)}) collective-permute-start(bf16[4,2,64,128]{3,2,1,0:T(8,128)(2,1)S(1)} %get-tuple-element.47.rest_0_), channel_id=1, source_target_pairs={{0,16},{1,9},{8,24},{9,1},{16,0},{17,25},{24,8},{25,17},{2,18},{3,... | collective-permute-start | bytes 393224 | tf_op jit(solution)/shard_map/ppermute | solution.py:530
  9.9 0.0 collective-permute-done.third
  9.9 0.0 collective-permute-start.7
  9.9 1.4 %mask.1 = (bf16[2,512,256]{2,1,0:T(8,128)(2,1)S(1)}, bf16[4608,128]{1,0:T(8,128)(2,1)S(1)}, s32[72]{0:T(128)S(4)}) custom-call(s32[2]{0:T(128)} %lengths_in, s32[64]{0:T(128)} %table_in.1, bf16[2,64,1024]{2,1,0:T(8,128)(2,1)} %queries_in.1, s32[16,32]{1,0:T(8,128)} %bitcast.2, s32[16,32]{1,0:T(8,128)} %bitcast.3), custom_call_target="tpu_custom_call" | custom-call | bytes 1000 | tf_op jit(solution)/shard_map/mask/pallas_call | solution.py:313
  11.3 0.4 %collective-permute-done.1.second = bf16[2,2,64,128]{3,2,1,0:T(8,128)(2,1)S(1)} collective-permute-done((bf16[2,2,64,128]{3,2,1,0:T(8,128)(2,1)S(1)}, bf16[2,2,64,128]{3,2,1,0:T(8,128)(2,1)S(1)}, u32[]{:S(2)}, u32[]{:S(2)}) %collective-permute-start.1) | collective-permute-done | bytes 65568 | tf_op jit(solution)/shard_map/ppermute | solution.py:552
  11.7 0.0 collective-permute-done.2.first
  11.7 0.2 collective-permute-start.10
  11.9 1.5 %collective-permute-start.3 = (bf16[2,384,128]{2,1,0:T(8,128)(2,1)S(1)}, bf16[2,384,128]{2,1,0:T(8,128)(2,1)S(1)}, u32[]{:S(2)}, u32[]{:S(2)}) collective-permute-start(bf16[2,384,128]{2,1,0:T(8,128)(2,1)S(1)} %join.1.rest_6_), channel_id=1, source_target_pairs={{0,8},{1,17},{8,0},{9,25},{16,24},{17,1},{24,16},{25,9},{2,10},{3,... | collective-permute-start | bytes 589832 | tf_op jit(solution)/shard_map/ppermute | solution.py:525
  13.4 1.5 %collective-permute-start.4 = (bf16[2,384,128]{2,1,0:T(8,128)(2,1)S(1)}, bf16[2,384,128]{2,1,0:T(8,128)(2,1)S(1)}, u32[]{:S(2)}, u32[]{:S(2)}) collective-permute-start(bf16[2,384,128]{2,1,0:T(8,128)(2,1)S(1)} %join.1.rest_6_), channel_id=1, source_target_pairs={{0,16},{1,9},{8,24},{9,1},{16,0},{17,25},{24,8},{25,17},{2,18},{3,... | collective-permute-start | bytes 589832 | tf_op jit(solution)/shard_map/ppermute | solution.py:530
  14.9 0.5 %collective-permute-start.9 = (bf16[4,2,64,128]{3,2,1,0:T(8,128)(2,1)S(1)}, bf16[4,2,64,128]{3,2,1,0:T(8,128)(2,1)S(1)}, u32[]{:S(2)}, u32[]{:S(2)}) collective-permute-start(bf16[4,2,64,128]{3,2,1,0:T(8,128)(2,1)S(1)} %collective-permute-done.6.rest_2_), channel_id=1, source_target_pairs={{0,1},{1,0},{2,3},{3,2},{4,5},{5,4},{6,7},{7,6},{8,9},{9,8},{10,11... | collective-permute-start | bytes 393224 | tf_op jit(solution)/shard_map/ppermute | solution.py:534
  15.4 0.0 collective-permute-done.10.rest_7_
  15.4 0.5 %collective-permute-start.14 = (bf16[4,2,64,128]{3,2,1,0:T(8,128)(2,1)S(1)}, bf16[4,2,64,128]{3,2,1,0:T(8,128)(2,1)S(1)}, u32[]{:S(2)}, u32[]{:S(2)}) collective-permute-start(bf16[4,2,64,128]{3,2,1,0:T(8,128)(2,1)S(1)} %collective-permute-done.5.rest_1_), channel_id=1, source_target_pairs={{0,16},{1,9},{8,24},{9,1},{16,0},{17,25},{24,8},{25,17},{2,18},{3,... | collective-permute-start | bytes 393224 | tf_op jit(solution)/shard_map/ppermute | solution.py:530
  15.9 0.3 %collective-permute-done.8.rest_4_ = bf16[4,2,64,128]{3,2,1,0:T(8,128)(2,1)S(1)} collective-permute-done((bf16[4,2,64,128]{3,2,1,0:T(8,128)(2,1)S(1)}, bf16[4,2,64,128]{3,2,1,0:T(8,128)(2,1)S(1)}, u32[]{:S(2)}, u32[]{:S(2)}) %collective-permute-start.8) | collective-permute-done | bytes 131104 | tf_op jit(solution)/shard_map/ppermute | solution.py:534
  16.3 0.2 collective-permute-done.9.rest_5_
  16.4 2.5 %open.1 = (f32[2,512,128]{2,1,0:T(8,128)S(1)}, f32[2,512,256]{2,1,0:T(8,128)S(1)}) custom-call(s32[72]{0:T(128)S(4)} %get-tuple-element.41.meta, bf16[2,512,256]{2,1,0:T(8,128)(2,1)S(1)} %get-tuple-element.42.wide_queries, bf16[4608,128]{1,0:T(8,128)(2,1)S(1)} %get-tuple-element.43.key_tags, bf16[4,2,64,128]{3,2,1,0:T(8,128)(2,1)S(1)} %get-tuple-element.47.rest_0_, ...), custom_call_target="tpu_custom_call" | custom-call | bytes 1000 | tf_op jit(solution)/shard_map/open/pallas_call | solution.py:480
  18.9 0.1 collective-permute-done.3.rest_0_
  19.0 0.1 collective-permute-done.4.rest_1_
  19.1 0.7 %collective-permute-start.11 = (bf16[2,384,128]{2,1,0:T(8,128)(2,1)S(1)}, bf16[2,384,128]{2,1,0:T(8,128)(2,1)S(1)}, u32[]{:S(2)}, u32[]{:S(2)}) collective-permute-start(bf16[2,384,128]{2,1,0:T(8,128)(2,1)S(1)} %collective-permute-done.3.rest_0_), channel_id=1, source_target_pairs={{0,1},{1,0},{2,3},{3,2},{4,5},{5,4},{6,7},{7,6},{8,9},{9,8},{10,11... | collective-permute-start | bytes 589832 | tf_op jit(solution)/shard_map/ppermute | solution.py:534
  19.8 0.0 collective-permute-start.12
  19.8 1.9 %collective-permute-start.13 = (bf16[2,384,128]{2,1,0:T(8,128)(2,1)S(1)}, bf16[2,384,128]{2,1,0:T(8,128)(2,1)S(1)}, u32[]{:S(2)}, u32[]{:S(2)}) collective-permute-start(bf16[2,384,128]{2,1,0:T(8,128)(2,1)S(1)} %collective-permute-done.3.rest_0_), channel_id=1, source_target_pairs={{0,16},{1,9},{8,24},{9,1},{16,0},{17,25},{24,8},{25,17},{2,18},{3,... | collective-permute-start | bytes 589832 | tf_op jit(solution)/shard_map/ppermute | solution.py:530
  21.7 0.0 collective-permute-done.11.rest_2_
  21.7 0.0 collective-permute-done.12.rest_3_
  21.7 2.0 %middle.1 = (f32[2,512,128]{2,1,0:T(8,128)S(1)}, f32[2,512,256]{2,1,0:T(8,128)S(1)}) custom-call(s32[72]{0:T(128)S(4)} %get-tuple-element.41.meta, bf16[2,512,256]{2,1,0:T(8,128)(2,1)S(1)} %get-tuple-element.42.wide_queries, bf16[4608,128]{1,0:T(8,128)(2,1)S(1)} %get-tuple-element.43.key_tags, f32[2,512,128]{2,1,0:T(8,128)S(1)} %get-tuple-element.50.before, ...), custom_call_target="tpu_custom_call" | custom-call | bytes 1000 | tf_op jit(solution)/shard_map/middle/pallas_call | solution.py:480
  23.7 1.8 %collective-permute-done.13.rest_2_ = bf16[2,384,128]{2,1,0:T(8,128)(2,1)S(1)} collective-permute-done((bf16[2,384,128]{2,1,0:T(8,128)(2,1)S(1)}, bf16[2,384,128]{2,1,0:T(8,128)(2,1)S(1)}, u32[]{:S(2)}, u32[]{:S(2)}) %collective-permute-start.13) | collective-permute-done | bytes 196640 | tf_op jit(solution)/shard_map/ppermute | solution.py:530
  25.5 0.0 collective-permute-start.16
  25.5 1.5 %beside.1 = (f32[2,512,128]{2,1,0:T(8,128)S(1)}, f32[2,512,256]{2,1,0:T(8,128)S(1)}) custom-call(s32[72]{0:T(128)S(4)} %get-tuple-element.41.meta, bf16[2,512,256]{2,1,0:T(8,128)(2,1)S(1)} %get-tuple-element.42.wide_queries, bf16[4608,128]{1,0:T(8,128)(2,1)S(1)} %get-tuple-element.43.key_tags, f32[2,512,128]{2,1,0:T(8,128)S(1)} %get-tuple-element.56.before, ...), custom_call_target="tpu_custom_call" | custom-call | flops 2000000000 | bytes 1000 | tf_op jit(solution)/shard_map/beside/pallas_call | solution.py:480
  27.0 1.6 %close.1 = bf16[2,64,1024]{2,1,0:T(8,128)(2,1)} custom-call(s32[72]{0:T(128)S(4)} %get-tuple-element.41.meta, bf16[2,512,256]{2,1,0:T(8,128)(2,1)S(1)} %get-tuple-element.42.wide_queries, bf16[4608,128]{1,0:T(8,128)(2,1)S(1)} %get-tuple-element.43.key_tags, f32[2,512,128]{2,1,0:T(8,128)S(1)} %get-tuple-element.59.before, ...), custom_call_target="tpu_custom_call" | custom-call | bytes 1000 | tf_op jit(solution)/shard_map/close/pallas_call | solution.py:480
  (9 shorter events, 0.0 us)
Async XLA Ops:
  1.0 8.9 %collective-permute-start = (bf16[2,2,64,128]{3,2,1,0:T(8,128)(2,1)S(1)}, bf16[2,2,64,128]{3,2,1,0:T(8,128)(2,1)S(1)}, u32[]{:S(2)}, u32[]{:S(2)}) collective-permute-start(bf16[2,2,64,128]{3,2,1,0:T(8,128)(2,1)S(1)} %get-tuple-element.33), channel_id=1, source_target_pairs={{0,6},{2,4},{4,2},{6,0},{1,7},{3,5},{5,3},{7,1},{8,14},{10,12},{12... | collective-permute-start | bytes 196616 | tf_op jit(solution)/shard_map/ppermute | solution.py:552
  6.1 5.6 %collective-permute-start.1 = (bf16[2,2,64,128]{3,2,1,0:T(8,128)(2,1)S(1)}, bf16[2,2,64,128]{3,2,1,0:T(8,128)(2,1)S(1)}, u32[]{:S(2)}, u32[]{:S(2)}) collective-permute-start(bf16[2,2,64,128]{3,2,1,0:T(8,128)(2,1)S(1)} %get-tuple-element.35), channel_id=1, source_target_pairs={{0,4},{2,6},{4,0},{6,2},{1,5},{3,7},{5,1},{7,3},{8,12},{10,14},{12... | collective-permute-start | bytes 196616 | tf_op jit(solution)/shard_map/ppermute | solution.py:552
  6.1 5.6 %collective-permute-start.2 = (bf16[2,2,64,128]{3,2,1,0:T(8,128)(2,1)S(1)}, bf16[2,2,64,128]{3,2,1,0:T(8,128)(2,1)S(1)}, u32[]{:S(2)}, u32[]{:S(2)}) collective-permute-start(bf16[2,2,64,128]{3,2,1,0:T(8,128)(2,1)S(1)} %get-tuple-element.36), channel_id=1, source_target_pairs={{0,2},{2,0},{4,6},{6,4},{1,3},{3,1},{5,7},{7,5},{8,10},{10,8},{12,... | collective-permute-start | bytes 196616 | tf_op jit(solution)/shard_map/ppermute | solution.py:552
  6.8 6.6 %collective-permute-start.5 = (bf16[4,2,64,128]{3,2,1,0:T(8,128)(2,1)S(1)}, bf16[4,2,64,128]{3,2,1,0:T(8,128)(2,1)S(1)}, u32[]{:S(2)}, u32[]{:S(2)}) collective-permute-start(bf16[4,2,64,128]{3,2,1,0:T(8,128)(2,1)S(1)} %get-tuple-element.47.rest_0_), channel_id=1, source_target_pairs={{0,8},{1,17},{8,0},{9,25},{16,24},{17,1},{24,16},{25,9},{2,10},{3,... | collective-permute-start | bytes 393224 | tf_op jit(solution)/shard_map/ppermute | solution.py:525
  8.4 6.5 %collective-permute-start.6 = (bf16[4,2,64,128]{3,2,1,0:T(8,128)(2,1)S(1)}, bf16[4,2,64,128]{3,2,1,0:T(8,128)(2,1)S(1)}, u32[]{:S(2)}, u32[]{:S(2)}) collective-permute-start(bf16[4,2,64,128]{3,2,1,0:T(8,128)(2,1)S(1)} %get-tuple-element.47.rest_0_), channel_id=1, source_target_pairs={{0,16},{1,9},{8,24},{9,1},{16,0},{17,25},{24,8},{25,17},{2,18},{3,... | collective-permute-start | bytes 393224 | tf_op jit(solution)/shard_map/ppermute | solution.py:530
  9.9 5.0 %collective-permute-start.7 = (bf16[4,2,64,128]{3,2,1,0:T(8,128)(2,1)S(1)}, bf16[4,2,64,128]{3,2,1,0:T(8,128)(2,1)S(1)}, u32[]{:S(2)}, u32[]{:S(2)}) collective-permute-start(bf16[4,2,64,128]{3,2,1,0:T(8,128)(2,1)S(1)} %get-tuple-element.47.rest_0_), channel_id=1, source_target_pairs={{0,1},{1,0},{2,3},{3,2},{4,5},{5,4},{6,7},{7,6},{8,9},{9,8},{10,11... | collective-permute-start | bytes 393224 | tf_op jit(solution)/shard_map/ppermute | solution.py:534
  11.7 3.7 %collective-permute-start.10 = (bf16[2,384,128]{2,1,0:T(8,128)(2,1)S(1)}, bf16[2,384,128]{2,1,0:T(8,128)(2,1)S(1)}, u32[]{:S(2)}, u32[]{:S(2)}) collective-permute-start(bf16[2,384,128]{2,1,0:T(8,128)(2,1)S(1)} %join.1.rest_6_), channel_id=1, source_target_pairs={{0,1},{1,0},{2,3},{3,2},{4,5},{5,4},{6,7},{7,6},{8,9},{9,8},{10,11... | collective-permute-start | bytes 589832 | tf_op jit(solution)/shard_map/ppermute | solution.py:534
  11.9 7.1 %collective-permute-start.3 = (bf16[2,384,128]{2,1,0:T(8,128)(2,1)S(1)}, bf16[2,384,128]{2,1,0:T(8,128)(2,1)S(1)}, u32[]{:S(2)}, u32[]{:S(2)}) collective-permute-start(bf16[2,384,128]{2,1,0:T(8,128)(2,1)S(1)} %join.1.rest_6_), channel_id=1, source_target_pairs={{0,8},{1,17},{8,0},{9,25},{16,24},{17,1},{24,16},{25,9},{2,10},{3,... | collective-permute-start | bytes 589832 | tf_op jit(solution)/shard_map/ppermute | solution.py:525
  13.4 5.7 %collective-permute-start.4 = (bf16[2,384,128]{2,1,0:T(8,128)(2,1)S(1)}, bf16[2,384,128]{2,1,0:T(8,128)(2,1)S(1)}, u32[]{:S(2)}, u32[]{:S(2)}) collective-permute-start(bf16[2,384,128]{2,1,0:T(8,128)(2,1)S(1)} %join.1.rest_6_), channel_id=1, source_target_pairs={{0,16},{1,9},{8,24},{9,1},{16,0},{17,25},{24,8},{25,17},{2,18},{3,... | collective-permute-start | bytes 589832 | tf_op jit(solution)/shard_map/ppermute | solution.py:530
  14.9 1.3 %collective-permute-start.8 = (bf16[4,2,64,128]{3,2,1,0:T(8,128)(2,1)S(1)}, bf16[4,2,64,128]{3,2,1,0:T(8,128)(2,1)S(1)}, u32[]{:S(2)}, u32[]{:S(2)}) collective-permute-start(bf16[4,2,64,128]{3,2,1,0:T(8,128)(2,1)S(1)} %collective-permute-done.5.rest_1_), channel_id=1, source_target_pairs={{0,1},{1,0},{2,3},{3,2},{4,5},{5,4},{6,7},{7,6},{8,9},{9,8},{10,11... | collective-permute-start | bytes 393224 | tf_op jit(solution)/shard_map/ppermute | solution.py:534
  14.9 1.5 %collective-permute-start.9 = (bf16[4,2,64,128]{3,2,1,0:T(8,128)(2,1)S(1)}, bf16[4,2,64,128]{3,2,1,0:T(8,128)(2,1)S(1)}, u32[]{:S(2)}, u32[]{:S(2)}) collective-permute-start(bf16[4,2,64,128]{3,2,1,0:T(8,128)(2,1)S(1)} %collective-permute-done.6.rest_2_), channel_id=1, source_target_pairs={{0,1},{1,0},{2,3},{3,2},{4,5},{5,4},{6,7},{7,6},{8,9},{9,8},{10,11... | collective-permute-start | bytes 393224 | tf_op jit(solution)/shard_map/ppermute | solution.py:534
  15.4 6.3 %collective-permute-start.14 = (bf16[4,2,64,128]{3,2,1,0:T(8,128)(2,1)S(1)}, bf16[4,2,64,128]{3,2,1,0:T(8,128)(2,1)S(1)}, u32[]{:S(2)}, u32[]{:S(2)}) collective-permute-start(bf16[4,2,64,128]{3,2,1,0:T(8,128)(2,1)S(1)} %collective-permute-done.5.rest_1_), channel_id=1, source_target_pairs={{0,16},{1,9},{8,24},{9,1},{16,0},{17,25},{24,8},{25,17},{2,18},{3,... | collective-permute-start | bytes 393224 | tf_op jit(solution)/shard_map/ppermute | solution.py:530
  19.1 2.6 %collective-permute-start.11 = (bf16[2,384,128]{2,1,0:T(8,128)(2,1)S(1)}, bf16[2,384,128]{2,1,0:T(8,128)(2,1)S(1)}, u32[]{:S(2)}, u32[]{:S(2)}) collective-permute-start(bf16[2,384,128]{2,1,0:T(8,128)(2,1)S(1)} %collective-permute-done.3.rest_0_), channel_id=1, source_target_pairs={{0,1},{1,0},{2,3},{3,2},{4,5},{5,4},{6,7},{7,6},{8,9},{9,8},{10,11... | collective-permute-start | bytes 589832 | tf_op jit(solution)/shard_map/ppermute | solution.py:534
  19.8 1.9 %collective-permute-start.12 = (bf16[2,384,128]{2,1,0:T(8,128)(2,1)S(1)}, bf16[2,384,128]{2,1,0:T(8,128)(2,1)S(1)}, u32[]{:S(2)}, u32[]{:S(2)}) collective-permute-start(bf16[2,384,128]{2,1,0:T(8,128)(2,1)S(1)} %collective-permute-done.4.rest_1_), channel_id=1, source_target_pairs={{0,1},{1,0},{2,3},{3,2},{4,5},{5,4},{6,7},{7,6},{8,9},{9,8},{10,11... | collective-permute-start | bytes 589832 | tf_op jit(solution)/shard_map/ppermute | solution.py:534
  19.8 5.7 %collective-permute-start.13 = (bf16[2,384,128]{2,1,0:T(8,128)(2,1)S(1)}, bf16[2,384,128]{2,1,0:T(8,128)(2,1)S(1)}, u32[]{:S(2)}, u32[]{:S(2)}) collective-permute-start(bf16[2,384,128]{2,1,0:T(8,128)(2,1)S(1)} %collective-permute-done.3.rest_0_), channel_id=1, source_target_pairs={{0,16},{1,9},{8,24},{9,1},{16,0},{17,25},{24,8},{25,17},{2,18},{3,... | collective-permute-start | bytes 589832 | tf_op jit(solution)/shard_map/ppermute | solution.py:530
  21.7 3.8 %collective-permute-start.15 = (bf16[4,2,64,128]{3,2,1,0:T(8,128)(2,1)S(1)}, bf16[4,2,64,128]{3,2,1,0:T(8,128)(2,1)S(1)}, u32[]{:S(2)}, u32[]{:S(2)}) collective-permute-start(bf16[4,2,64,128]{3,2,1,0:T(8,128)(2,1)S(1)} %collective-permute-done.14.rest_0_), channel_id=1, source_target_pairs={{0,1},{1,0},{2,3},{3,2},{4,5},{5,4},{6,7},{7,6},{8,9},{9,8},{10,11... | collective-permute-start | bytes 393224 | tf_op jit(solution)/shard_map/ppermute | solution.py:534
  25.5 1.5 %collective-permute-start.16 = (bf16[2,384,128]{2,1,0:T(8,128)(2,1)S(1)}, bf16[2,384,128]{2,1,0:T(8,128)(2,1)S(1)}, u32[]{:S(2)}, u32[]{:S(2)}) collective-permute-start(bf16[2,384,128]{2,1,0:T(8,128)(2,1)S(1)} %collective-permute-done.13.rest_2_), channel_id=1, source_target_pairs={{0,1},{1,0},{2,3},{3,2},{4,5},{5,4},{6,7},{7,6},{8,9},{9,8},{10,11... | collective-permute-start | bytes 589832 | tf_op jit(solution)/shard_map/ppermute | solution.py:534

commit v6 on v5

--- a/solution.py
+++ b/solution.py
@@ -443,9 +443,9 @@
 
 
 def middle_kernel(meta, wide_queries, key_tags, before, given, *rest):
-    pieces = rest[:4]
-    high_out, sums_out, scores = rest[4:]
-    shared = []
+    bundle, pieces = rest[0], rest[1:5]
+    high_out, sums_out, scores = rest[5:]
+    shared = bundle_pages(meta, key_tags, bundle, 0, 3)
     for other in range(2):
         for role in range(2):
             shared += joined_pages(meta, key_tags, pieces[other * 2 + role], other, 1 + role)
@@ -458,9 +458,9 @@
     high_out, sums_out, scores = rest[3:]
     shared, own = joined_pages(meta, key_tags, mine, 0, 3), ([], [])
     for other in range(2):
-        shared += bundle_pages(meta, key_tags, bundles[other], other, 3)
         for prompt in range(2):
             own[prompt].extend(bundle_stretch(key_tags, bundles[other], other, 3, prompt))
+    shared += bundle_pages(meta, key_tags, bundles[1], 1, 3)
     state = (before, given)
     keep(absorb_pages(wide_queries, shared, own, state, scores), high_out, sums_out)
 
@@ -499,16 +499,16 @@
     )
 
 
-def middle_stage(meta, wide_queries, key_tags, state, pieces):
+def middle_stage(meta, wide_queries, key_tags, state, bundle, pieces):
     return call(
-        middle_kernel, "middle", running(), 24 * 64,
-        meta, wide_queries, key_tags, *state, *pieces,
+        middle_kernel, "middle", running(), 26 * 64,
+        meta, wide_queries, key_tags, *state, bundle, *pieces,
     )
 
 
 def beside_stage(meta, wide_queries, key_tags, state, bundles, mine):
     return call(
-        beside_kernel, "beside", running(), 12 * 64,
+        beside_kernel, "beside", running(), 10 * 64,
         meta, wide_queries, key_tags, *state, *bundles, mine, flops=beside_flops,
     )
 
@@ -567,7 +567,7 @@
     late_both = to_second(late_first)
     late = [late_first, late_second]
     late += [to_sibling(one) for one in late]
-    state = middle_stage(meta, wide_queries, key_tags, state, late)
+    state = middle_stage(meta, wide_queries, key_tags, state, by_both, late)
     state, late_both = lax.optimization_barrier((state, late_both))
     far = [by_both, to_sibling(by_both)]
     theirs = to_sibling(late_both)

time: 28.9 us -> 28.7 us (level)
  transfers between devices with their start and end apart: 17 -> 17, of which waited for: 6 -> 7; matrix products, arithmetic and copies ran while one was open for 0% -> 0% of each run, Pallas kernels for 26% -> 25%
where the time goes in v6:
time: 28.7 us; the launch traced here: 28.5 us
  starting transfers between devices  15.7 us (55%)
  Pallas kernels  9.82 us (34%)
  waiting for transfers between devices  2.94 us (10%)
    pallas_call x4, Pallas kernels, call(): pl.pallas_call(kernel, out_shape=out_shape, in_specs=[smem] + [vmem] * (l...  7.45 us
    ppermute x3, starting transfers between devices, small_body(): lax.ppermute(piece, 'head', [(z, z ^ shift) for z in range(4)])  5.76 us
    ppermute x4, starting transfers between devices, to_second(): return lax.ppermute(value, page_axes, pairs)  5.43 us
    ppermute x2, starting transfers between devices, to_first(): return lax.ppermute(value, page_axes, pairs)  3.12 us
    ppermute x4, waiting for transfers between devices, to_second(): return lax.ppermute(value, page_axes, pairs)  1.62 us
    pallas_call x1, Pallas kernels, mask(): pl.pallas_call(mask_kernel, out_shape=(pltpu.VMEM((2, 512, 256), jnp.bflo...  1.36 us
    ppermute x8, starting transfers between devices, to_sibling(): return lax.ppermute(value, 'pool', [(0, 1), (1, 0)])  1.35 us
    pallas_call x1, Pallas kernels, split(): pl.pallas_call(split_kernel, out_shape=(piece, piece, piece, bundle), in_...  0.99 us
  transfers between devices with their start and end apart: 17, of which 7 were waited for; matrix products, arithmetic and copies ran while one was open for 0% of the time, Pallas kernels for 25%

profile of v6, /device:TPU:0, one launch (start us, length us, event | category | flops | bytes accessed | tf_op | source)
XLA Modules:
  0.0 28.5 jit_solution(8768227852670693723)
XLA Ops:
  0.0 1.0 %split.1 = (bf16[2,2,64,128]{3,2,1,0:T(8,128)(2,1)S(1)}, bf16[2,2,64,128]{3,2,1,0:T(8,128)(2,1)S(1)}, bf16[2,2,64,128]{3,2,1,0:T(8,128)(2,1)S(1)}, bf16[4,2,64,128]{3,2,1,0:T(8,128)(2,1)S(1)}) custom-call(bf16[2,64,512]{2,1,0:T(8,128)(2,1)} %pool_keys.1, bf16[2,64,512]{2,1,0:T(8,128)(2,1)} %pool_values.1, bf16[2,64,128]{2,1,0:T(8,128)(2,1)} %stretch_keys.1, ...), custom_call_target="tpu_custom_call" | custom-call | tf_op jit(solution)/shard_map/split/pallas_call | solution.py:186
  1.0 5.1 %collective-permute-start = (bf16[2,2,64,128]{3,2,1,0:T(8,128)(2,1)S(1)}, bf16[2,2,64,128]{3,2,1,0:T(8,128)(2,1)S(1)}, u32[]{:S(2)}, u32[]{:S(2)}) collective-permute-start(bf16[2,2,64,128]{3,2,1,0:T(8,128)(2,1)S(1)} %get-tuple-element.33), channel_id=1, source_target_pairs={{0,6},{2,4},{4,2},{6,0},{1,7},{3,5},{5,3},{7,1},{8,14},{10,12},{12... | collective-permute-start | bytes 196616 | tf_op jit(solution)/shard_map/ppermute | solution.py:552
  6.1 0.6 %collective-permute-start.2 = (bf16[2,2,64,128]{3,2,1,0:T(8,128)(2,1)S(1)}, bf16[2,2,64,128]{3,2,1,0:T(8,128)(2,1)S(1)}, u32[]{:S(2)}, u32[]{:S(2)}) collective-permute-start(bf16[2,2,64,128]{3,2,1,0:T(8,128)(2,1)S(1)} %get-tuple-element.36), channel_id=1, source_target_pairs={{0,2},{2,0},{4,6},{6,4},{1,3},{3,1},{5,7},{7,5},{8,10},{10,8},{12,... | collective-permute-start | bytes 196616 | tf_op jit(solution)/shard_map/ppermute | solution.py:552
  6.8 1.6 %collective-permute-start.5 = (bf16[4,2,64,128]{3,2,1,0:T(8,128)(2,1)S(1)}, bf16[4,2,64,128]{3,2,1,0:T(8,128)(2,1)S(1)}, u32[]{:S(2)}, u32[]{:S(2)}) collective-permute-start(bf16[4,2,64,128]{3,2,1,0:T(8,128)(2,1)S(1)} %get-tuple-element.47.rest_0_), channel_id=1, source_target_pairs={{0,8},{1,17},{8,0},{9,25},{16,24},{17,1},{24,16},{25,9},{2,10},{3,... | collective-permute-start | bytes 393224 | tf_op jit(solution)/shard_map/ppermute | solution.py:525
  8.4 1.5 %collective-permute-start.6 = (bf16[4,2,64,128]{3,2,1,0:T(8,128)(2,1)S(1)}, bf16[4,2,64,128]{3,2,1,0:T(8,128)(2,1)S(1)}, u32[]{:S(2)}, u32[]{:S(2)}) collective-permute-start(bf16[4,2,64,128]{3,2,1,0:T(8,128)(2,1)S(1)} %get-tuple-element.47.rest_0_), channel_id=1, source_target_pairs={{0,16},{1,9},{8,24},{9,1},{16,0},{17,25},{24,8},{25,17},{2,18},{3,... | collective-permute-start | bytes 393224 | tf_op jit(solution)/shard_map/ppermute | solution.py:530
  9.9 1.4 %mask.1 = (bf16[2,512,256]{2,1,0:T(8,128)(2,1)S(1)}, bf16[4608,128]{1,0:T(8,128)(2,1)S(1)}, s32[72]{0:T(128)S(4)}) custom-call(s32[2]{0:T(128)} %lengths_in, s32[64]{0:T(128)} %table_in.1, bf16[2,64,1024]{2,1,0:T(8,128)(2,1)} %queries_in.1, s32[16,32]{1,0:T(8,128)} %bitcast.2, s32[16,32]{1,0:T(8,128)} %bitcast.3), custom_call_target="tpu_custom_call" | custom-call | bytes 1000 | tf_op jit(solution)/shard_map/mask/pallas_call | solution.py:313
  11.3 0.4 %collective-permute-done.1.second = bf16[2,2,64,128]{3,2,1,0:T(8,128)(2,1)S(1)} collective-permute-done((bf16[2,2,64,128]{3,2,1,0:T(8,128)(2,1)S(1)}, bf16[2,2,64,128]{3,2,1,0:T(8,128)(2,1)S(1)}, u32[]{:S(2)}, u32[]{:S(2)}) %collective-permute-start.1) | collective-permute-done | bytes 65568 | tf_op jit(solution)/shard_map/ppermute | solution.py:552
  11.7 0.2 collective-permute-start.10
  11.9 1.5 %collective-permute-start.3 = (bf16[2,384,128]{2,1,0:T(8,128)(2,1)S(1)}, bf16[2,384,128]{2,1,0:T(8,128)(2,1)S(1)}, u32[]{:S(2)}, u32[]{:S(2)}) collective-permute-start(bf16[2,384,128]{2,1,0:T(8,128)(2,1)S(1)} %join.1.rest_6_), channel_id=1, source_target_pairs={{0,8},{1,17},{8,0},{9,25},{16,24},{17,1},{24,16},{25,9},{2,10},{3,... | collective-permute-start | bytes 589832 | tf_op jit(solution)/shard_map/ppermute | solution.py:525
  13.4 0.0 collective-permute-done.5.rest_1_
  13.4 1.5 %collective-permute-start.4 = (bf16[2,384,128]{2,1,0:T(8,128)(2,1)S(1)}, bf16[2,384,128]{2,1,0:T(8,128)(2,1)S(1)}, u32[]{:S(2)}, u32[]{:S(2)}) collective-permute-start(bf16[2,384,128]{2,1,0:T(8,128)(2,1)S(1)} %join.1.rest_6_), channel_id=1, source_target_pairs={{0,16},{1,9},{8,24},{9,1},{16,0},{17,25},{24,8},{25,17},{2,18},{3,... | collective-permute-start | bytes 589832 | tf_op jit(solution)/shard_map/ppermute | solution.py:530
  14.9 0.0 collective-permute-done.6.rest_2_
  14.9 0.0 collective-permute-start.8
  14.9 0.0 collective-permute-done.7.rest_3_
  14.9 0.5 %collective-permute-start.9 = (bf16[4,2,64,128]{3,2,1,0:T(8,128)(2,1)S(1)}, bf16[4,2,64,128]{3,2,1,0:T(8,128)(2,1)S(1)}, u32[]{:S(2)}, u32[]{:S(2)}) collective-permute-start(bf16[4,2,64,128]{3,2,1,0:T(8,128)(2,1)S(1)} %collective-permute-done.6.rest_2_), channel_id=1, source_target_pairs={{0,1},{1,0},{2,3},{3,2},{4,5},{5,4},{6,7},{7,6},{8,9},{9,8},{10,11... | collective-permute-start | bytes 393224 | tf_op jit(solution)/shard_map/ppermute | solution.py:534
  15.4 0.0 collective-permute-done.10.rest_7_
  15.4 0.5 %collective-permute-start.11 = (bf16[4,2,64,128]{3,2,1,0:T(8,128)(2,1)S(1)}, bf16[4,2,64,128]{3,2,1,0:T(8,128)(2,1)S(1)}, u32[]{:S(2)}, u32[]{:S(2)}) collective-permute-start(bf16[4,2,64,128]{3,2,1,0:T(8,128)(2,1)S(1)} %collective-permute-done.5.rest_1_), channel_id=1, source_target_pairs={{0,16},{1,9},{8,24},{9,1},{16,0},{17,25},{24,8},{25,17},{2,18},{3,... | collective-permute-start | bytes 393224 | tf_op jit(solution)/shard_map/ppermute | solution.py:530
  15.9 0.3 %collective-permute-done.8.rest_4_ = bf16[4,2,64,128]{3,2,1,0:T(8,128)(2,1)S(1)} collective-permute-done((bf16[4,2,64,128]{3,2,1,0:T(8,128)(2,1)S(1)}, bf16[4,2,64,128]{3,2,1,0:T(8,128)(2,1)S(1)}, u32[]{:S(2)}, u32[]{:S(2)}) %collective-permute-start.8) | collective-permute-done | bytes 131104 | tf_op jit(solution)/shard_map/ppermute | solution.py:534
  16.3 0.2 collective-permute-done.9.rest_5_
  16.4 2.5 %open.1 = (f32[2,512,128]{2,1,0:T(8,128)S(1)}, f32[2,512,256]{2,1,0:T(8,128)S(1)}) custom-call(s32[72]{0:T(128)S(4)} %get-tuple-element.41.meta, bf16[2,512,256]{2,1,0:T(8,128)(2,1)S(1)} %get-tuple-element.42.wide_queries, bf16[4608,128]{1,0:T(8,128)(2,1)S(1)} %get-tuple-element.43.key_tags, bf16[4,2,64,128]{3,2,1,0:T(8,128)(2,1)S(1)} %get-tuple-element.47.rest_0_, ...), custom_call_target="tpu_custom_call" | custom-call | bytes 1000 | tf_op jit(solution)/shard_map/open/pallas_call | solution.py:480
  18.9 0.1 collective-permute-done.3.rest_1_
  19.0 0.1 collective-permute-done.4.rest_2_
  19.1 0.7 %collective-permute-start.12 = (bf16[2,384,128]{2,1,0:T(8,128)(2,1)S(1)}, bf16[2,384,128]{2,1,0:T(8,128)(2,1)S(1)}, u32[]{:S(2)}, u32[]{:S(2)}) collective-permute-start(bf16[2,384,128]{2,1,0:T(8,128)(2,1)S(1)} %collective-permute-done.3.rest_1_), channel_id=1, source_target_pairs={{0,1},{1,0},{2,3},{3,2},{4,5},{5,4},{6,7},{7,6},{8,9},{9,8},{10,11... | collective-permute-start | bytes 589832 | tf_op jit(solution)/shard_map/ppermute | solution.py:534
  19.8 0.0 collective-permute-start.13
  19.8 1.9 %collective-permute-start.14 = (bf16[2,384,128]{2,1,0:T(8,128)(2,1)S(1)}, bf16[2,384,128]{2,1,0:T(8,128)(2,1)S(1)}, u32[]{:S(2)}, u32[]{:S(2)}) collective-permute-start(bf16[2,384,128]{2,1,0:T(8,128)(2,1)S(1)} %collective-permute-done.3.rest_1_), channel_id=1, source_target_pairs={{0,16},{1,9},{8,24},{9,1},{16,0},{17,25},{24,8},{25,17},{2,18},{3,... | collective-permute-start | bytes 589832 | tf_op jit(solution)/shard_map/ppermute | solution.py:530
  21.7 0.0 collective-permute-done.11.rest_0_
  21.7 0.0 collective-permute-start.15
  21.7 2.2 %middle.1 = (f32[2,512,128]{2,1,0:T(8,128)S(1)}, f32[2,512,256]{2,1,0:T(8,128)S(1)}) custom-call(s32[72]{0:T(128)S(4)} %get-tuple-element.41.meta, bf16[2,512,256]{2,1,0:T(8,128)(2,1)S(1)} %get-tuple-element.42.wide_queries, bf16[4608,128]{1,0:T(8,128)(2,1)S(1)} %get-tuple-element.43.key_tags, f32[2,512,128]{2,1,0:T(8,128)S(1)} %get-tuple-element.50.before, ...), custom_call_target="tpu_custom_call" | custom-call | bytes 1000 | tf_op jit(solution)/shard_map/middle/pallas_call | solution.py:480
  23.9 1.5 %collective-permute-done.14.rest_2_ = bf16[2,384,128]{2,1,0:T(8,128)(2,1)S(1)} collective-permute-done((bf16[2,384,128]{2,1,0:T(8,128)(2,1)S(1)}, bf16[2,384,128]{2,1,0:T(8,128)(2,1)S(1)}, u32[]{:S(2)}, u32[]{:S(2)}) %collective-permute-start.14) | collective-permute-done | bytes 196640 | tf_op jit(solution)/shard_map/ppermute | solution.py:530
  25.5 1.2 %beside.1 = (f32[2,512,128]{2,1,0:T(8,128)S(1)}, f32[2,512,256]{2,1,0:T(8,128)S(1)}) custom-call(s32[72]{0:T(128)S(4)} %get-tuple-element.41.meta, bf16[2,512,256]{2,1,0:T(8,128)(2,1)S(1)} %get-tuple-element.42.wide_queries, bf16[4608,128]{1,0:T(8,128)(2,1)S(1)} %get-tuple-element.43.key_tags, f32[2,512,128]{2,1,0:T(8,128)S(1)} %get-tuple-element.56.before, ...), custom_call_target="tpu_custom_call" | custom-call | flops 2000000000 | bytes 1000 | tf_op jit(solution)/shard_map/beside/pallas_call | solution.py:480
  26.6 0.3 collective-permute-done.16.theirs
  26.9 1.6 %close.1 = bf16[2,64,1024]{2,1,0:T(8,128)(2,1)} custom-call(s32[72]{0:T(128)S(4)} %get-tuple-element.41.meta, bf16[2,512,256]{2,1,0:T(8,128)(2,1)S(1)} %get-tuple-element.42.wide_queries, bf16[4608,128]{1,0:T(8,128)(2,1)S(1)} %get-tuple-element.43.key_tags, f32[2,512,128]{2,1,0:T(8,128)S(1)} %get-tuple-element.59.before, ...), custom_call_target="tpu_custom_call" | custom-call | bytes 1000 | tf_op jit(solution)/shard_map/close/pallas_call | solution.py:480
  (9 shorter events, 0.0 us)
Async XLA Ops:
  1.0 8.9 %collective-permute-start = (bf16[2,2,64,128]{3,2,1,0:T(8,128)(2,1)S(1)}, bf16[2,2,64,128]{3,2,1,0:T(8,128)(2,1)S(1)}, u32[]{:S(2)}, u32[]{:S(2)}) collective-permute-start(bf16[2,2,64,128]{3,2,1,0:T(8,128)(2,1)S(1)} %get-tuple-element.33), channel_id=1, source_target_pairs={{0,6},{2,4},{4,2},{6,0},{1,7},{3,5},{5,3},{7,1},{8,14},{10,12},{12... | collective-permute-start | bytes 196616 | tf_op jit(solution)/shard_map/ppermute | solution.py:552
  6.1 5.6 %collective-permute-start.1 = (bf16[2,2,64,128]{3,2,1,0:T(8,128)(2,1)S(1)}, bf16[2,2,64,128]{3,2,1,0:T(8,128)(2,1)S(1)}, u32[]{:S(2)}, u32[]{:S(2)}) collective-permute-start(bf16[2,2,64,128]{3,2,1,0:T(8,128)(2,1)S(1)} %get-tuple-element.35), channel_id=1, source_target_pairs={{0,4},{2,6},{4,0},{6,2},{1,5},{3,7},{5,1},{7,3},{8,12},{10,14},{12... | collective-permute-start | bytes 196616 | tf_op jit(solution)/shard_map/ppermute | solution.py:552
  6.1 5.6 %collective-permute-start.2 = (bf16[2,2,64,128]{3,2,1,0:T(8,128)(2,1)S(1)}, bf16[2,2,64,128]{3,2,1,0:T(8,128)(2,1)S(1)}, u32[]{:S(2)}, u32[]{:S(2)}) collective-permute-start(bf16[2,2,64,128]{3,2,1,0:T(8,128)(2,1)S(1)} %get-tuple-element.36), channel_id=1, source_target_pairs={{0,2},{2,0},{4,6},{6,4},{1,3},{3,1},{5,7},{7,5},{8,10},{10,8},{12,... | collective-permute-start | bytes 196616 | tf_op jit(solution)/shard_map/ppermute | solution.py:552
  6.8 6.6 %collective-permute-start.5 = (bf16[4,2,64,128]{3,2,1,0:T(8,128)(2,1)S(1)}, bf16[4,2,64,128]{3,2,1,0:T(8,128)(2,1)S(1)}, u32[]{:S(2)}, u32[]{:S(2)}) collective-permute-start(bf16[4,2,64,128]{3,2,1,0:T(8,128)(2,1)S(1)} %get-tuple-element.47.rest_0_), channel_id=1, source_target_pairs={{0,8},{1,17},{8,0},{9,25},{16,24},{17,1},{24,16},{25,9},{2,10},{3,... | collective-permute-start | bytes 393224 | tf_op jit(solution)/shard_map/ppermute | solution.py:525
  8.4 6.5 %collective-permute-start.6 = (bf16[4,2,64,128]{3,2,1,0:T(8,128)(2,1)S(1)}, bf16[4,2,64,128]{3,2,1,0:T(8,128)(2,1)S(1)}, u32[]{:S(2)}, u32[]{:S(2)}) collective-permute-start(bf16[4,2,64,128]{3,2,1,0:T(8,128)(2,1)S(1)} %get-tuple-element.47.rest_0_), channel_id=1, source_target_pairs={{0,16},{1,9},{8,24},{9,1},{16,0},{17,25},{24,8},{25,17},{2,18},{3,... | collective-permute-start | bytes 393224 | tf_op jit(solution)/shard_map/ppermute | solution.py:530
  9.9 5.0 %collective-permute-start.7 = (bf16[4,2,64,128]{3,2,1,0:T(8,128)(2,1)S(1)}, bf16[4,2,64,128]{3,2,1,0:T(8,128)(2,1)S(1)}, u32[]{:S(2)}, u32[]{:S(2)}) collective-permute-start(bf16[4,2,64,128]{3,2,1,0:T(8,128)(2,1)S(1)} %get-tuple-element.47.rest_0_), channel_id=1, source_target_pairs={{0,1},{1,0},{2,3},{3,2},{4,5},{5,4},{6,7},{7,6},{8,9},{9,8},{10,11... | collective-permute-start | bytes 393224 | tf_op jit(solution)/shard_map/ppermute | solution.py:534
  11.7 3.7 %collective-permute-start.10 = (bf16[2,384,128]{2,1,0:T(8,128)(2,1)S(1)}, bf16[2,384,128]{2,1,0:T(8,128)(2,1)S(1)}, u32[]{:S(2)}, u32[]{:S(2)}) collective-permute-start(bf16[2,384,128]{2,1,0:T(8,128)(2,1)S(1)} %join.1.rest_6_), channel_id=1, source_target_pairs={{0,1},{1,0},{2,3},{3,2},{4,5},{5,4},{6,7},{7,6},{8,9},{9,8},{10,11... | collective-permute-start | bytes 589832 | tf_op jit(solution)/shard_map/ppermute | solution.py:534
  11.9 7.1 %collective-permute-start.3 = (bf16[2,384,128]{2,1,0:T(8,128)(2,1)S(1)}, bf16[2,384,128]{2,1,0:T(8,128)(2,1)S(1)}, u32[]{:S(2)}, u32[]{:S(2)}) collective-permute-start(bf16[2,384,128]{2,1,0:T(8,128)(2,1)S(1)} %join.1.rest_6_), channel_id=1, source_target_pairs={{0,8},{1,17},{8,0},{9,25},{16,24},{17,1},{24,16},{25,9},{2,10},{3,... | collective-permute-start | bytes 589832 | tf_op jit(solution)/shard_map/ppermute | solution.py:525
  13.4 5.7 %collective-permute-start.4 = (bf16[2,384,128]{2,1,0:T(8,128)(2,1)S(1)}, bf16[2,384,128]{2,1,0:T(8,128)(2,1)S(1)}, u32[]{:S(2)}, u32[]{:S(2)}) collective-permute-start(bf16[2,384,128]{2,1,0:T(8,128)(2,1)S(1)} %join.1.rest_6_), channel_id=1, source_target_pairs={{0,16},{1,9},{8,24},{9,1},{16,0},{17,25},{24,8},{25,17},{2,18},{3,... | collective-permute-start | bytes 589832 | tf_op jit(solution)/shard_map/ppermute | solution.py:530
  14.9 1.3 %collective-permute-start.8 = (bf16[4,2,64,128]{3,2,1,0:T(8,128)(2,1)S(1)}, bf16[4,2,64,128]{3,2,1,0:T(8,128)(2,1)S(1)}, u32[]{:S(2)}, u32[]{:S(2)}) collective-permute-start(bf16[4,2,64,128]{3,2,1,0:T(8,128)(2,1)S(1)} %collective-permute-done.5.rest_1_), channel_id=1, source_target_pairs={{0,1},{1,0},{2,3},{3,2},{4,5},{5,4},{6,7},{7,6},{8,9},{9,8},{10,11... | collective-permute-start | bytes 393224 | tf_op jit(solution)/shard_map/ppermute | solution.py:534
  14.9 1.5 %collective-permute-start.9 = (bf16[4,2,64,128]{3,2,1,0:T(8,128)(2,1)S(1)}, bf16[4,2,64,128]{3,2,1,0:T(8,128)(2,1)S(1)}, u32[]{:S(2)}, u32[]{:S(2)}) collective-permute-start(bf16[4,2,64,128]{3,2,1,0:T(8,128)(2,1)S(1)} %collective-permute-done.6.rest_2_), channel_id=1, source_target_pairs={{0,1},{1,0},{2,3},{3,2},{4,5},{5,4},{6,7},{7,6},{8,9},{9,8},{10,11... | collective-permute-start | bytes 393224 | tf_op jit(solution)/shard_map/ppermute | solution.py:534
  15.4 6.3 %collective-permute-start.11 = (bf16[4,2,64,128]{3,2,1,0:T(8,128)(2,1)S(1)}, bf16[4,2,64,128]{3,2,1,0:T(8,128)(2,1)S(1)}, u32[]{:S(2)}, u32[]{:S(2)}) collective-permute-start(bf16[4,2,64,128]{3,2,1,0:T(8,128)(2,1)S(1)} %collective-permute-done.5.rest_1_), channel_id=1, source_target_pairs={{0,16},{1,9},{8,24},{9,1},{16,0},{17,25},{24,8},{25,17},{2,18},{3,... | collective-permute-start | bytes 393224 | tf_op jit(solution)/shard_map/ppermute | solution.py:530
  19.1 2.6 %collective-permute-start.12 = (bf16[2,384,128]{2,1,0:T(8,128)(2,1)S(1)}, bf16[2,384,128]{2,1,0:T(8,128)(2,1)S(1)}, u32[]{:S(2)}, u32[]{:S(2)}) collective-permute-start(bf16[2,384,128]{2,1,0:T(8,128)(2,1)S(1)} %collective-permute-done.3.rest_1_), channel_id=1, source_target_pairs={{0,1},{1,0},{2,3},{3,2},{4,5},{5,4},{6,7},{7,6},{8,9},{9,8},{10,11... | collective-permute-start | bytes 589832 | tf_op jit(solution)/shard_map/ppermute | solution.py:534
  19.8 1.9 %collective-permute-start.13 = (bf16[2,384,128]{2,1,0:T(8,128)(2,1)S(1)}, bf16[2,384,128]{2,1,0:T(8,128)(2,1)S(1)}, u32[]{:S(2)}, u32[]{:S(2)}) collective-permute-start(bf16[2,384,128]{2,1,0:T(8,128)(2,1)S(1)} %collective-permute-done.4.rest_2_), channel_id=1, source_target_pairs={{0,1},{1,0},{2,3},{3,2},{4,5},{5,4},{6,7},{7,6},{8,9},{9,8},{10,11... | collective-permute-start | bytes 589832 | tf_op jit(solution)/shard_map/ppermute | solution.py:534
  19.8 5.7 %collective-permute-start.14 = (bf16[2,384,128]{2,1,0:T(8,128)(2,1)S(1)}, bf16[2,384,128]{2,1,0:T(8,128)(2,1)S(1)}, u32[]{:S(2)}, u32[]{:S(2)}) collective-permute-start(bf16[2,384,128]{2,1,0:T(8,128)(2,1)S(1)} %collective-permute-done.3.rest_1_), channel_id=1, source_target_pairs={{0,16},{1,9},{8,24},{9,1},{16,0},{17,25},{24,8},{25,17},{2,18},{3,... | collective-permute-start | bytes 589832 | tf_op jit(solution)/shard_map/ppermute | solution.py:530
  21.7 3.8 %collective-permute-start.15 = (bf16[4,2,64,128]{3,2,1,0:T(8,128)(2,1)S(1)}, bf16[4,2,64,128]{3,2,1,0:T(8,128)(2,1)S(1)}, u32[]{:S(2)}, u32[]{:S(2)}) collective-permute-start(bf16[4,2,64,128]{3,2,1,0:T(8,128)(2,1)S(1)} %collective-permute-done.11.rest_0_), channel_id=1, source_target_pairs={{0,1},{1,0},{2,3},{3,2},{4,5},{5,4},{6,7},{7,6},{8,9},{9,8},{10,11... | collective-permute-start | bytes 393224 | tf_op jit(solution)/shard_map/ppermute | solution.py:534
  25.5 1.4 %collective-permute-start.16 = (bf16[2,384,128]{2,1,0:T(8,128)(2,1)S(1)}, bf16[2,384,128]{2,1,0:T(8,128)(2,1)S(1)}, u32[]{:S(2)}, u32[]{:S(2)}) collective-permute-start(bf16[2,384,128]{2,1,0:T(8,128)(2,1)S(1)} %collective-permute-done.14.rest_2_), channel_id=1, source_target_pairs={{0,1},{1,0},{2,3},{3,2},{4,5},{5,4},{6,7},{7,6},{8,9},{9,8},{10,11... | collective-permute-start | bytes 589832 | tf_op jit(solution)/shard_map/ppermute | solution.py:534
